TPU v7x, 256 devices: a whole 4x4x8 slice. The times are simulated.
256 devices in a mesh: ctx: 64 (over z, y_lo, x), head: 4 (over y_hi, core).
Axes of the slice: x: 4, y: 4 (y_hi: 2, y_lo: 2; y = y_hi * 2 + y_lo), z: 8, core: 2. Of those that a mesh axis runs over, the one named last changes fastest.
Arguments:
- queries: bfloat16 [1536, 36864], P('ctx', 'head'), may hold values from -40 to 40
- kv_latent: bfloat16 [576, 8192], P(None, 'ctx'), may hold values from -6 to 6
- index_queries: bfloat16 [1536, 8192], P('ctx', 'head'), may hold values from -6 to 6
- index_keys: bfloat16 [8192, 128], P('ctx'), may hold values from -6 to 6
- head_weights: float32 [1536, 64], P('ctx', 'head'), may hold values from -600 to 600
- positions: int32 [1536], P('ctx'), may hold values from 0 to 8191, as said below
Outputs:
- grad_queries: float32 [1536, 8192], P('ctx', 'head')
- grad_keys: float32 [8192, 128], P(('ctx', 'head'))
Inputs may be any that keep to these rules, and one draw needn't show every extreme that they name: Entries c * 24 to (c + 1) * 24 - 1 are positions among tokens c * 128 to (c + 1) * 128 - 1; the first entry of each such group is the first of those tokens and the second is the last.
All inputs are finite; a program needn't handle non-finite values.
Results may differ from a plain program's by a relative error of at most 0.013.
Values may be sent and summed in bfloat16 or wider, within the bound.
No kernel may reach another device: no remote copies, remote signals or barrier semaphores. Data moves between devices by JAX's collectives and lax.ppermute only.
A program may use at most 64 MiB of HBM per device.

v0:
```python
import math

import jax
import jax.numpy as jnp
from jax import lax
from jax.sharding import PartitionSpec as P

DL = 576
HEADS = 64
IHEADS = 64
DI = 128


negative = -1e30
loss_scale = 64.0
score_scale = 1.0 / math.sqrt(192.0)


def against(left, right):
    return lax.dot_general(
        left, right, (((1,), (1,)), ((), ())), preferred_element_type=jnp.float32
    )


def body(queries, kv_latent, index_queries, index_keys, head_weights, positions):
    query_rows = queries.shape[0]
    local_heads = queries.shape[1] // DL
    query_heads = jnp.transpose(queries.reshape(query_rows, local_heads, DL), (1, 0, 2))
    index_heads = jnp.transpose(
        index_queries.reshape(query_rows, index_queries.shape[1] // DI, DI), (1, 0, 2)
    )
    weight_cols = jnp.transpose(head_weights)
    coeff = 1.0 / math.sqrt(IHEADS * DI)

    def visible_from(length):
        key_positions = jnp.arange(length, dtype=jnp.int32)
        return key_positions[None, :] <= positions[:, None]

    start_pair = (
        jnp.full((local_heads, query_rows), negative, jnp.float32),
        jnp.zeros((local_heads, query_rows), jnp.float32),
    )
    shard_part = lax.all_gather(kv_latent, "ctx", axis=1, tiled=True)
    visible = visible_from(shard_part.shape[1])

    def one_head(inputs):
        q_head, best_score, head_total = inputs
        scores = jnp.dot(q_head, shard_part, preferred_element_type=jnp.float32) * score_scale
        scores = jnp.where(visible, scores, negative)
        new_best = jnp.maximum(best_score, jnp.max(scores, axis=1))
        expo_terms = jnp.where(visible, jnp.exp(scores - new_best[:, None]), 0.0)
        return (new_best, head_total * jnp.exp(best_score - new_best) + jnp.sum(expo_terms, axis=1))

    best_all, total_all = lax.map(one_head, (query_heads, start_pair[0], start_pair[1]))
    make_shard_part = lax.all_gather(kv_latent, "ctx", axis=1, tiled=True)
    make_visible = visible_from(make_shard_part.shape[1])

    def make_add_head(running, inputs):
        q_head, best_score, head_total = inputs
        scores = jnp.dot(q_head, make_shard_part, preferred_element_type=jnp.float32) * score_scale
        probs = jnp.where(
            make_visible, jnp.exp(scores - best_score[:, None]) / head_total[:, None], 0.0
        )
        return (running + probs, None)

    running, _ = lax.scan(
        make_add_head,
        jnp.zeros((query_rows, make_shard_part.shape[1]), jnp.float32),
        (query_heads, best_all, total_all),
    )
    target_part = running / HEADS
    keys_all = lax.all_gather(index_keys, "ctx", axis=0, tiled=True)
    key_count = keys_all.shape[0]

    def logit_step(running, inputs):
        q_head, w_col = inputs
        return (running + w_col[:, None] * jnp.maximum(against(q_head, keys_all), 0.0), None)

    weighted, _ = lax.scan(
        logit_step, jnp.zeros((query_rows, key_count), jnp.float32), (index_heads, weight_cols)
    )
    logit_part = coeff * weighted
    target, logits = lax.psum((target_part, logit_part), "head")
    visible_all = visible_from(key_count)
    masked = jnp.where(visible_all, logits, negative)
    row_top = jnp.max(masked, axis=1, keepdims=True)
    expo_logits = jnp.where(visible_all, jnp.exp(masked - row_top), 0.0)
    predicted = expo_logits / jnp.sum(expo_logits, axis=1, keepdims=True)
    grad_logits = jnp.where(visible_all, loss_scale * (predicted - target), 0.0).astype(
        jnp.bfloat16
    )

    def back_step(unused, inputs):
        q_head, w_col = inputs
        head_grads = jnp.where(
            against(q_head, keys_all) > 0.0, (coeff * w_col)[:, None] * grad_logits, 0.0
        )
        head_grads = head_grads.astype(jnp.bfloat16)
        return (unused, jnp.dot(head_grads, keys_all, preferred_element_type=jnp.float32))

    _, query_grads = lax.scan(back_step, jnp.zeros((), jnp.float32), (index_heads, weight_cols))
    grad_queries = jnp.transpose(query_grads, (1, 0, 2)).reshape(query_rows, -1)
    out_rows = key_count // (lax.axis_size("ctx") * lax.axis_size("head"))

    def key_add_head(running, inputs):
        q_head, w_col = inputs
        head_grads = jnp.where(
            against(q_head, keys_all) > 0.0, (coeff * w_col)[:, None] * grad_logits, 0.0
        )
        head_grads = head_grads.astype(jnp.bfloat16)
        term = lax.dot_general(
            head_grads, q_head, (((0,), (0,)), ((), ())), preferred_element_type=jnp.float32
        )
        return (running + term, None)

    running, _ = lax.scan(
        key_add_head,
        jnp.zeros((out_rows * lax.axis_size(("ctx", "head")), DI), jnp.float32),
        (index_heads, weight_cols),
    )
    grad_keys = lax.psum_scatter(running, ("ctx", "head"), scatter_dimension=0, tiled=True)
    return (grad_queries, grad_keys)


def solution(mesh):
    in_specs = (
        P("ctx", "head"),
        P(None, "ctx"),
        P("ctx", "head"),
        P("ctx", None),
        P("ctx", "head"),
        P("ctx"),
    )
    out_specs = (P("ctx", "head"), P(("ctx", "head"), None))
    return jax.shard_map(body, mesh=mesh, in_specs=in_specs, out_specs=out_specs, check_vma=False)
```

profile of v0, /device:TPU:2, one launch (start us, length us, event | category | flops | bytes accessed | tf_op | source)
XLA Modules:
  0.0 2204.5 jit_solution(4491155993071524113)
XLA Ops:
  11.2 300.2 %all-gather.3.cloned.1.call-done = bf16[8192,128]{1,0:T(8,128)(2,1)} async-done(((bf16[128,128]{1,0:T(8,128)(2,1)}), bf16[8192,128]{1,0:T(8,128)(2,1)}) %all-gather.3.cloned.1.call-update) | async-done | bytes 2097168 | tf_op jit(solution)/shard_map/all_gather | solution.py:72
  311.4 56.5 %while.58 = (s32[]{:T(128)}, f32[24,8192]{1,0:T(8,128)S(1)}, f32[16,24]{1,0:T(8,128)}, bf16[16,24,128]{2,1,0:T(8,128)(2,1)S(1)}, bf16[8192,128]{1,0:T(8,128)(2,1)}, /*index=5*/s32[]{:T(128)}, s32[]{:T(128)}) while((s32[]{:T(128)}, f32[24,8192]{1,0:T(8,128)S(1)}, f32[16,24]{1,0:T(8,128)}, bf16[16,24,128]{2,1,0:T(8,128)(2,1)S(1)}, ...), condition=%wide.region_1.2_spmd.clone, body=%wide.region_0.1_spmd.clone.sunk | while | flops 51118080 | bytes 3676959 | solution.py:79
  319.2 2.8 fusion.96
  322.7 2.8 fusion.96
  326.2 2.8 fusion.96
  329.8 2.8 fusion.96
  343.9 2.8 fusion.96
  347.4 2.8 fusion.96
  350.9 2.8 fusion.96
  367.9 222.7 %all-gather.5.cloned.1.call-done = bf16[576,8192]{1,0:T(8,128)(2,1)} async-done(((bf16[576,128]{1,0:T(8,128)(2,1)}), bf16[576,8192]{1,0:T(8,128)(2,1)}) %all-gather.5.cloned.1.call-update) | async-done | bytes 9437200 | tf_op jit(solution)/shard_map/all_gather | solution.py:43
  590.6 91.9 %while.57 = (s32[]{:T(128)}, f32[16,24]{1,0:T(8,128)S(1)}, f32[16,24]{1,0:T(8,128)S(1)}, bf16[16,24,576]{2,1,0:T(8,128)(2,1)S(1)}, bf16[576,8192]{1,0:T(8,128)(2,1)}, /*index=5*/s32[24]{0:T(128)S(1)}, s32[]{:T(128)}, s32[]{:T(128)}) while((s32[]{:T(128)}, f32[16,24]{1,0:T(8,128)S(1)}, f32[16,24]{1,0:T(8,128)S(1)}, ...), condition=%wide.region_8.9_spmd.clone, body=%wide.region_5.8_spmd.clone.sunk | while | flops 228065344 | bytes 11042721 | solution.py:54
  590.6 5.2 fusion.92
  596.4 5.3 fusion.92
  602.1 5.3 fusion.92
  607.9 5.3 fusion.92
  613.6 5.3 fusion.92
  619.4 5.3 fusion.92
  625.1 5.3 fusion.92
  630.8 5.3 fusion.92
  636.6 5.3 fusion.92
  642.3 5.3 fusion.92
  648.1 5.3 fusion.92
  653.8 5.3 fusion.92
  659.6 5.3 fusion.92
  665.3 5.3 fusion.92
  671.0 5.3 fusion.92
  676.8 5.3 fusion.92
  682.5 83.8 %while.59 = (s32[]{:T(128)}, f32[24,8192]{1,0:T(8,128)S(1)}, bf16[16,24,576]{2,1,0:T(8,128)(2,1)S(1)}, bf16[576,8192]{1,0:T(8,128)(2,1)}, f32[16,24]{1,0:T(8,128...) while((s32[]{:T(128)}, f32[24,8192]{1,0:T(8,128)S(1)}, ...), condition=%wide.region_10.11_spmd.clone, body=%wide.region_9.10_spmd.clone.sunk | while | flops 227868672 | bytes 11042799 | solution.py:66
  682.6 5.2 fusion.100
  687.8 5.2 fusion.100
  693.0 5.2 fusion.100
  698.3 5.2 fusion.100
  703.5 5.2 fusion.100
  708.8 5.2 fusion.100
  714.0 5.2 fusion.100
  719.2 5.2 fusion.100
  724.5 5.2 fusion.100
  729.7 5.2 fusion.100
  734.9 5.2 fusion.100
  740.2 5.2 fusion.100
  745.4 5.2 fusion.100
  750.7 5.2 fusion.100
  755.9 5.2 fusion.100
  761.1 5.2 fusion.100
  769.0 55.2 %all-reduce.3.cloned.1.call-done = (f32[24,8192]{1,0:T(8,128)}, f32[24,8192]{1,0:T(8,128)}) async-done(((f32[24,8192]{1,0:T(8,128)}, f32[24,8192]{1,0:T(8,128)}), (f32[24,8192]{1,0:T(8,128)}, f32[24,8192]{1,0:T(8,128)})) %all-reduce.3.cloned.1.call-update) | async-done | bytes 1572880 | tf_op jit(solution)/shard_map/psum | solution.py:83
  828.8 104.1 %while.60 = (s32[]{:T(128)}, f32[8192,128]{1,0:T(8,128)}, bf16[16,24,128]{2,1,0:T(8,128)(2,1)S(1)}, bf16[8192,128]{1,0:T(8,128)(2,1)S(1)}, f32[16,24]{1,0:T(8,12...) while((s32[]{:T(128)}, f32[8192,128]{1,0:T(8,128)}, ...), condition=%wide.region_15.16_spmd.clone, body=%wide.region_14.15_spmd.clone.sunk | while | flops 103743512 | bytes 10893091 | solution.py:116
  829.6 3.8 convolution_add_fusion.2
  834.0 5.9 convolution_add_fusion.2
  840.7 5.9 convolution_add_fusion.2
  847.3 5.9 convolution_add_fusion.2
  853.9 5.9 convolution_add_fusion.2
  860.6 5.9 convolution_add_fusion.2
  867.2 5.9 convolution_add_fusion.2
  873.8 5.9 convolution_add_fusion.2
  880.5 5.9 convolution_add_fusion.2
  887.1 5.9 convolution_add_fusion.2
  893.8 5.9 convolution_add_fusion.2
  900.4 5.9 convolution_add_fusion.2
  907.0 5.9 convolution_add_fusion.2
  913.7 5.9 convolution_add_fusion.2
  920.3 5.9 convolution_add_fusion.2
  927.0 5.9 convolution_add_fusion.2
  932.9 35.2 %while.56 = (s32[]{:T(128)}, f32[16,24,128]{2,1,0:T(8,128)S(1)}, bf16[16,24,128]{2,1,0:T(8,128)(2,1)S(1)}, bf16[8192,128]{1,0:T(8,128)(2,1)S(1)}, f32[16,24]{1,0...) while((s32[]{:T(128)}, f32[16,24,128]{2,1,0:T(8,128)S(1)}, bf16[16,24,128]{2,1,0:T(8,128)(2,1)S(1)}, ...), condition=%wide.region_13.14_spmd, body=%wide.region_12.13_spmd.sunk | while | flops 101646360 | bytes 4607761 | solution.py:101
  968.8 1229.2 %reduce-scatter.2.cloned.1.call-done = f32[32,128]{1,0:T(8,128)} async-done(((f32[8192,128]{1,0:T(8,128)}), f32[32,128]{1,0:T(8,128)}) %reduce-scatter.2.cloned.1.call-update) | async-done | bytes 16400 | tf_op jit(solution)/shard_map/reduce_scatter | solution.py:121
  (198 shorter events, 101.8 us)
Async XLA Ops:
  7.2 304.3 %all-gather.3.cloned.1.call-start = ((), (), s32[]{:S(2)}) async-start(), calls=%async_computation.1 | async-start | bytes 2129920 | tf_op jit(solution)/shard_map/all_gather | solution.py:72
  7.9 582.7 %all-gather.5.cloned.1.call-start = ((), (), s32[]{:S(2)}) async-start(), calls=%async_computation.2 | async-start | bytes 9584640 | tf_op jit(solution)/shard_map/all_gather | solution.py:43
  8.6 815.6 %all-reduce.3.cloned.1.call-start = ((), (), s32[]{:S(2)}) async-start(), calls=%async_computation.4 | async-start | bytes 3145728 | tf_op jit(solution)/shard_map/psum | solution.py:83
  311.4 279.2 %copy-start.2 = (s32[24]{0:T(128)S(1)}, s32[24]{0:T(128)}, u32[]{:S(2)}) copy-start(s32[24]{0:T(128)} %param.21) | copy-start | bytes 292
  367.9 222.7 %copy-start.1 = (f32[24,8192]{1,0:T(8,128)}, f32[24,8192]{1,0:T(8,128)S(1)}, u32[]{:S(2)}) copy-start(f32[24,8192]{1,0:T(8,128)S(1)} %get-tuple-element.163) | copy-start | bytes 2359300
  766.3 62.5 %copy-start = (bf16[8192,128]{1,0:T(8,128)(2,1)S(1)}, bf16[8192,128]{1,0:T(8,128)(2,1)}, u32[]{:S(2)}) copy-start(bf16[8192,128]{1,0:T(8,128)(2,1)} %get-tuple-element.674) | copy-start | bytes 6291460
  768.9 1429.1 %reduce-scatter.2.cloned.1.call-start = ((), (), s32[]{:S(2)}) async-start(), calls=%async_computation.3 | async-start | bytes 4210688 | tf_op jit(solution)/shard_map/reduce_scatter | solution.py:121
Sparse Core Ops, SparseCore 0:
  9.8 301.5 all-gather.2
  313.1 277.4 all-gather.4
  769.1 55.1 all-reduce.2
  933.0 1264.9 reduce-scatter.1
where the time goes:
time: 2220 us; the launch traced here: 2200 us
  waiting for transfers between devices  1810 us (82%)
  matrix products  329 us (15%)
  other arithmetic  35.6 us (2%)
    reduce_scatter x1, waiting for transfers between devices, body(): lax.psum_scatter(running, ('ctx', 'head'), scatter_dimension=0, tiled=True)  1230 us
    all_gather x1, waiting for transfers between devices, body(): keys_all = lax.all_gather(index_keys, 'ctx', axis=0, tiled=True)  300 us
    all_gather x1, waiting for transfers between devices, body(): shard_part = lax.all_gather(kv_latent, 'ctx', axis=1, tiled=True)  223 us
    dot_general x16, matrix products, key_add_head(): lax.dot_general(head_grads, q_head, (((0,), (0,)), ((), ())), preferred_e...  92.9 us
    dot_general x16, matrix products, one_head(): jnp.dot(q_head, shard_part, preferred_element_type=jnp.float32)  84 us
    dot_general x16, matrix products, make_add_head(): jnp.dot(q_head, make_shard_part, preferred_element_type=jnp.float32)  83.1 us
    psum x1, waiting for transfers between devices, body(): target, logits = lax.psum((target_part, logit_part), 'head')  55.2 us
    dot_general x16, matrix products, against(): lax.dot_general(left, right, (((1,), (1,)), ((), ())), preferred_element_...  45 us
  transfers between devices with their start and end apart: 4, of which 4 were waited for; matrix products, arithmetic and copies ran while one was open for 4% of the time, Pallas kernels for 0%

commit v1 on v0

v1 whole, which is shorter than its diff:
```python
import math

import jax
import jax.numpy as jnp
from jax import lax
from jax.experimental import pallas as pl
from jax.experimental.pallas import tpu as pltpu
from jax.sharding import Mesh, PartitionSpec as P

DL = 576
HEADS = 64
IHEADS = 64
DI = 128
ROWS = 24
KPAD = 640
LOCAL = 16
RH = ROWS * HEADS
BLOCK = 384
KEYS = 2048

negative = -1e30
loss_scale = 64.0
score_scale = 1.0 / math.sqrt(192.0)
expo_scale = score_scale / math.log(2.0)
log2e = 1.0 / math.log(2.0)
coeff = 1.0 / math.sqrt(IHEADS * DI)

CTX = ("z", "yl", "x")
HEAD = ("yh", "core")
f32 = jnp.float32
bf16 = jnp.bfloat16


def nt(left, right):
    return lax.dot_general(left, right, (((1,), (1,)), ((), ())), preferred_element_type=f32)


def nn(left, right):
    return lax.dot_general(left, right, (((1,), (0,)), ((), ())), preferred_element_type=f32)


def weight_of(q_block):
    parts = q_block[:, DL : DL + 3].astype(f32)
    return parts[:, 0:1] + parts[:, 1:2] + parts[:, 2:3]


def forward_kernel(pos_ref, kpos_ref, q_ref, kk_ref, e_ref, logit_ref, stat_ref, bias, stat, acc):
    step = pl.program_id(0)
    keys = kk_ref.shape[0]

    @pl.when(step == 0)
    def _():
        bias[...] = jnp.where(kpos_ref[...] <= pos_ref[...], 0.0, negative)
        acc[...] = jnp.zeros_like(acc)

    heads = BLOCK // ROWS
    scores = nt(q_ref[:, :KPAD], kk_ref[:, :KPAD])
    scores = (scores.reshape(heads, ROWS, keys) + bias[...][None]).reshape(BLOCK, keys)
    best = jnp.max(scores, axis=1, keepdims=True)
    expo = jnp.exp2((scores - best) * expo_scale)
    total = jnp.sum(expo, axis=1, keepdims=True)
    e_ref[...] = expo.astype(bf16)
    lane = lax.broadcasted_iota(jnp.int32, (BLOCK, 128), 1)
    stat[pl.ds(step * BLOCK, BLOCK), :] = jnp.where(lane == 0, best, jnp.where(lane == 1, total, 0.0))
    inner = nt(q_ref[:, KPAD:], kk_ref[:, KPAD:])
    weighted = jnp.maximum(inner, 0.0) * weight_of(q_ref[:, :KPAD])
    acc[...] += jnp.sum(weighted.reshape(heads, ROWS, keys), axis=0)

    @pl.when(step == pl.num_programs(0) - 1)
    def _():
        logits = coeff * acc[...]
        logit_ref[...] = logits
        masked = logits + bias[...]
        top = jnp.max(masked, axis=1, keepdims=True)
        expo_sum = jnp.sum(jnp.exp2((masked - top) * log2e), axis=1, keepdims=True)
        small_lane = lax.broadcasted_iota(jnp.int32, (ROWS, 128), 1)
        stat[RH : RH + ROWS, :] = jnp.where(
            small_lane == 0, top, jnp.where(small_lane == 1, expo_sum, 0.0)
        )
        stat[RH + ROWS :, :] = jnp.zeros((128 - ROWS, 128), f32)
        stat_ref[...] = jnp.transpose(stat[...])[0:8, :]


def forward(positions, kpos, q_all, kk):
    keys = kk.shape[0]
    return pl.pallas_call(
        forward_kernel,
        grid=(RH // BLOCK,),
        in_specs=[
            pl.BlockSpec((ROWS, 1), lambda i: (0, 0)),
            pl.BlockSpec((1, keys), lambda i: (0, 0)),
            pl.BlockSpec((BLOCK, KPAD + DI), lambda i: (i, 0)),
            pl.BlockSpec((keys, KPAD + DI), lambda i: (0, 0)),
        ],
        out_specs=[
            pl.BlockSpec((BLOCK, keys), lambda i: (i, 0)),
            pl.BlockSpec((ROWS, keys), lambda i: (0, 0)),
            pl.BlockSpec((8, RH + 128), lambda i: (0, 0)),
        ],
        out_shape=[
            jax.ShapeDtypeStruct((RH, keys), bf16),
            jax.ShapeDtypeStruct((ROWS, keys), f32),
            jax.ShapeDtypeStruct((8, RH + 128), f32),
        ],
        scratch_shapes=[
            pltpu.VMEM((ROWS, keys), f32),
            pltpu.VMEM((RH + 128, 128), f32),
            pltpu.VMEM((ROWS, keys), f32),
        ],
        compiler_params=pltpu.CompilerParams(vmem_limit_bytes=56 * 1024 * 1024),
        cost_estimate=pl.CostEstimate(
            flops=2 * RH * keys * 768, bytes_accessed=2 * RH * keys, transcendentals=RH * keys
        ),
        name="forward",
    )(positions, kpos, q_all, kk)


def backward_kernel(
    pos_ref, kpos_ref, own_ref, others_ref, e_ref, logit_ref, q_ref, kk_ref, dq_ref, dk_ref, factor, target, grad, dkt
):
    step = pl.program_id(0)
    half = pl.num_programs(0) // 2
    keys = kk_ref.shape[0]
    heads = BLOCK // ROWS

    @pl.when(step == 0)
    def _():
        best = own_ref[0:1, :]
        gbest = best
        for j in range(3):
            gbest = jnp.maximum(gbest, others_ref[j, 0:1, :])
        is_logit = lax.broadcasted_iota(jnp.int32, (1, RH + 128), 1) >= RH
        scale = jnp.where(is_logit, log2e, expo_scale)
        total = own_ref[1:2, :] * jnp.exp2((best - gbest) * scale)
        for j in range(3):
            total += others_ref[j, 1:2, :] * jnp.exp2((others_ref[j, 0:1, :] - gbest) * scale)
        own_factor = jnp.where(is_logit, 1.0, jnp.exp2((best - gbest) * scale) / HEADS) / total
        rows = lax.broadcasted_iota(jnp.int32, (8, RH + 128), 0)
        packed = jnp.where(rows == 0, own_factor, jnp.where(rows == 1, gbest, 0.0))
        packed = jnp.concatenate([packed, jnp.zeros((120, RH + 128), f32)], axis=0)
        factor[...] = jnp.transpose(packed)
        target[...] = jnp.zeros_like(target)

    @pl.when(step < half)
    def _():
        start = pl.multiple_of(step * BLOCK, BLOCK)
        scaled = e_ref[...].astype(f32) * factor[pl.ds(start, BLOCK), 0:1]
        target[...] += jnp.sum(scaled.reshape(heads, ROWS, keys), axis=0)

    @pl.when(step == half - 1)
    def _():
        top = factor[RH : RH + ROWS, 1:2]
        inverse = factor[RH : RH + ROWS, 0:1]
        visible = kpos_ref[...] <= pos_ref[...]
        masked = jnp.where(visible, logit_ref[...], negative)
        predicted = jnp.exp2((masked - top) * log2e) * inverse
        value = jnp.where(visible, loss_scale * (predicted - target[...]), 0.0)
        grad[...] = value.astype(bf16).astype(f32)
        dkt[...] = jnp.zeros_like(dkt)

    @pl.when(step >= half)
    def _():
        keys_mat = kk_ref[:, KPAD:]
        iq = q_ref[:, KPAD:]
        inner = nt(iq, keys_mat)
        weight = coeff * weight_of(q_ref[:, :KPAD])
        spread = jnp.broadcast_to(grad[...][None], (heads, ROWS, keys)).reshape(BLOCK, keys)
        head_grads = jnp.where(inner > 0.0, weight * spread, 0.0).astype(bf16)
        dq = nn(head_grads, keys_mat)
        for j in range(heads):
            dq_ref[0, :, j * DI : (j + 1) * DI] = dq[j * ROWS : (j + 1) * ROWS].astype(bf16)
        dkt[...] += nn(jnp.transpose(iq), head_grads)

    @pl.when(step == 2 * half - 1)
    def _():
        dk_ref[...] = jnp.transpose(dkt[...]).astype(bf16)


def backward(positions, kpos, own, others, expo, logits, q_all, kk):
    keys = kk.shape[0]
    half = RH // BLOCK
    first = lambda i: jnp.minimum(i, half - 1)
    second = lambda i: jnp.maximum(i - half, 0)
    return pl.pallas_call(
        backward_kernel,
        grid=(2 * half,),
        in_specs=[
            pl.BlockSpec((ROWS, 1), lambda i: (0, 0)),
            pl.BlockSpec((1, keys), lambda i: (0, 0)),
            pl.BlockSpec((8, RH + 128), lambda i: (0, 0)),
            pl.BlockSpec((3, 8, RH + 128), lambda i: (0, 0, 0)),
            pl.BlockSpec((BLOCK, keys), lambda i: (first(i), 0)),
            pl.BlockSpec((ROWS, keys), lambda i: (0, 0)),
            pl.BlockSpec((BLOCK, KPAD + DI), lambda i: (second(i), 0)),
            pl.BlockSpec((keys, KPAD + DI), lambda i: (0, 0)),
        ],
        out_specs=[
            pl.BlockSpec((1, ROWS, LOCAL * DI), lambda i: (second(i), 0, 0)),
            pl.BlockSpec((keys, DI), lambda i: (0, 0)),
        ],
        out_shape=[
            jax.ShapeDtypeStruct((4, ROWS, LOCAL * DI), bf16),
            jax.ShapeDtypeStruct((keys, DI), bf16),
        ],
        scratch_shapes=[
            pltpu.VMEM((RH + 128, 128), f32),
            pltpu.VMEM((ROWS, keys), f32),
            pltpu.VMEM((ROWS, keys), f32),
            pltpu.VMEM((DI, keys), f32),
        ],
        compiler_params=pltpu.CompilerParams(vmem_limit_bytes=56 * 1024 * 1024),
        cost_estimate=pl.CostEstimate(
            flops=6 * RH * keys * 128, bytes_accessed=2 * RH * keys, transcendentals=0
        ),
        name="backward",
    )(positions, kpos, own, others, expo, logits, q_all, kk)


def flip(value, axis):
    return lax.ppermute(value, axis, [(0, 1), (1, 0)])


def head_xor(value, bits):
    return lax.ppermute(value, HEAD, [(i, i ^ bits) for i in range(4)])


def body(queries, kv_latent, index_queries, index_keys, head_weights, positions):
    z, yl, x = (lax.axis_index(a) for a in CTX)
    head = lax.axis_index(HEAD)
    with jax.named_scope("local_prep"):
        own_keys = jnp.concatenate(
            [
                jnp.transpose(lax.dynamic_slice_in_dim(kv_latent, head * 32, 32, 1)),
                jnp.zeros((32, KPAD - DL), bf16),
                lax.dynamic_slice_in_dim(index_keys, head * 32, 32, 0),
            ],
            axis=1,
        )
        w = jnp.transpose(head_weights).reshape(LOCAL * ROWS, 1)
        hi = lax.reduce_precision(w, 8, 7)
        mid = lax.reduce_precision(w - hi, 8, 7)
        low = w - hi - mid
        q_own = jnp.concatenate(
            [
                jnp.transpose(queries.reshape(ROWS, LOCAL, DL), (1, 0, 2)).reshape(LOCAL * ROWS, DL),
                hi.astype(bf16),
                mid.astype(bf16),
                low.astype(bf16),
                jnp.zeros((LOCAL * ROWS, KPAD - DL - 3), bf16),
                jnp.transpose(index_queries.reshape(ROWS, LOCAL, DI), (1, 0, 2)).reshape(
                    LOCAL * ROWS, DI
                ),
            ],
            axis=1,
        )
    with jax.named_scope("gather_queries"):
        q_yh = flip(q_own, "yh")
        q_core = flip(q_own, "core")
        q_both = flip(q_yh, "core")
        q_all = jnp.concatenate([q_own, q_core, q_yh, q_both], axis=0)
    with jax.named_scope("gather_keys"):
        over_z = lax.all_to_all(
            jnp.broadcast_to(own_keys[None], (8, 32, KPAD + DI)), "z", 0, 0, tiled=True
        ).reshape(256, KPAD + DI)
        over_y = jnp.concatenate([over_z, flip(over_z, "yl")], axis=0)
        pieces = [over_y] + [
            lax.ppermute(over_y, "x", [((i + s) % 4, i) for i in range(4)]) for s in (1, 2, 3)
        ]
        kk = jnp.concatenate(pieces, axis=0)
    index = jnp.arange(KEYS, dtype=jnp.int32)
    slot_x = (x + index // 512) % 4
    slot_y = (yl + (index // 256) % 2) % 2
    slot_z = (index // 32) % 8
    kpos = ((slot_z * 8 + slot_y * 4 + slot_x) * 128 + head * 32 + index % 32)[None, :]
    pos = positions[:, None]
    expo, logits, stats = forward(pos, kpos, q_all, kk)
    with jax.named_scope("exchange_stats"):
        others = []
        for bits in (1, 2, 3):
            got = head_xor(stats, bits)
            groups = [got[:, (s ^ bits) * 384 : (s ^ bits) * 384 + 384] for s in range(4)]
            others.append(jnp.concatenate(groups + [got[:, RH:]], axis=1))
        others = jnp.stack(others)
    dq, dk = backward(pos, kpos, stats, others, expo, logits, q_all, kk)
    with jax.named_scope("reduce_keys"):
        got = [
            lax.ppermute(dk[512 * s : 512 * s + 512], "x", [(i, (i + s) % 4) for i in range(4)])
            for s in (1, 2, 3)
        ]
        dk_x = dk[:512].astype(f32)
        for part in got:
            dk_x = dk_x + part.astype(f32)
        away = flip(dk_x[256:].astype(bf16), "yl")
        dk_y = dk_x[:256] + away.astype(f32)
        dk_z = lax.all_to_all(dk_y.astype(bf16).reshape(8, 32, DI), "z", 0, 0, tiled=True)
        grad_keys = jnp.sum(dk_z.astype(f32), axis=0)
    with jax.named_scope("reduce_queries"):
        grad_queries = dq[0].astype(f32)
        for bits in (1, 2, 3):
            grad_queries = grad_queries + head_xor(dq[bits], bits).astype(f32)
    return (grad_queries, grad_keys)


def solution(mesh):
    fine = Mesh(mesh.devices.reshape(8, 2, 4, 2, 2), CTX + HEAD)
    in_specs = (
        P(CTX, HEAD),
        P(None, CTX),
        P(CTX, HEAD),
        P(CTX, None),
        P(CTX, HEAD),
        P(CTX),
    )
    out_specs = (P(CTX, HEAD), P(CTX + HEAD, None))
    return jax.shard_map(body, mesh=fine, in_specs=in_specs, out_specs=out_specs, check_vma=False)
```

time: 2220 us -> 149 us (0.07)
  waiting for transfers between devices: 1810 us -> 63.4 us
  matrix products: 329 us -> 0 us
  starting transfers between devices: 0.16 us -> 37.4 us
  other arithmetic: 35.6 us -> 8.35 us
  Pallas kernels: 0 us -> 25.9 us
    reduce_scatter x1 -> x0, waiting for transfers between devices: 1230 us -> none  [body(): lax.psum_scatter(running, ('ctx', 'head'), scatter_dimension=0, tiled=True)]
    all_gather x2 -> x0, waiting for transfers between devices: 523 us -> none  [the longest x1 300 us: body(): keys_all = lax.all_gather(index_keys, 'ctx', axis=0, tiled=True)]
    dot_general x80 -> x0, matrix products: 329 us -> none  [the longest x16 92.9 us: key_add_head(): lax.dot_general(head_grads, q_head, (((0,), (0,)), ((), ())), preferred_e...]
    psum x1 -> x0, waiting for transfers between devices: 55.2 us -> none  [body(): target, logits = lax.psum((target_part, logit_part), 'head')]
    ppermute x0 -> x17, waiting for transfers between devices: none -> 48.6 us  [the longest x3 26.7 us: body(): lax.ppermute(over_y, 'x', [((i + s) % 4, i) for i in range(4)])]
    pallas_call x0 -> x2, Pallas kernels: none -> 25.9 us  [the longest x1 13.5 us: forward(): pl.pallas_call(forward_kernel, grid=(RH // BLOCK,), in_specs=[pl.BlockSpe...]
    ppermute x0 -> x17, starting transfers between devices: none -> 22.3 us  [the longest x6 7.42 us: head_xor(): return lax.ppermute(value, HEAD, [(i, i ^ bits) for i in range(4)])]
    mul x32 -> x0, other arithmetic: 22.2 us -> none  [the longest x16 11.2 us: back_step(): coeff * w_col]
  transfers between devices with their start and end apart: 4 -> 19, of which waited for: 4 -> 11; matrix products, arithmetic and copies ran while one was open for 4% -> 8% of each run, Pallas kernels for 0% -> 0%
where the time goes in v1:
time: 149 us; the launch traced here: 147 us
  waiting for transfers between devices  63.4 us (43%)
  starting transfers between devices  37.4 us (25%)
  Pallas kernels  25.9 us (17%)
  local copies, waits for them, and re-layouts  11 us (7%)
  other arithmetic  8.35 us (6%)
    ppermute x3, waiting for transfers between devices, body(): lax.ppermute(over_y, 'x', [((i + s) % 4, i) for i in range(4)])  26.7 us
    pallas_call x1, Pallas kernels, forward(): pl.pallas_call(forward_kernel, grid=(RH // BLOCK,), in_specs=[pl.BlockSpe...  13.5 us
    pallas_call x1, Pallas kernels, backward(): pl.pallas_call(backward_kernel, grid=(2 * half,), in_specs=[pl.BlockSpec(...  12.4 us
    ppermute x5, waiting for transfers between devices, flip(): return lax.ppermute(value, axis, [(0, 1), (1, 0)])  12.2 us
    all_to_all x1, starting transfers between devices, body(): lax.all_to_all(jnp.broadcast_to(own_keys[None], (8, 32, KPAD + DI)), 'z',...  8.47 us
    all_to_all x1, waiting for transfers between devices, body(): lax.all_to_all(jnp.broadcast_to(own_keys[None], (8, 32, KPAD + DI)), 'z',...  8.05 us
    ppermute x6, starting transfers between devices, head_xor(): return lax.ppermute(value, HEAD, [(i, i ^ bits) for i in range(4)])  7.42 us
    all_to_all x1, waiting for transfers between devices, body(): lax.all_to_all(dk_y.astype(bf16).reshape(8, 32, DI), 'z', 0, 0, tiled=True)  6.73 us
  transfers between devices with their start and end apart: 19, of which 11 were waited for; matrix products, arithmetic and copies ran while one was open for 8% of the time, Pallas kernels for 0%

profile of v1, /device:TPU:2, one launch (start us, length us, event | category | flops | bytes accessed | tf_op | source)
XLA Modules:
  0.0 147.0 jit_solution(11716690608518531291)
XLA Ops:
  0.6 0.0 copy-start
  0.7 0.7 constant_dynamic-slice_fusion
  1.4 0.1 copy-done
  1.5 0.1 constant_dynamic-slice_fusion.1
  1.7 0.1 copy.37
  1.8 0.1 pad.9.clone
  1.9 0.8 broadcast_in_dim.19
  2.7 8.5 %all-to-all-start = ((bf16[8,32,768]{2,1,0:T(8,128)(2,1)}), bf16[8,32,768]{2,1,0:T(8,128)(2,1)S(1)}, u32[]{:S(2)}, u32[]{:S(2)}) async-start(bf16[8,32,768]{2,1,0:T(8,128)(2,1)} %broadcast_in_dim.19), calls=%async_computation | async-start | bytes 786432 | tf_op jit(solution)/shard_map/gather_keys/all_to_all | solution.py:262
  11.1 0.8 reshape.342
  11.9 0.1 copy.30
  12.1 0.0 copy-start.3
  12.1 0.2 copy.33
  12.3 0.1 copy.31
  12.4 1.4 reshape.340
  13.9 0.1 copy.29
  14.1 0.4 concatenate.26
  14.5 3.3 %collective-permute-start.1 = (bf16[384,768]{1,0:T(8,128)(2,1)S(1)}, bf16[384,768]{1,0:T(8,128)(2,1)}, u32[]{:S(2)}, u32[]{:S(2)}) collective-permute-start(bf16[384,768]{1,0:T(8,128)(2,1)S(1)} %concatenate.26), channel_id=1, source_target_pairs={{0,2},{2,0},{1,3},{3,1},{4,6},{6,4},{5,7},{7,5},{8,10},{10,8},{9,1... | collective-permute-start | bytes 1769480 | tf_op jit(solution)/shard_map/gather_queries/ppermute | solution.py:220
  17.8 8.1 %all-to-all-done = bf16[8,32,768]{2,1,0:T(8,128)(2,1)S(1)} async-done(((bf16[8,32,768]{2,1,0:T(8,128)(2,1)}), bf16[8,32,768]{2,1,0:T(8,128)(2,1)S(1)}, u32[]{:S(2)}, u32[]{:S(2)}) %all-to-all-start) | async-done | bytes 393248 | tf_op jit(solution)/shard_map/gather_keys/all_to_all | solution.py:262
  25.8 1.6 %collective-permute-start.3 = (bf16[256,768]{1,0:T(8,128)(2,1)S(1)}, bf16[256,768]{1,0:T(8,128)(2,1)S(1)}, u32[]{:S(2)}, u32[]{:S(2)}) collective-permute-start(bf16[256,768]{1,0:T(8,128)(2,1)S(1)} %bitcast.29), channel_id=1, source_target_pairs={{0,16},{16,0},{1,17},{17,1},{2,18},{18,2},{3,19},{19,3},{4,20},{20... | collective-permute-start | bytes 1179656 | tf_op jit(solution)/shard_map/gather_keys/ppermute | solution.py:220
  27.4 4.4 %collective-permute-done.1 = bf16[384,768]{1,0:T(8,128)(2,1)} collective-permute-done((bf16[384,768]{1,0:T(8,128)(2,1)S(1)}, bf16[384,768]{1,0:T(8,128)(2,1)}, u32[]{:S(2)}, u32[]{:S(2)}) %collective-permute-start.1) | collective-permute-done | bytes 589856 | tf_op jit(solution)/shard_map/gather_queries/ppermute | solution.py:220
  31.9 0.0 collective-permute-start.2
  31.9 7.8 %collective-permute-done.3 = bf16[256,768]{1,0:T(8,128)(2,1)S(1)} collective-permute-done((bf16[256,768]{1,0:T(8,128)(2,1)S(1)}, bf16[256,768]{1,0:T(8,128)(2,1)S(1)}, u32[]{:S(2)}, u32[]{:S(2)}) %collective-permute-start.3) | collective-permute-done | bytes 393248 | tf_op jit(solution)/shard_map/gather_keys/ppermute | solution.py:220
  39.6 0.1 pad_maximum_fusion.1
  39.7 0.6 collective-permute-start.4
  40.3 2.4 %collective-permute-start.5 = (bf16[512,768]{1,0:T(8,128)(2,1)S(1)}, bf16[512,768]{1,0:T(8,128)(2,1)}, u32[]{:S(2)}, u32[]{:S(2)}) collective-permute-start(bf16[512,768]{1,0:T(8,128)(2,1)S(1)} %pad_maximum_fusion.1), channel_id=1, source_target_pairs={{8,0},{12,4},{0,8},{4,12},{9,1},{13,5},{1,9},{5,13},{10,2},{14,6},... | collective-permute-start | bytes 2359304 | tf_op jit(solution)/shard_map/gather_keys/ppermute | solution.py:267
  42.7 0.7 fusion.4.kpos_ref
  43.4 0.7 copy.36.pos_ref
  44.1 1.8 %collective-permute-start.6 = (bf16[512,768]{1,0:T(8,128)(2,1)S(1)}, bf16[512,768]{1,0:T(8,128)(2,1)S(1)}, u32[]{:S(2)}, u32[]{:S(2)}) collective-permute-start(bf16[512,768]{1,0:T(8,128)(2,1)S(1)} %pad_maximum_fusion.1), channel_id=1, source_target_pairs={{12,0},{0,4},{4,8},{8,12},{13,1},{1,5},{5,9},{9,13},{14,2},{2,6},{... | collective-permute-start | bytes 2359304 | tf_op jit(solution)/shard_map/gather_keys/ppermute | solution.py:267
  46.0 0.0 collective-permute-done.2
  46.0 3.0 %pad_maximum_fusion.q_ref = bf16[1536,768]{1,0:T(8,128)(2,1)} fusion(bf16[384,768]{1,0:T(8,128)(2,1)} %collective-permute-done.2, bf16[384,768]{1,0:T(8,128)(2,1)} %collective-permute-done.1, bf16[384,768]{1,0:T(8,128)(2,1)} %collective-permute-done, bf16[384,768]{1,0:T(8,128)(2,1)S(1)} %concatenate.26), kind=kLoop, calls=%fused_computation | loop fusion | flops 9437184 | bytes 4718592 | tf_op jit(solution)/shard_map/gather_queries/concatenate | solution.py:260
  49.0 10.3 %collective-permute-done.4 = bf16[512,768]{1,0:T(8,128)(2,1)S(1)} collective-permute-done((bf16[512,768]{1,0:T(8,128)(2,1)S(1)}, bf16[512,768]{1,0:T(8,128)(2,1)S(1)}, u32[]{:S(2)}, u32[]{:S(2)}) %collective-permute-start.4) | collective-permute-done | bytes 786464 | tf_op jit(solution)/shard_map/gather_keys/ppermute | solution.py:267
  59.3 0.1 constant_dynamic-update-slice_fusion.2
  59.4 16.4 %collective-permute-done.5 = bf16[512,768]{1,0:T(8,128)(2,1)} collective-permute-done((bf16[512,768]{1,0:T(8,128)(2,1)S(1)}, bf16[512,768]{1,0:T(8,128)(2,1)}, u32[]{:S(2)}, u32[]{:S(2)}) %collective-permute-start.5) | collective-permute-done | bytes 786464 | tf_op jit(solution)/shard_map/gather_keys/ppermute | solution.py:267
  75.8 1.2 constant_dynamic-update-slice_fusion.1
  76.9 0.0 collective-permute-done.6
  77.0 0.1 constant_dynamic-update-slice_fusion.kk_ref
  77.0 1.6 %copy-done.1 = bf16[2048,768]{1,0:T(8,128)(2,1)} copy-done((bf16[2048,768]{1,0:T(8,128)(2,1)}, bf16[2048,768]{1,0:T(8,128)(2,1)S(1)}, u32[]{:S(2)}) %copy-start.1) | copy-done | bytes 3145752
  78.7 13.5 %forward.1 = (bf16[1536,2048]{1,0:T(8,128)(2,1)}, f32[24,2048]{1,0:T(8,128)}, f32[8,1664]{1,0:T(8,128)}) custom-call(s32[24,1]{1,0:T(8,128)} %copy.36.pos_ref, s32[1,2048]{1,0:T(1,128)} %fusion.4.kpos_ref, bf16[1536,768]{1,0:T(8,128)(2,1)} %pad_maximum_fusion.q_ref, bf16[2048,768]{1,0:T(8,128)(2,1)} %copy-done.1), custom_call_target="tpu_custom_call" | custom-call | flops 4831838208 | bytes 6291456 | tf_op jit(solution)/shard_map/forward/pallas_call | solution.py:86
  92.2 1.8 %collective-permute-start.8 = (f32[8,1664]{1,0:T(8,128)}, f32[8,1664]{1,0:T(8,128)S(1)}, u32[]{:S(2)}, u32[]{:S(2)}) collective-permute-start(f32[8,1664]{1,0:T(8,128)} %get-tuple-element.7.own_ref), channel_id=1, source_target_pairs={{0,2},{1,3},{2,0},{3,1},{4,6},{5,7},{6,4},{7,5},{8,10},{9,11},{10,... | collective-permute-start | bytes 159752 | tf_op jit(solution)/shard_map/exchange_stats/ppermute | solution.py:224
  94.0 1.8 %collective-permute-start.7 = (f32[8,1664]{1,0:T(8,128)}, f32[8,1664]{1,0:T(8,128)S(1)}, u32[]{:S(2)}, u32[]{:S(2)}) collective-permute-start(f32[8,1664]{1,0:T(8,128)} %get-tuple-element.7.own_ref), channel_id=1, source_target_pairs={{0,1},{1,0},{2,3},{3,2},{4,5},{5,4},{6,7},{7,6},{8,9},{9,8},{10,11... | collective-permute-start | bytes 159752 | tf_op jit(solution)/shard_map/exchange_stats/ppermute | solution.py:224
  95.8 2.2 %collective-permute-done.8 = f32[8,1664]{1,0:T(8,128)S(1)} collective-permute-done((f32[8,1664]{1,0:T(8,128)}, f32[8,1664]{1,0:T(8,128)S(1)}, u32[]{:S(2)}, u32[]{:S(2)}) %collective-permute-start.8) | collective-permute-done | bytes 53280 | tf_op jit(solution)/shard_map/exchange_stats/ppermute | solution.py:224
  98.0 1.3 collective-permute-done.9
  99.3 0.0 collective-permute-done.7
  99.4 0.7 pad_maximum_fusion.2.others_ref
  100.1 12.4 %backward.1 = (bf16[4,24,2048]{2,1,0:T(8,128)(2,1)}, bf16[2048,128]{1,0:T(8,128)(2,1)}) custom-call(s32[24,1]{1,0:T(8,128)} %copy.36.pos_ref, s32[1,2048]{1,0:T(1,128)} %fusion.4.kpos_ref, f32[8,1664]{1,0:T(8,128)} %get-tuple-element.7.own_ref, f32[3,8,1664]{2,1,0:T(8,128)} %pad_maximum_fusion.2.others_ref, bf16[1536,2048]{1,0:T(8,128)(2,1)} %get-tuple-element.8.e_ref, ...), custom_call_target="tpu_custom_call" | custom-call | flops 2415919104 | bytes 6291456 | tf_op jit(solution)/shard_map/backward/pallas_call | solution.py:184
  112.5 1.1 fusion.18
  113.5 1.6 %collective-permute-start.13 = (bf16[512,128]{1,0:T(8,128)(2,1)S(1)}, bf16[512,128]{1,0:T(8,128)(2,1)S(1)}, u32[]{:S(2)}, u32[]{:S(2)}) collective-permute-start(bf16[512,128]{1,0:T(8,128)(2,1)S(1)} %get-tuple-element.12), channel_id=1, source_target_pairs={{0,4},{4,8},{8,12},{12,0},{1,5},{5,9},{9,13},{13,1},{2,6},{6,10},{... | collective-permute-start | bytes 393224 | tf_op jit(solution)/shard_map/reduce_keys/ppermute | solution.py:287
  115.1 1.4 collective-permute-start.15
  116.5 2.0 %collective-permute-start.14 = (bf16[512,128]{1,0:T(8,128)(2,1)S(1)}, bf16[512,128]{1,0:T(8,128)(2,1)S(1)}, u32[]{:S(2)}, u32[]{:S(2)}) collective-permute-start(bf16[512,128]{1,0:T(8,128)(2,1)S(1)} %get-tuple-element.14), channel_id=1, source_target_pairs={{0,8},{4,12},{8,0},{12,4},{1,9},{5,13},{9,1},{13,5},{2,10},{6,14},... | collective-permute-start | bytes 393224 | tf_op jit(solution)/shard_map/reduce_keys/ppermute | solution.py:287
  118.5 1.7 %collective-permute-done.13 = bf16[512,128]{1,0:T(8,128)(2,1)S(1)} collective-permute-done((bf16[512,128]{1,0:T(8,128)(2,1)S(1)}, bf16[512,128]{1,0:T(8,128)(2,1)S(1)}, u32[]{:S(2)}, u32[]{:S(2)}) %collective-permute-start.13) | collective-permute-done | bytes 131104 | tf_op jit(solution)/shard_map/reduce_keys/ppermute | solution.py:287
  120.1 0.2 collective-permute-done.15
  120.4 4.3 %collective-permute-done.14 = bf16[512,128]{1,0:T(8,128)(2,1)S(1)} collective-permute-done((bf16[512,128]{1,0:T(8,128)(2,1)S(1)}, bf16[512,128]{1,0:T(8,128)(2,1)S(1)}, u32[]{:S(2)}, u32[]{:S(2)}) %collective-permute-start.14) | collective-permute-done | bytes 131104 | tf_op jit(solution)/shard_map/reduce_keys/ppermute | solution.py:287
  124.7 1.0 convert_add_fusion
  125.7 0.2 collective-permute-start.16
  125.9 1.0 slice_bitcast_fusion.2
  126.9 0.1 collective-permute-start.10
  127.0 3.6 %collective-permute-start.12 = (bf16[24,2048]{1,0:T(8,128)(2,1)S(1)}, bf16[24,2048]{1,0:T(8,128)(2,1)S(1)}, u32[]{:S(2)}, u32[]{:S(2)}) collective-permute-start(bf16[24,2048]{1,0:T(8,128)(2,1)S(1)} %get-tuple-element.16), channel_id=1, source_target_pairs={{0,3},{1,2},{2,1},{3,0},{4,7},{5,6},{6,5},{7,4},{8,11},{9,10},{10,... | collective-permute-start | bytes 294920 | tf_op jit(solution)/shard_map/reduce_queries/ppermute | solution.py:224
  130.6 0.1 collective-permute-start.11
  130.7 0.6 fusion.3
  131.3 6.6 %all-to-all-start.1 = ((bf16[8,32,128]{2,1,0:T(8,128)(2,1)}), bf16[8,32,128]{2,1,0:T(8,128)(2,1)S(1)}, u32[]{:S(2)}, u32[]{:S(2)}) async-start(bf16[8,32,128]{2,1,0:T(8,128)(2,1)} %bitcast.15), calls=%async_computation.1 | async-start | bytes 131072 | tf_op jit(solution)/shard_map/reduce_keys/all_to_all | solution.py:295
  138.0 0.0 collective-permute-done.12
  138.0 1.6 %fusion.2 = f32[24,2048]{1,0:T(8,128)} fusion(bf16[24,2048]{1,0:T(8,128)(2,1)S(1)} %collective-permute-done.12, bf16[24,2048]{1,0:T(8,128)(2,1)S(1)} %collective-permute-done.11, bf16[24,2048]{1,0:T(8,128)(2,1)S(1)} %collective-permute-done.10, bf16[4,24,2048]{2,1,0:T(8,128)(2,1)} %get-tuple-element.10), kind=kLoop, calls=%fused_computation.8 | loop fusion | flops 344064 | bytes 589824 | tf_op jit(solution)/shard_map/reduce_queries/add | solution.py:300
  139.6 6.7 %all-to-all-done.1 = bf16[8,32,128]{2,1,0:T(8,128)(2,1)S(1)} async-done(((bf16[8,32,128]{2,1,0:T(8,128)(2,1)}), bf16[8,32,128]{2,1,0:T(8,128)(2,1)S(1)}, u32[]{:S(2)}, u32[]{:S(2)}) %all-to-all-start.1) | async-done | bytes 65568 | tf_op jit(solution)/shard_map/reduce_keys/all_to_all | solution.py:295
  146.3 0.6 convert_reduce_fusion
  (32 shorter events, 0.2 us)
Async XLA Ops:
  0.6 0.9 copy-start
  0.6 13.3 %copy-start.2 = (bf16[24,2048]{1,0:T(8,128)(2,1)S(1)}, bf16[24,2048]{1,0:T(8,128)(2,1)}, u32[]{:S(2)}) copy-start(bf16[24,2048]{1,0:T(8,128)(2,1)} %param.8) | copy-start | bytes 294916
  2.7 23.2 %all-to-all-start = ((bf16[8,32,768]{2,1,0:T(8,128)(2,1)}), bf16[8,32,768]{2,1,0:T(8,128)(2,1)S(1)}, u32[]{:S(2)}, u32[]{:S(2)}) async-start(bf16[8,32,768]{2,1,0:T(8,128)(2,1)} %broadcast_in_dim.19), calls=%async_computation | async-start | bytes 786432 | tf_op jit(solution)/shard_map/gather_keys/all_to_all | solution.py:262
  12.1 31.3 %copy-start.3 = (s32[24]{0:T(128)S(1)}, s32[24]{0:T(128)}, u32[]{:S(2)}) copy-start(s32[24]{0:T(128)} %param.11) | copy-start | bytes 292
  14.5 17.4 %collective-permute-start.1 = (bf16[384,768]{1,0:T(8,128)(2,1)S(1)}, bf16[384,768]{1,0:T(8,128)(2,1)}, u32[]{:S(2)}, u32[]{:S(2)}) collective-permute-start(bf16[384,768]{1,0:T(8,128)(2,1)S(1)} %concatenate.26), channel_id=1, source_target_pairs={{0,2},{2,0},{1,3},{3,1},{4,6},{6,4},{5,7},{7,5},{8,10},{10,8},{9,1... | collective-permute-start | bytes 1769480 | tf_op jit(solution)/shard_map/gather_queries/ppermute | solution.py:220
  25.8 13.8 %collective-permute-start.3 = (bf16[256,768]{1,0:T(8,128)(2,1)S(1)}, bf16[256,768]{1,0:T(8,128)(2,1)S(1)}, u32[]{:S(2)}, u32[]{:S(2)}) collective-permute-start(bf16[256,768]{1,0:T(8,128)(2,1)S(1)} %bitcast.29), channel_id=1, source_target_pairs={{0,16},{16,0},{1,17},{17,1},{2,18},{18,2},{3,19},{19,3},{4,20},{20... | collective-permute-start | bytes 1179656 | tf_op jit(solution)/shard_map/gather_keys/ppermute | solution.py:220
  27.4 18.6 %collective-permute-start = (bf16[384,768]{1,0:T(8,128)(2,1)S(1)}, bf16[384,768]{1,0:T(8,128)(2,1)}, u32[]{:S(2)}, u32[]{:S(2)}) collective-permute-start(bf16[384,768]{1,0:T(8,128)(2,1)S(1)} %concatenate.26), channel_id=1, source_target_pairs={{0,1},{1,0},{2,3},{3,2},{4,5},{5,4},{6,7},{7,6},{8,9},{9,8},{10,11... | collective-permute-start | bytes 1769480 | tf_op jit(solution)/shard_map/gather_queries/ppermute | solution.py:220
  31.9 14.1 %collective-permute-start.2 = (bf16[384,768]{1,0:T(8,128)(2,1)}, bf16[384,768]{1,0:T(8,128)(2,1)}, u32[]{:S(2)}, u32[]{:S(2)}) collective-permute-start(bf16[384,768]{1,0:T(8,128)(2,1)} %collective-permute-done.1), channel_id=1, source_target_pairs={{0,1},{1,0},{2,3},{3,2},{4,5},{5,4},{6,7},{7,6},{8,9},{9,8},{10,11... | collective-permute-start | bytes 1769480 | tf_op jit(solution)/shard_map/gather_queries/ppermute | solution.py:220
  39.7 19.6 %collective-permute-start.4 = (bf16[512,768]{1,0:T(8,128)(2,1)S(1)}, bf16[512,768]{1,0:T(8,128)(2,1)S(1)}, u32[]{:S(2)}, u32[]{:S(2)}) collective-permute-start(bf16[512,768]{1,0:T(8,128)(2,1)S(1)} %pad_maximum_fusion.1), channel_id=1, source_target_pairs={{4,0},{8,4},{12,8},{0,12},{5,1},{9,5},{13,9},{1,13},{6,2},{10,6},{... | collective-permute-start | bytes 2359304 | tf_op jit(solution)/shard_map/gather_keys/ppermute | solution.py:267
  40.3 35.4 %collective-permute-start.5 = (bf16[512,768]{1,0:T(8,128)(2,1)S(1)}, bf16[512,768]{1,0:T(8,128)(2,1)}, u32[]{:S(2)}, u32[]{:S(2)}) collective-permute-start(bf16[512,768]{1,0:T(8,128)(2,1)S(1)} %pad_maximum_fusion.1), channel_id=1, source_target_pairs={{8,0},{12,4},{0,8},{4,12},{9,1},{13,5},{1,9},{5,13},{10,2},{14,6},... | collective-permute-start | bytes 2359304 | tf_op jit(solution)/shard_map/gather_keys/ppermute | solution.py:267
  44.1 32.8 %collective-permute-start.6 = (bf16[512,768]{1,0:T(8,128)(2,1)S(1)}, bf16[512,768]{1,0:T(8,128)(2,1)S(1)}, u32[]{:S(2)}, u32[]{:S(2)}) collective-permute-start(bf16[512,768]{1,0:T(8,128)(2,1)S(1)} %pad_maximum_fusion.1), channel_id=1, source_target_pairs={{12,0},{0,4},{4,8},{8,12},{13,1},{1,5},{5,9},{9,13},{14,2},{2,6},{... | collective-permute-start | bytes 2359304 | tf_op jit(solution)/shard_map/gather_keys/ppermute | solution.py:267
  77.0 1.7 %copy-start.1 = (bf16[2048,768]{1,0:T(8,128)(2,1)}, bf16[2048,768]{1,0:T(8,128)(2,1)S(1)}, u32[]{:S(2)}) copy-start(bf16[2048,768]{1,0:T(8,128)(2,1)S(1)} %constant_dynamic-update-slice_fusion.kk_ref) | copy-start | bytes 9437188
  92.2 5.8 %collective-permute-start.8 = (f32[8,1664]{1,0:T(8,128)}, f32[8,1664]{1,0:T(8,128)S(1)}, u32[]{:S(2)}, u32[]{:S(2)}) collective-permute-start(f32[8,1664]{1,0:T(8,128)} %get-tuple-element.7.own_ref), channel_id=1, source_target_pairs={{0,2},{1,3},{2,0},{3,1},{4,6},{5,7},{6,4},{7,5},{8,10},{9,11},{10,... | collective-permute-start | bytes 159752 | tf_op jit(solution)/shard_map/exchange_stats/ppermute | solution.py:224
  94.0 5.3 %collective-permute-start.9 = (f32[8,1664]{1,0:T(8,128)}, f32[8,1664]{1,0:T(8,128)S(1)}, u32[]{:S(2)}, u32[]{:S(2)}) collective-permute-start(f32[8,1664]{1,0:T(8,128)} %get-tuple-element.7.own_ref), channel_id=1, source_target_pairs={{0,3},{1,2},{2,1},{3,0},{4,7},{5,6},{6,5},{7,4},{8,11},{9,10},{10,... | collective-permute-start | bytes 159752 | tf_op jit(solution)/shard_map/exchange_stats/ppermute | solution.py:224
  94.0 5.3 %collective-permute-start.7 = (f32[8,1664]{1,0:T(8,128)}, f32[8,1664]{1,0:T(8,128)S(1)}, u32[]{:S(2)}, u32[]{:S(2)}) collective-permute-start(f32[8,1664]{1,0:T(8,128)} %get-tuple-element.7.own_ref), channel_id=1, source_target_pairs={{0,1},{1,0},{2,3},{3,2},{4,5},{5,4},{6,7},{7,6},{8,9},{9,8},{10,11... | collective-permute-start | bytes 159752 | tf_op jit(solution)/shard_map/exchange_stats/ppermute | solution.py:224
  113.5 6.6 %collective-permute-start.13 = (bf16[512,128]{1,0:T(8,128)(2,1)S(1)}, bf16[512,128]{1,0:T(8,128)(2,1)S(1)}, u32[]{:S(2)}, u32[]{:S(2)}) collective-permute-start(bf16[512,128]{1,0:T(8,128)(2,1)S(1)} %get-tuple-element.12), channel_id=1, source_target_pairs={{0,4},{4,8},{8,12},{12,0},{1,5},{5,9},{9,13},{13,1},{2,6},{6,10},{... | collective-permute-start | bytes 393224 | tf_op jit(solution)/shard_map/reduce_keys/ppermute | solution.py:287
  115.1 5.2 %collective-permute-start.15 = (bf16[512,128]{1,0:T(8,128)(2,1)S(1)}, bf16[512,128]{1,0:T(8,128)(2,1)S(1)}, u32[]{:S(2)}, u32[]{:S(2)}) collective-permute-start(bf16[512,128]{1,0:T(8,128)(2,1)S(1)} %get-tuple-element.13), channel_id=1, source_target_pairs={{0,12},{4,0},{8,4},{12,8},{1,13},{5,1},{9,5},{13,9},{2,14},{6,2},{... | collective-permute-start | bytes 393224 | tf_op jit(solution)/shard_map/reduce_keys/ppermute | solution.py:287
  116.5 8.2 %collective-permute-start.14 = (bf16[512,128]{1,0:T(8,128)(2,1)S(1)}, bf16[512,128]{1,0:T(8,128)(2,1)S(1)}, u32[]{:S(2)}, u32[]{:S(2)}) collective-permute-start(bf16[512,128]{1,0:T(8,128)(2,1)S(1)} %get-tuple-element.14), channel_id=1, source_target_pairs={{0,8},{4,12},{8,0},{12,4},{1,9},{5,13},{9,1},{13,5},{2,10},{6,14},... | collective-permute-start | bytes 393224 | tf_op jit(solution)/shard_map/reduce_keys/ppermute | solution.py:287
  125.7 5.0 %collective-permute-start.16 = (bf16[256,128]{1,0:T(8,128)(2,1)S(1)}, bf16[256,128]{1,0:T(8,128)(2,1)S(1)}, u32[]{:S(2)}, u32[]{:S(2)}) collective-permute-start(bf16[256,128]{1,0:T(8,128)(2,1)S(1)} %slice.131), channel_id=1, source_target_pairs={{0,16},{16,0},{1,17},{17,1},{2,18},{18,2},{3,19},{19,3},{4,20},{20... | collective-permute-start | bytes 196616 | tf_op jit(solution)/shard_map/reduce_keys/ppermute | solution.py:220
  126.9 11.1 %collective-permute-start.10 = (bf16[24,2048]{1,0:T(8,128)(2,1)S(1)}, bf16[24,2048]{1,0:T(8,128)(2,1)S(1)}, u32[]{:S(2)}, u32[]{:S(2)}) collective-permute-start(bf16[24,2048]{1,0:T(8,128)(2,1)S(1)} %get-tuple-element.15), channel_id=1, source_target_pairs={{0,1},{1,0},{2,3},{3,2},{4,5},{5,4},{6,7},{7,6},{8,9},{9,8},{10,11... | collective-permute-start | bytes 294920 | tf_op jit(solution)/shard_map/reduce_queries/ppermute | solution.py:224
  127.0 11.0 %collective-permute-start.12 = (bf16[24,2048]{1,0:T(8,128)(2,1)S(1)}, bf16[24,2048]{1,0:T(8,128)(2,1)S(1)}, u32[]{:S(2)}, u32[]{:S(2)}) collective-permute-start(bf16[24,2048]{1,0:T(8,128)(2,1)S(1)} %get-tuple-element.16), channel_id=1, source_target_pairs={{0,3},{1,2},{2,1},{3,0},{4,7},{5,6},{6,5},{7,4},{8,11},{9,10},{10,... | collective-permute-start | bytes 294920 | tf_op jit(solution)/shard_map/reduce_queries/ppermute | solution.py:224
  130.6 7.3 %collective-permute-start.11 = (bf16[24,2048]{1,0:T(8,128)(2,1)S(1)}, bf16[24,2048]{1,0:T(8,128)(2,1)S(1)}, u32[]{:S(2)}, u32[]{:S(2)}) collective-permute-start(bf16[24,2048]{1,0:T(8,128)(2,1)S(1)} %get-tuple-element.17), channel_id=1, source_target_pairs={{0,2},{1,3},{2,0},{3,1},{4,6},{5,7},{6,4},{7,5},{8,10},{9,11},{10,... | collective-permute-start | bytes 294920 | tf_op jit(solution)/shard_map/reduce_queries/ppermute | solution.py:224
  131.3 15.0 %all-to-all-start.1 = ((bf16[8,32,128]{2,1,0:T(8,128)(2,1)}), bf16[8,32,128]{2,1,0:T(8,128)(2,1)S(1)}, u32[]{:S(2)}, u32[]{:S(2)}) async-start(bf16[8,32,128]{2,1,0:T(8,128)(2,1)} %bitcast.15), calls=%async_computation.1 | async-start | bytes 131072 | tf_op jit(solution)/shard_map/reduce_keys/all_to_all | solution.py:295

commit v2 on v0

v2 whole, which is shorter than its diff:
```python
import functools
import math

import jax
import jax.numpy as jnp
from jax import lax
from jax.experimental import pallas as pl
from jax.experimental.pallas import tpu as pltpu
from jax.sharding import Mesh, PartitionSpec as P

DL = 576
HEADS = 64
IHEADS = 64
DI = 128
ROWS = 24
KPAD = 640
LOCAL = 16
RH = ROWS * HEADS
BLOCK = 384
KEYS = 2048
PIECE = 256
STATS = RH + 128
IQ_AT = LOCAL * DL
W_AT = IQ_AT + LOCAL * DI
RAW = W_AT + 128
FORWARD_SPLIT = True
BACKWARD_STARTS = (0, 2, 5)
VMEM_LIMIT = 28 * 1024 * 1024

negative = -1e30
loss_scale = 64.0
score_scale = 1.0 / math.sqrt(192.0)
expo_scale = score_scale / math.log(2.0)
log2e = 1.0 / math.log(2.0)
coeff = 1.0 / math.sqrt(IHEADS * DI)

CTX = ("z", "yl", "x")
HEAD = ("yh", "core")
f32 = jnp.float32
bf16 = jnp.bfloat16


def nt(left, right):
    return lax.dot_general(left, right, (((1,), (1,)), ((), ())), preferred_element_type=f32)


def nn(left, right):
    return lax.dot_general(left, right, (((1,), (0,)), ((), ())), preferred_element_type=f32)


def weight_of(q_block, at=DL):
    parts = q_block[:, at : at + 3].astype(f32)
    return parts[:, 0:1] + parts[:, 1:2] + parts[:, 2:3]


def is_logit_row():
    return lax.broadcasted_iota(jnp.int32, (1, STATS), 1) >= RH


def scale_row():
    return jnp.where(is_logit_row(), log2e, expo_scale)


def merge(pairs):
    best = pairs[0][0]
    for other, _ in pairs[1:]:
        best = jnp.maximum(best, other)
    total = None
    for other, part in pairs:
        term = part * jnp.exp2((other - best) * scale_row())
        total = term if total is None else total + term
    return best, total


def assemble_kernel(*refs):
    raws, q_ref = refs[:4], refs[4]
    lane = lax.broadcasted_iota(jnp.int32, (ROWS, 128), 1)
    for b in range(4):
        weights = raws[b][:, W_AT : W_AT + 128].astype(f32)
        for pair in range(LOCAL // 2):
            rows = []
            for j in (2 * pair, 2 * pair + 1):
                start = j * DL - (j % 2) * 64
                wide = raws[b][:, start : start + KPAD].astype(f32)
                if j % 2:
                    wide = pltpu.roll(wide, KPAD - 64, 1)
                held = pltpu.roll(weights, (64 - 8 * j) % 128, 1)
                last = jnp.where(lane < 64, wide[:, 512:], jnp.where(lane < 67, held, 0.0))
                iq = raws[b][:, IQ_AT + j * DI : IQ_AT + (j + 1) * DI].astype(f32)
                rows.append(jnp.concatenate([wide[:, :512], last, iq], axis=1))
            at = (b * LOCAL + 2 * pair) * ROWS
            q_ref[at : at + 2 * ROWS, :] = jnp.concatenate(rows, axis=0).astype(bf16)


def assemble(raws):
    return pl.pallas_call(
        assemble_kernel,
        grid=(1,),
        in_specs=[pl.BlockSpec((ROWS, RAW), lambda i: (0, 0))] * 4,
        out_specs=pl.BlockSpec((RH, KPAD + DI), lambda i: (0, 0)),
        out_shape=jax.ShapeDtypeStruct((RH, KPAD + DI), bf16),
        compiler_params=pltpu.CompilerParams(vmem_limit_bytes=VMEM_LIMIT),
        cost_estimate=pl.CostEstimate(flops=0, bytes_accessed=5000000, transcendentals=0),
        name="assemble",
    )(*raws)


def key_positions(base):
    lane = lax.broadcasted_iota(jnp.int32, (1, PIECE), 1)
    return base + (lane // 32) * 1024 + lane % 32


class Copies:
    def __init__(self, sems):
        self.sems, self.used = sems, 0

    def make(self, source, target):
        copy = pltpu.make_async_copy(source, target, self.sems.at[self.used])
        self.used += 1
        return copy


def forward_kernel(count, first, *refs):
    base_ref, pos_ref, prev_ref, q_ref = refs[:4]
    pieces = refs[4 : 4 + count]
    e_hbm, logit_hbm, stat_ref, keys_hbm = refs[4 + count : 8 + count]
    expos, logits, stat, sems = refs[8 + count :]
    copies = Copies(sems)
    weight = weight_of(q_ref[:, :KPAD])
    stores = []

    def store(source, target):
        copy = copies.make(source, target)
        copy.start()
        stores.append(copy)

    done = 0
    for j in range(count):
        kpos = key_positions(base_ref[first + j])
        bias = jnp.where(kpos <= pos_ref[:, 0:1], 0.0, negative)
        part = nt(q_ref[:, :KPAD], pieces[j][:, :KPAD])
        inner = nt(q_ref[:, KPAD:], pieces[j][:, KPAD:])
        part = (part.reshape(HEADS, ROWS, PIECE) + bias[None]).reshape(RH, PIECE)
        best = jnp.max(part, axis=1, keepdims=True)
        weighted = jnp.maximum(inner, 0.0) * weight
        logit = coeff * jnp.sum(weighted.reshape(HEADS, ROWS, PIECE), axis=0)
        logits[j] = logit
        expo = jnp.exp2((part - best) * expo_scale)
        expos[j] = expo.astype(bf16)
        stat[:RH, 2 * j : 2 * j + 1] = best
        stat[:RH, 2 * j + 1 : 2 * j + 2] = jnp.sum(expo, axis=1, keepdims=True)
        masked = logit + bias
        top = jnp.max(masked, axis=1, keepdims=True)
        stat[RH : RH + ROWS, 2 * j : 2 * j + 1] = top
        stat[RH : RH + ROWS, 2 * j + 1 : 2 * j + 2] = jnp.sum(
            jnp.exp2((masked - top) * log2e), axis=1, keepdims=True
        )
        if j + 1 == count or (count - j - 1) % 2 == 0 and FORWARD_SPLIT:
            for i in range(done, j + 1):
                store(expos.at[i], e_hbm.at[i])
                store(logits.at[i], logit_hbm.at[i])
                store(pieces[i].at[:, pl.ds(KPAD, DI)], keys_hbm.at[i])
            done = j + 1
    stat[RH + ROWS :, :] = jnp.zeros((128 - ROWS, 128), f32)
    turned = jnp.transpose(stat[...])
    pairs = [(turned[2 * j : 2 * j + 1], turned[2 * j + 1 : 2 * j + 2]) for j in range(count)]
    best, total = merge([(prev_ref[0:1, :], prev_ref[1:2, :])] + pairs)
    rows = [best, total] + [p[0] for p in pairs]
    if len(rows) < 8:
        rows.append(jnp.zeros((8 - len(rows), STATS), f32))
    stat_ref[...] = jnp.concatenate(rows, axis=0)
    for copy in stores:
        copy.wait()


def forward(bases, first, positions, prev, q_all, pieces):
    count = len(pieces)
    keys = PIECE * count
    hbm = pl.BlockSpec(memory_space=pl.ANY)
    vmem = pl.BlockSpec(memory_space=pltpu.VMEM)
    return pl.pallas_call(
        functools.partial(forward_kernel, count, first),
        in_specs=[pl.BlockSpec(memory_space=pltpu.SMEM)] + [vmem] * (3 + count),
        out_specs=[hbm, hbm, vmem, hbm],
        out_shape=[
            jax.ShapeDtypeStruct((count, RH, PIECE), bf16),
            jax.ShapeDtypeStruct((count, ROWS, PIECE), f32),
            jax.ShapeDtypeStruct((8, STATS), f32),
            jax.ShapeDtypeStruct((count, PIECE, DI), bf16),
        ],
        scratch_shapes=[
            pltpu.VMEM((count, RH, PIECE), bf16),
            pltpu.VMEM((count, ROWS, PIECE), f32),
            pltpu.VMEM((STATS, 128), f32),
            pltpu.SemaphoreType.DMA((3 * count,)),
        ],
        compiler_params=pltpu.CompilerParams(vmem_limit_bytes=VMEM_LIMIT),
        cost_estimate=pl.CostEstimate(
            flops=2 * RH * keys * 1536, bytes_accessed=2 * RH * keys, transcendentals=RH * keys
        ),
        name="forward",
    )(bases, positions, prev, q_all, *pieces)


def backward_keys_kernel(sizes, *refs):
    n = len(sizes)
    place_ref, base_ref, pos_ref = refs[:3]
    stats = refs[3 : 6 + n]
    e_hbm = refs[6 + n : 6 + 2 * n]
    logit_hbm = refs[6 + 2 * n : 6 + 3 * n]
    key_hbm = refs[6 + 3 * n : 6 + 4 * n]
    q_ref = refs[6 + 4 * n]
    dk_hbm, grad_hbm, keys_hbm = refs[7 + 4 * n : 10 + 4 * n]
    rest = refs[10 + 4 * n :]
    factor, expos, logits, keys_ref, dk_ref, grad_ref, sems = rest
    count = sum(sizes)
    flat = [(j, i) for j in range(n) for i in range(sizes[j])]
    copies = Copies(sems)
    load_e = [copies.make(e_hbm[j].at[i], expos.at[k]) for k, (j, i) in enumerate(flat)]
    load_logits = [copies.make(logit_hbm[j].at[i], logits.at[k]) for k, (j, i) in enumerate(flat)]
    load_keys = [copies.make(key_hbm[j].at[i], keys_ref.at[k]) for k, (j, i) in enumerate(flat)]

    def fetch(k):
        for load in (load_e[k], load_logits[k], load_keys[k]):
            load.start()

    for k in range(count):
        fetch(k)
    stores = []

    def store(source, target):
        copy = copies.make(source, target)
        copy.start()
        stores.append(copy)

    other_refs = stats[:3]
    stat_refs = stats[3:]
    pairs = [(stat_refs[n - 1][0:1, :], stat_refs[n - 1][1:2, :])]
    for bits in (1, 2, 3):
        got = other_refs[bits - 1]
        pair = []
        for r in range(2):
            parts = [got[r : r + 1, (s ^ bits) * 384 : (s ^ bits) * 384 + 384] for s in range(4)]
            pair.append(jnp.concatenate(parts + [got[r : r + 1, RH:]], axis=1))
        pairs.append(tuple(pair))
    gbest, total = merge(pairs)
    inverse = 1.0 / total
    rows = [inverse, gbest]
    for j, i in flat:
        rows.append(
            jnp.exp2((stat_refs[j][2 + i : 3 + i, :] - gbest) * expo_scale)
            * (inverse * (1.0 / HEADS))
        )
    rows.append(jnp.zeros((128 - len(rows), STATS), f32))
    factor[...] = jnp.transpose(jnp.concatenate(rows, axis=0))
    top = factor[RH : RH + ROWS, 1:2]
    inverse = factor[RH : RH + ROWS, 0:1]
    repeat = (
        lax.broadcasted_iota(jnp.int32, (ROWS, BLOCK), 1) % ROWS
        == lax.broadcasted_iota(jnp.int32, (ROWS, BLOCK), 0)
    ).astype(bf16)
    weight_rows = jnp.transpose(jnp.broadcast_to(coeff * weight_of(q_ref[:, :KPAD]), (RH, 128)))[0:1, :]
    done = 0
    for k in range(count):
        if k in BACKWARD_STARTS:
            upto = min([i for i in BACKWARD_STARTS if i > k] + [count])
            for i in range(k, upto):
                for load in (load_e[i], load_logits[i], load_keys[i]):
                    load.wait()
        scaled = expos[k].astype(f32) * factor[:RH, 2 + k : 3 + k]
        target = jnp.sum(scaled.reshape(HEADS, ROWS, PIECE), axis=0)
        visible = key_positions(base_ref[k]) <= pos_ref[:, 0:1]
        masked = jnp.where(visible, logits[k], negative)
        predicted = jnp.exp2((masked - top) * log2e) * inverse
        value = jnp.where(visible, loss_scale * (predicted - target), 0.0)
        rounded = value.astype(bf16)
        grad_ref[k] = rounded.astype(f32)
        spread = tn(rounded, repeat)
        dk = None
        for r in range(RH // BLOCK):
            iq = q_ref[r * BLOCK : (r + 1) * BLOCK, KPAD:]
            inner = nt(keys_ref[k], iq)
            weight = weight_rows[:, r * BLOCK : (r + 1) * BLOCK]
            head_grads = jnp.where(inner > 0.0, spread * weight, 0.0).astype(bf16)
            term = nn(head_grads, iq)
            dk = term if dk is None else dk + term
        dk_ref[k] = dk.astype(bf16)
        if k + 1 in BACKWARD_STARTS or k + 1 == count:
            for i in range(done, k + 1):
                store(dk_ref.at[i], dk_hbm.at[place_ref[i]])
                store(grad_ref.at[i], grad_hbm.at[:, pl.ds(i * PIECE, PIECE)])
                store(keys_ref.at[i], keys_hbm.at[pl.ds(i * PIECE, PIECE)])
            done = k + 1
    for copy in stores:
        copy.wait()


def tn(left, right):
    return lax.dot_general(left, right, (((0,), (0,)), ((), ())), preferred_element_type=f32)


def head_grads_of(q_ref, keys_mat, grad):
    heads = BLOCK // ROWS
    keys = keys_mat.shape[0]
    inner = nt(q_ref[:, KPAD:], keys_mat)
    weight = coeff * weight_of(q_ref[:, :KPAD])
    spread = jnp.broadcast_to(grad[None], (heads, ROWS, keys)).reshape(BLOCK, keys)
    return jnp.where(inner > 0.0, weight * spread, 0.0).astype(bf16)


def backward_keys(place, bases, positions, others, stats, expos, logits, keys_list, q_all):
    sizes = tuple(e.shape[0] for e in expos)
    count = sum(sizes)
    keys = PIECE * count
    hbm = pl.BlockSpec(memory_space=pl.ANY)
    vmem = pl.BlockSpec(memory_space=pltpu.VMEM)
    smem = pl.BlockSpec(memory_space=pltpu.SMEM)
    return pl.pallas_call(
        functools.partial(backward_keys_kernel, sizes),
        in_specs=[smem, smem] + [vmem] * (4 + len(sizes)) + [hbm] * (3 * len(sizes)) + [vmem],
        out_specs=[hbm] * 3,
        scratch_shapes=[
            pltpu.VMEM((STATS, 128), f32),
            pltpu.VMEM((count, RH, PIECE), bf16),
            pltpu.VMEM((count, ROWS, PIECE), f32),
            pltpu.VMEM((count, PIECE, DI), bf16),
            pltpu.VMEM((count, PIECE, DI), bf16),
            pltpu.VMEM((count, ROWS, PIECE), f32),
            pltpu.SemaphoreType.DMA((6 * count,)),
        ],
        out_shape=[
            jax.ShapeDtypeStruct((count, PIECE, DI), bf16),
            jax.ShapeDtypeStruct((ROWS, keys), f32),
            jax.ShapeDtypeStruct((keys, DI), bf16),
        ],
        compiler_params=pltpu.CompilerParams(vmem_limit_bytes=VMEM_LIMIT),
        cost_estimate=pl.CostEstimate(
            flops=8 * RH * keys * 128, bytes_accessed=2 * RH * keys, transcendentals=0
        ),
        name="backward_keys",
    )(place, bases, positions, *others, *stats, *expos, *logits, *keys_list, q_all)


def backward_queries_kernel(q_ref, keys_ref, grad_ref, dq_ref):
    dq = nn(head_grads_of(q_ref, keys_ref[...], grad_ref[...]), keys_ref[...])
    for j in range(BLOCK // ROWS):
        dq_ref[0, :, j * DI : (j + 1) * DI] = dq[j * ROWS : (j + 1) * ROWS].astype(bf16)


def backward_queries(q_all, iqkeys, grad):
    keys = iqkeys.shape[0]
    return pl.pallas_call(
        backward_queries_kernel,
        grid=(RH // BLOCK,),
        in_specs=[
            pl.BlockSpec((BLOCK, KPAD + DI), lambda i: (i, 0)),
            pl.BlockSpec((keys, DI), lambda i: (0, 0)),
            pl.BlockSpec((ROWS, keys), lambda i: (0, 0)),
        ],
        out_specs=pl.BlockSpec((1, ROWS, LOCAL * DI), lambda i: (i, 0, 0)),
        out_shape=jax.ShapeDtypeStruct((4, ROWS, LOCAL * DI), bf16),
        compiler_params=pltpu.CompilerParams(vmem_limit_bytes=VMEM_LIMIT),
        cost_estimate=pl.CostEstimate(
            flops=8 * RH * keys * 128, bytes_accessed=2 * RH * keys, transcendentals=0
        ),
        name="backward_queries",
    )(q_all, iqkeys, grad)


def flip(value, axis):
    return lax.ppermute(value, axis, [(0, 1), (1, 0)])


def head_xor(value, bits):
    return lax.ppermute(value, HEAD, [(i, i ^ bits) for i in range(4)])


def body(queries, kv_latent, index_queries, index_keys, head_weights, positions):
    z, yl, x = (lax.axis_index(a) for a in CTX)
    head = lax.axis_index(HEAD)
    with jax.named_scope("own_keys"):
        own_keys = jnp.concatenate(
            [
                jnp.transpose(lax.dynamic_slice_in_dim(kv_latent, head * 32, 32, 1)),
                jnp.zeros((32, KPAD - DL), bf16),
                lax.dynamic_slice_in_dim(index_keys, head * 32, 32, 0),
            ],
            axis=1,
        )
        own_keys = jnp.broadcast_to(own_keys[None], (8, 32, KPAD + DI))
        own_keys, queries, index_queries, head_weights = lax.optimization_barrier(
            (own_keys, queries, index_queries, head_weights)
        )
    with jax.named_scope("own_queries"):
        w = head_weights
        hi = lax.reduce_precision(w, 8, 7)
        mid = lax.reduce_precision(w - hi, 8, 7)
        low = w - hi - mid
        w_parts = jnp.stack([hi, mid, low] + [jnp.zeros_like(w)] * 5, axis=2).astype(bf16)
        q_own = jnp.concatenate([queries, index_queries, w_parts.reshape(ROWS, 128)], axis=1)
    with jax.named_scope("gather_queries"):
        q_yh = flip(q_own, "yh")
        q_core = flip(q_own, "core")
        q_both = flip(q_yh, "core")
        q_all = assemble([q_own, q_core, q_yh, q_both])

    def shift(value, s):
        return lax.ppermute(value, "x", [((i + s) % 4, i) for i in range(4)])

    with jax.named_scope("gather_keys"):
        p00 = lax.all_to_all(own_keys, "z", 0, 0, tiled=True).reshape(PIECE, KPAD + DI)
        p00, q_all = lax.optimization_barrier((p00, q_all))
        p01 = flip(p00, "yl")
        p10, p30 = shift(p00, 1), shift(p00, 3)
        p20 = shift(p00, 2)
        p11, p31 = shift(p01, 1), shift(p01, 3)
        p21 = flip(p20, "yl")
    groups = [
        [(0, 0, p00), (1, 0, p10), (3, 0, p30), (0, 1, p01), (2, 0, p20)],
        [(1, 1, p11), (3, 1, p31), (2, 1, p21)],
    ]
    flat = [entry for group in groups for entry in group]
    place = jnp.stack([((yl + b) % 2) * 4 + (x + s) % 4 for s, b, _ in flat])
    bases = place * 128 + head * 32
    pos = jnp.broadcast_to(positions[:, None], (ROWS, 128))
    stat = jnp.concatenate(
        [jnp.full((1, STATS), negative, f32), jnp.zeros((7, STATS), f32)], axis=0
    )
    expos, logits, stats, keys_list = [], [], [], []
    first = 0
    for group in groups:
        expo, logit, stat, keys = forward(
            bases, first, pos, stat, q_all, [p for _, _, p in group]
        )
        first += len(group)
        expos.append(expo)
        logits.append(logit)
        stats.append(stat)
        keys_list.append(keys)
    with jax.named_scope("exchange_stats"):
        others = [head_xor(stat, bits) for bits in (1, 2, 3)]
    dk, grad, iqkeys = backward_keys(
        place, bases, pos, others, stats, expos, logits, keys_list, q_all
    )
    dq = backward_queries(q_all, iqkeys, grad)
    with jax.named_scope("reduce_keys"):
        dk_xy = lax.all_to_all(dk, ("yl", "x"), 0, 0, tiled=True)
        dk_xy = jnp.sum(dk_xy.astype(f32), axis=0).astype(bf16)
        dk_z = lax.all_to_all(dk_xy.reshape(8, 32, DI), "z", 0, 0, tiled=True)
        grad_keys = jnp.sum(dk_z.astype(f32), axis=0)
    with jax.named_scope("reduce_queries"):
        grad_queries = dq[0].astype(f32)
        for bits in (1, 2, 3):
            grad_queries = grad_queries + head_xor(dq[bits], bits).astype(f32)
    return (grad_queries, grad_keys)


def solution(mesh):
    fine = Mesh(mesh.devices.reshape(8, 2, 4, 2, 2), CTX + HEAD)
    in_specs = (
        P(CTX, HEAD),
        P(None, CTX),
        P(CTX, HEAD),
        P(CTX, None),
        P(CTX, HEAD),
        P(CTX),
    )
    out_specs = (P(CTX, HEAD), P(CTX + HEAD, None))
    return jax.shard_map(body, mesh=fine, in_specs=in_specs, out_specs=out_specs, check_vma=False)
```

time: 2220 us -> 114 us (0.05)
  waiting for transfers between devices: 1810 us -> 36.9 us
  matrix products: 329 us -> 0 us
  starting transfers between devices: 0.16 us -> 35.8 us
  other arithmetic: 35.6 us -> 3.86 us
  Pallas kernels: 0 us -> 30.3 us
    reduce_scatter x1 -> x0, waiting for transfers between devices: 1230 us -> none  [body(): lax.psum_scatter(running, ('ctx', 'head'), scatter_dimension=0, tiled=True)]
    all_gather x2 -> x0, waiting for transfers between devices: 523 us -> none  [the longest x1 300 us: body(): keys_all = lax.all_gather(index_keys, 'ctx', axis=0, tiled=True)]
    dot_general x80 -> x0, matrix products: 329 us -> none  [the longest x16 92.9 us: key_add_head(): lax.dot_general(head_grads, q_head, (((0,), (0,)), ((), ())), preferred_e...]
    psum x1 -> x0, waiting for transfers between devices: 55.2 us -> none  [body(): target, logits = lax.psum((target_part, logit_part), 'head')]
    pallas_call x0 -> x5, Pallas kernels: none -> 30.3 us  [the longest x2 14.3 us: forward(): pl.pallas_call(functools.partial(forward_kernel, count, first), in_specs=...]
    mul x32 -> x0, other arithmetic: 22.2 us -> none  [the longest x16 11.2 us: back_step(): coeff * w_col]
  transfers between devices with their start and end apart: 4 -> 19, of which waited for: 4 -> 10; matrix products, arithmetic and copies ran while one was open for 4% -> 2% of each run, Pallas kernels for 0% -> 12%
where the time goes in v2:
time: 114 us; the launch traced here: 113 us
  waiting for transfers between devices  36.9 us (32%)
  starting transfers between devices  35.8 us (31%)
  Pallas kernels  30.3 us (27%)
  local copies, waits for them, and re-layouts  5.17 us (5%)
  other arithmetic  3.86 us (3%)
    pallas_call x2, Pallas kernels, forward(): pl.pallas_call(functools.partial(forward_kernel, count, first), in_specs=...  14.3 us
    pallas_call x1, Pallas kernels, backward_keys(): pl.pallas_call(functools.partial(backward_keys_kernel, sizes), in_specs=[...  10.9 us
    ppermute x5, waiting for transfers between devices, shift(): return lax.ppermute(value, 'x', [((i + s) % 4, i) for i in range(4)])  10.2 us
    ppermute x5, waiting for transfers between devices, flip(): return lax.ppermute(value, axis, [(0, 1), (1, 0)])  9.3 us
    all_to_all x1, starting transfers between devices, body(): lax.all_to_all(own_keys, 'z', 0, 0, tiled=True).reshape(PIECE, KPAD + DI)  8.6 us
    all_to_all x1, waiting for transfers between devices, body(): dk_z = lax.all_to_all(dk_xy.reshape(8, 32, DI), 'z', 0, 0, tiled=True)  7.62 us
    ppermute x6, starting transfers between devices, head_xor(): return lax.ppermute(value, HEAD, [(i, i ^ bits) for i in range(4)])  7.19 us
    all_to_all x1, waiting for transfers between devices, body(): lax.all_to_all(own_keys, 'z', 0, 0, tiled=True).reshape(PIECE, KPAD + DI)  7.09 us
  transfers between devices with their start and end apart: 19, of which 10 were waited for; matrix products, arithmetic and copies ran while one was open for 2% of the time, Pallas kernels for 12%

profile of v2, /device:TPU:2, one launch (start us, length us, event | category | flops | bytes accessed | tf_op | source)
XLA Modules:
  0.0 112.9 jit_solution(12249530856862169183)
XLA Ops:
  0.6 0.0 copy-start
  0.7 0.8 constant_dynamic-slice_fusion
  1.4 0.1 copy-done
  1.5 0.1 constant_dynamic-slice_fusion.1
  1.7 0.1 copy.29
  1.8 0.1 pad.4.clone
  1.9 0.8 broadcast_in_dim.9
  2.7 0.7 fusion.3
  3.5 0.1 stack.50
  3.5 0.1 copy.28
  3.6 0.0 copy-done.6
  3.7 3.3 %collective-permute-start.1 = (bf16[24,11392]{1,0:T(8,128)(2,1)S(1)}, bf16[24,11392]{1,0:T(8,128)(2,1)S(1)}, u32[]{:S(2)}, u32[]{:S(2)}) collective-permute-start(bf16[24,11392]{1,0:T(8,128)(2,1)S(1)} %pad_maximum_fusion.refs_0_), channel_id=1, source_target_pairs={{0,2},{2,0},{1,3},{3,1},{4,6},{6,4},{5,7},{7,5},{8,10},{10,8},{9,1... | collective-permute-start | bytes 1640456 | tf_op jit(solution)/shard_map/gather_queries/ppermute | solution.py:371
  7.0 8.6 %all-to-all-start = ((bf16[8,32,768]{2,1,0:T(8,128)(2,1)}), bf16[8,32,768]{2,1,0:T(8,128)(2,1)S(1)}, u32[]{:S(2)}, u32[]{:S(2)}) async-start(bf16[8,32,768]{2,1,0:T(8,128)(2,1)} %broadcast_in_dim.9), calls=%async_computation | async-start | bytes 786432 | tf_op jit(solution)/shard_map/gather_keys/all_to_all | solution.py:411
  15.6 0.0 collective-permute-start
  15.6 3.8 %collective-permute-done.1.refs_2_ = bf16[24,11392]{1,0:T(8,128)(2,1)S(1)} collective-permute-done((bf16[24,11392]{1,0:T(8,128)(2,1)S(1)}, bf16[24,11392]{1,0:T(8,128)(2,1)S(1)}, u32[]{:S(2)}, u32[]{:S(2)}) %collective-permute-start.1) | collective-permute-done | bytes 546848 | tf_op jit(solution)/shard_map/gather_queries/ppermute | solution.py:371
  19.4 0.0 collective-permute-start.2
  19.4 0.8 copy-done.1
  20.2 0.0 collective-permute-done.refs_1_
  20.2 1.1 collective-permute-done.2.refs_3_
  21.4 1.0 copy-done.2
  22.4 0.5 assemble.1.refs_3_.refs_14_.q_ref
  22.9 7.1 %all-to-all-done = bf16[8,32,768]{2,1,0:T(8,128)(2,1)S(1)} async-done(((bf16[8,32,768]{2,1,0:T(8,128)(2,1)}), bf16[8,32,768]{2,1,0:T(8,128)(2,1)S(1)}, u32[]{:S(2)}, u32[]{:S(2)}) %all-to-all-start) | async-done | bytes 393248 | tf_op jit(solution)/shard_map/gather_keys/all_to_all | solution.py:411
  30.0 0.7 collective-permute-start.5
  30.6 2.1 %collective-permute-start.6 = (bf16[256,768]{1,0:T(8,128)(2,1)S(1)}, bf16[256,768]{1,0:T(8,128)(2,1)}, u32[]{:S(2)}, u32[]{:S(2)}) collective-permute-start(bf16[256,768]{1,0:T(8,128)(2,1)S(1)} %bitcast.30), channel_id=1, source_target_pairs={{8,0},{12,4},{0,8},{4,12},{9,1},{13,5},{1,9},{5,13},{10,2},{14,6},... | collective-permute-start | bytes 1179656 | tf_op jit(solution)/shard_map/gather_keys/ppermute | solution.py:408
  32.8 0.0 collective-permute-start.4
  32.8 2.0 %collective-permute-start.3 = (bf16[256,768]{1,0:T(8,128)(2,1)S(1)}, bf16[256,768]{1,0:T(8,128)(2,1)}, u32[]{:S(2)}, u32[]{:S(2)}) collective-permute-start(bf16[256,768]{1,0:T(8,128)(2,1)S(1)} %bitcast.32), channel_id=1, source_target_pairs={{4,0},{8,4},{12,8},{0,12},{5,1},{9,5},{13,9},{1,13},{6,2},{10,6},{... | collective-permute-start | bytes 1179656 | tf_op jit(solution)/shard_map/gather_keys/ppermute | solution.py:408
  34.8 0.1 stack.59.refs_0_
  34.9 4.3 %collective-permute-done.5.refs_7_ = bf16[256,768]{1,0:T(8,128)(2,1)S(1)} collective-permute-done((bf16[256,768]{1,0:T(8,128)(2,1)S(1)}, bf16[256,768]{1,0:T(8,128)(2,1)S(1)}, u32[]{:S(2)}, u32[]{:S(2)}) %collective-permute-start.5) | collective-permute-done | bytes 393248 | tf_op jit(solution)/shard_map/gather_keys/ppermute | solution.py:371
  39.2 1.5 %collective-permute-start.8 = (bf16[256,768]{1,0:T(8,128)(2,1)S(1)}, bf16[256,768]{1,0:T(8,128)(2,1)S(1)}, u32[]{:S(2)}, u32[]{:S(2)}) collective-permute-start(bf16[256,768]{1,0:T(8,128)(2,1)S(1)} %collective-permute-done.5.refs_7_), channel_id=1, source_target_pairs={{12,0},{0,4},{4,8},{8,12},{13,1},{1,5},{5,9},{9,13},{14,2},{2,6},{... | collective-permute-start | bytes 1179656 | tf_op jit(solution)/shard_map/gather_keys/ppermute | solution.py:408
  40.7 0.5 collective-permute-start.7
  41.3 3.0 %collective-permute-done.6.refs_8_ = bf16[256,768]{1,0:T(8,128)(2,1)} collective-permute-done((bf16[256,768]{1,0:T(8,128)(2,1)S(1)}, bf16[256,768]{1,0:T(8,128)(2,1)}, u32[]{:S(2)}, u32[]{:S(2)}) %collective-permute-start.6) | collective-permute-done | bytes 393248 | tf_op jit(solution)/shard_map/gather_keys/ppermute | solution.py:408
  44.3 1.3 %collective-permute-start.9 = (bf16[256,768]{1,0:T(8,128)(2,1)}, bf16[256,768]{1,0:T(8,128)(2,1)S(1)}, u32[]{:S(2)}, u32[]{:S(2)}) collective-permute-start(bf16[256,768]{1,0:T(8,128)(2,1)} %collective-permute-done.6.refs_8_), channel_id=1, source_target_pairs={{0,16},{16,0},{1,17},{17,1},{2,18},{18,2},{3,19},{19,3},{4,20},{20... | collective-permute-start | bytes 1179656 | tf_op jit(solution)/shard_map/gather_keys/ppermute | solution.py:371
  45.7 7.1 %collective-permute-done.4.refs_6_ = bf16[256,768]{1,0:T(8,128)(2,1)} collective-permute-done((bf16[256,768]{1,0:T(8,128)(2,1)S(1)}, bf16[256,768]{1,0:T(8,128)(2,1)}, u32[]{:S(2)}, u32[]{:S(2)}) %collective-permute-start.4) | collective-permute-done | bytes 393248 | tf_op jit(solution)/shard_map/gather_keys/ppermute | solution.py:408
  52.8 0.0 collective-permute-done.3.refs_5_
  52.8 0.0 copy-done.8
  52.8 0.1 broadcast_in_dim.21.refs_1_.refs_2_
  52.8 9.0 %forward.2 = (bf16[5,1536,256]{2,1,0:T(8,128)(2,1)S(1)}, f32[5,24,256]{2,1,0:T(8,128)S(1)}, f32[8,1664]{1,0:T(8,128)S(1)}, bf16[5,256,128]{2,1,0:T(8,128)(2,1)S(1)}) custom-call(s32[8]{0:T(128)S(1)} %multiply_add_fusion.refs_0_.refs_1_, s32[24,128]{1,0:T(8,128)S(1)} %broadcast_in_dim.21.refs_1_.refs_2_, f32[8,1664]{1,0:T(8,128)S(1)} %copy-done.3, ...), custom_call_target="tpu_custom_call" | custom-call | flops 6039797760 | bytes 3932160 | tf_op jit(solution)/shard_map/forward/pallas_call | solution.py:181
  61.8 0.0 collective-permute-done.9.refs_6_
  61.8 0.0 collective-permute-done.8.refs_5_
  61.9 0.0 collective-permute-done.7.refs_4_
  61.9 5.3 %forward.3 = (bf16[3,1536,256]{2,1,0:T(8,128)(2,1)S(1)}, f32[3,24,256]{2,1,0:T(8,128)S(1)}, f32[8,1664]{1,0:T(8,128)S(1)}, bf16[3,256,128]{2,1,0:T(8,128)(2,1)S(1)}) custom-call(s32[8]{0:T(128)S(1)} %multiply_add_fusion.refs_0_.refs_1_, s32[24,128]{1,0:T(8,128)S(1)} %broadcast_in_dim.21.refs_1_.refs_2_, f32[8,1664]{1,0:T(8,128)S(1)} %get-tuple-element.25.refs_2_.refs_6_, ...), custom_call_target="tpu_custom_call" | custom-call | flops 3623878656 | bytes 2359296 | tf_op jit(solution)/shard_map/forward/pallas_call | solution.py:181
  67.2 0.1 collective-permute-start.12
  67.3 1.9 %collective-permute-start.11 = (f32[8,1664]{1,0:T(8,128)S(1)}, f32[8,1664]{1,0:T(8,128)S(1)}, u32[]{:S(2)}, u32[]{:S(2)}) collective-permute-start(f32[8,1664]{1,0:T(8,128)S(1)} %get-tuple-element.26.refs_7_), channel_id=1, source_target_pairs={{0,2},{1,3},{2,0},{3,1},{4,6},{5,7},{6,4},{7,5},{8,10},{9,11},{10,... | collective-permute-start | bytes 159752 | tf_op jit(solution)/shard_map/exchange_stats/ppermute | solution.py:375
  69.2 1.4 %collective-permute-start.10 = (f32[8,1664]{1,0:T(8,128)S(1)}, f32[8,1664]{1,0:T(8,128)S(1)}, u32[]{:S(2)}, u32[]{:S(2)}) collective-permute-start(f32[8,1664]{1,0:T(8,128)S(1)} %get-tuple-element.26.refs_7_), channel_id=1, source_target_pairs={{0,1},{1,0},{2,3},{3,2},{4,5},{5,4},{6,7},{7,6},{8,9},{9,8},{10,11... | collective-permute-start | bytes 159752 | tf_op jit(solution)/shard_map/exchange_stats/ppermute | solution.py:375
  70.6 1.7 %collective-permute-done.12.refs_5_ = f32[8,1664]{1,0:T(8,128)S(1)} collective-permute-done((f32[8,1664]{1,0:T(8,128)S(1)}, f32[8,1664]{1,0:T(8,128)S(1)}, u32[]{:S(2)}, u32[]{:S(2)}) %collective-permute-start.12) | collective-permute-done | bytes 53280 | tf_op jit(solution)/shard_map/exchange_stats/ppermute | solution.py:375
  72.3 0.7 collective-permute-done.11.refs_4_
  73.0 0.0 collective-permute-done.10.refs_3_
  73.0 10.9 %backward_keys.1 = (bf16[8,256,128]{2,1,0:T(8,128)(2,1)}, f32[24,2048]{1,0:T(8,128)S(1)}, bf16[2048,128]{1,0:T(8,128)(2,1)S(1)}) custom-call(s32[8]{0:T(128)S(1)} %stack.59.refs_0_, s32[8]{0:T(128)S(1)} %multiply_add_fusion.refs_0_.refs_1_, s32[24,128]{1,0:T(8,128)S(1)} %broadcast_in_dim.21.refs_1_.refs_2_, f32[8,1664]{1,0:T(8,128)S(1)} %collective-permute-done.10.refs_3_, ...), custom_call_target="tpu_custom_call" | custom-call | flops 3221225472 | bytes 6291456 | tf_op jit(solution)/shard_map/backward_keys/pallas_call | solution.py:318
  83.9 0.0 copy-start.4
  83.9 5.1 %all-to-all-start.1 = ((bf16[8,256,128]{2,1,0:T(8,128)(2,1)}), bf16[8,256,128]{2,1,0:T(8,128)(2,1)}, u32[]{:S(2)}, u32[]{:S(2)}) async-start(bf16[8,256,128]{2,1,0:T(8,128)(2,1)} %get-tuple-element.35), calls=%async_computation.1 | async-start | bytes 1048576 | tf_op jit(solution)/shard_map/reduce_keys/all_to_all | solution.py:447
  89.0 0.9 copy-done.5
  90.0 4.7 %backward_queries.1 = bf16[4,24,2048]{2,1,0:T(8,128)(2,1)S(1)} custom-call(bf16[1536,768]{1,0:T(8,128)(2,1)S(1)} %assemble.1.refs_3_.refs_14_.q_ref, bf16[2048,128]{1,0:T(8,128)(2,1)S(1)} %get-tuple-element.33.keys_ref, f32[24,2048]{1,0:T(8,128)S(1)} %copy-done.5), custom_call_target="tpu_custom_call" | custom-call | flops 3221225472 | bytes 6291456 | tf_op jit(solution)/shard_map/backward_queries/pallas_call | solution.py:352
  94.7 0.1 collective-permute-start.13
  94.8 1.7 %collective-permute-start.15 = (bf16[24,2048]{1,0:T(8,128)(2,1)S(1)}, bf16[24,2048]{1,0:T(8,128)(2,1)S(1)}, u32[]{:S(2)}, u32[]{:S(2)}) collective-permute-start(bf16[24,2048]{1,0:T(8,128)(2,1)S(1)} %get-tuple-element.37), channel_id=1, source_target_pairs={{0,3},{1,2},{2,1},{3,0},{4,7},{5,6},{6,5},{7,4},{8,11},{9,10},{10,... | collective-permute-start | bytes 294920 | tf_op jit(solution)/shard_map/reduce_queries/ppermute | solution.py:375
  96.4 2.0 %collective-permute-start.14 = (bf16[24,2048]{1,0:T(8,128)(2,1)S(1)}, bf16[24,2048]{1,0:T(8,128)(2,1)S(1)}, u32[]{:S(2)}, u32[]{:S(2)}) collective-permute-start(bf16[24,2048]{1,0:T(8,128)(2,1)S(1)} %get-tuple-element.38), channel_id=1, source_target_pairs={{0,2},{1,3},{2,0},{3,1},{4,6},{5,7},{6,4},{7,5},{8,10},{9,11},{10,... | collective-permute-start | bytes 294920 | tf_op jit(solution)/shard_map/reduce_queries/ppermute | solution.py:375
  98.4 0.4 all-to-all-done.1
  98.8 1.8 %reduce_sum.21 = bf16[256,128]{1,0:T(8,128)(2,1)} reduce(bf16[8,256,128]{2,1,0:T(8,128)(2,1)} %all-to-all-done.1, bf16[]{:T(256)} %constant.83.clone.1), dimensions={0}, to_apply=%region_0.1 | reduce | flops 229376 | bytes 589826 | tf_op jit(solution)/shard_map/reduce_keys/reduce_sum | solution.py:448
  100.5 3.4 %all-to-all-start.2 = ((bf16[8,32,128]{2,1,0:T(8,128)(2,1)}), bf16[8,32,128]{2,1,0:T(8,128)(2,1)S(1)}, u32[]{:S(2)}, u32[]{:S(2)}) async-start(bf16[8,32,128]{2,1,0:T(8,128)(2,1)} %bitcast.18), calls=%async_computation.2 | async-start | bytes 131072 | tf_op jit(solution)/shard_map/reduce_keys/all_to_all | solution.py:449
  103.9 0.0 collective-permute-done.13
  103.9 0.0 collective-permute-done.15
  103.9 0.0 collective-permute-done.14
  104.0 0.7 fusion.1
  104.7 7.6 %all-to-all-done.2 = bf16[8,32,128]{2,1,0:T(8,128)(2,1)S(1)} async-done(((bf16[8,32,128]{2,1,0:T(8,128)(2,1)}), bf16[8,32,128]{2,1,0:T(8,128)(2,1)S(1)}, u32[]{:S(2)}, u32[]{:S(2)}) %all-to-all-start.2) | async-done | bytes 65568 | tf_op jit(solution)/shard_map/reduce_keys/all_to_all | solution.py:449
  112.3 0.6 convert_reduce_fusion
  (20 shorter events, 0.1 us)
Async XLA Ops:
  0.6 0.9 copy-start
  0.6 3.0 %copy-start.7 = (bf16[24,2048]{1,0:T(8,128)(2,1)S(1)}, bf16[24,2048]{1,0:T(8,128)(2,1)}, u32[]{:S(2)}) copy-start(bf16[24,2048]{1,0:T(8,128)(2,1)} %param.8) | copy-start | bytes 294916
  0.7 3.0 %copy-start.6 = (bf16[24,9216]{1,0:T(8,128)(2,1)S(1)}, bf16[24,9216]{1,0:T(8,128)(2,1)}, u32[]{:S(2)}) copy-start(bf16[24,9216]{1,0:T(8,128)(2,1)} %param.6) | copy-start | bytes 1327108
  3.7 15.7 %collective-permute-start.1 = (bf16[24,11392]{1,0:T(8,128)(2,1)S(1)}, bf16[24,11392]{1,0:T(8,128)(2,1)S(1)}, u32[]{:S(2)}, u32[]{:S(2)}) collective-permute-start(bf16[24,11392]{1,0:T(8,128)(2,1)S(1)} %pad_maximum_fusion.refs_0_), channel_id=1, source_target_pairs={{0,2},{2,0},{1,3},{3,1},{4,6},{6,4},{5,7},{7,5},{8,10},{10,8},{9,1... | collective-permute-start | bytes 1640456 | tf_op jit(solution)/shard_map/gather_queries/ppermute | solution.py:371
  7.0 45.8 %copy-start.8 = (s32[24]{0:T(128)S(1)}, s32[24]{0:T(128)}, u32[]{:S(2)}) copy-start(s32[24]{0:T(128)} %param.11) | copy-start | bytes 292
  7.0 45.9 %copy-start.3 = (f32[8,1664]{1,0:T(8,128)S(1)}, f32[8,1664]{1,0:T(8,128)}, u32[]{:S(2)}) copy-start(f32[8,1664]{1,0:T(8,128)} %constant.90.clone.1.refs_2_) | copy-start | bytes 159748
  7.0 23.0 %all-to-all-start = ((bf16[8,32,768]{2,1,0:T(8,128)(2,1)}), bf16[8,32,768]{2,1,0:T(8,128)(2,1)S(1)}, u32[]{:S(2)}, u32[]{:S(2)}) async-start(bf16[8,32,768]{2,1,0:T(8,128)(2,1)} %broadcast_in_dim.9), calls=%async_computation | async-start | bytes 786432 | tf_op jit(solution)/shard_map/gather_keys/all_to_all | solution.py:411
  15.6 4.7 %collective-permute-start = (bf16[24,11392]{1,0:T(8,128)(2,1)S(1)}, bf16[24,11392]{1,0:T(8,128)(2,1)S(1)}, u32[]{:S(2)}, u32[]{:S(2)}) collective-permute-start(bf16[24,11392]{1,0:T(8,128)(2,1)S(1)} %pad_maximum_fusion.refs_0_), channel_id=1, source_target_pairs={{0,1},{1,0},{2,3},{3,2},{4,5},{5,4},{6,7},{7,6},{8,9},{9,8},{10,11... | collective-permute-start | bytes 1640456 | tf_op jit(solution)/shard_map/gather_queries/ppermute | solution.py:371
  19.4 1.9 %collective-permute-start.2 = (bf16[24,11392]{1,0:T(8,128)(2,1)S(1)}, bf16[24,11392]{1,0:T(8,128)(2,1)S(1)}, u32[]{:S(2)}, u32[]{:S(2)}) collective-permute-start(bf16[24,11392]{1,0:T(8,128)(2,1)S(1)} %collective-permute-done.1.refs_2_), channel_id=1, source_target_pairs={{0,1},{1,0},{2,3},{3,2},{4,5},{5,4},{6,7},{7,6},{8,9},{9,8},{10,11... | collective-permute-start | bytes 1640456 | tf_op jit(solution)/shard_map/gather_queries/ppermute | solution.py:371
  19.4 0.8 copy-start.1
  21.4 1.1 copy-start.2
  30.0 9.3 %collective-permute-start.5 = (bf16[256,768]{1,0:T(8,128)(2,1)S(1)}, bf16[256,768]{1,0:T(8,128)(2,1)S(1)}, u32[]{:S(2)}, u32[]{:S(2)}) collective-permute-start(bf16[256,768]{1,0:T(8,128)(2,1)S(1)} %bitcast.29), channel_id=1, source_target_pairs={{0,16},{16,0},{1,17},{17,1},{2,18},{18,2},{3,19},{19,3},{4,20},{20... | collective-permute-start | bytes 1179656 | tf_op jit(solution)/shard_map/gather_keys/ppermute | solution.py:371
  30.6 13.7 %collective-permute-start.6 = (bf16[256,768]{1,0:T(8,128)(2,1)S(1)}, bf16[256,768]{1,0:T(8,128)(2,1)}, u32[]{:S(2)}, u32[]{:S(2)}) collective-permute-start(bf16[256,768]{1,0:T(8,128)(2,1)S(1)} %bitcast.30), channel_id=1, source_target_pairs={{8,0},{12,4},{0,8},{4,12},{9,1},{13,5},{1,9},{5,13},{10,2},{14,6},... | collective-permute-start | bytes 1179656 | tf_op jit(solution)/shard_map/gather_keys/ppermute | solution.py:408
  32.8 20.0 %collective-permute-start.4 = (bf16[256,768]{1,0:T(8,128)(2,1)S(1)}, bf16[256,768]{1,0:T(8,128)(2,1)}, u32[]{:S(2)}, u32[]{:S(2)}) collective-permute-start(bf16[256,768]{1,0:T(8,128)(2,1)S(1)} %bitcast.31), channel_id=1, source_target_pairs={{12,0},{0,4},{4,8},{8,12},{13,1},{1,5},{5,9},{9,13},{14,2},{2,6},{... | collective-permute-start | bytes 1179656 | tf_op jit(solution)/shard_map/gather_keys/ppermute | solution.py:408
  32.8 20.0 %collective-permute-start.3 = (bf16[256,768]{1,0:T(8,128)(2,1)S(1)}, bf16[256,768]{1,0:T(8,128)(2,1)}, u32[]{:S(2)}, u32[]{:S(2)}) collective-permute-start(bf16[256,768]{1,0:T(8,128)(2,1)S(1)} %bitcast.32), channel_id=1, source_target_pairs={{4,0},{8,4},{12,8},{0,12},{5,1},{9,5},{13,9},{1,13},{6,2},{10,6},{... | collective-permute-start | bytes 1179656 | tf_op jit(solution)/shard_map/gather_keys/ppermute | solution.py:408
  39.2 22.6 %collective-permute-start.8 = (bf16[256,768]{1,0:T(8,128)(2,1)S(1)}, bf16[256,768]{1,0:T(8,128)(2,1)S(1)}, u32[]{:S(2)}, u32[]{:S(2)}) collective-permute-start(bf16[256,768]{1,0:T(8,128)(2,1)S(1)} %collective-permute-done.5.refs_7_), channel_id=1, source_target_pairs={{12,0},{0,4},{4,8},{8,12},{13,1},{1,5},{5,9},{9,13},{14,2},{2,6},{... | collective-permute-start | bytes 1179656 | tf_op jit(solution)/shard_map/gather_keys/ppermute | solution.py:408
  40.7 21.1 %collective-permute-start.7 = (bf16[256,768]{1,0:T(8,128)(2,1)S(1)}, bf16[256,768]{1,0:T(8,128)(2,1)S(1)}, u32[]{:S(2)}, u32[]{:S(2)}) collective-permute-start(bf16[256,768]{1,0:T(8,128)(2,1)S(1)} %collective-permute-done.5.refs_7_), channel_id=1, source_target_pairs={{4,0},{8,4},{12,8},{0,12},{5,1},{9,5},{13,9},{1,13},{6,2},{10,6},{... | collective-permute-start | bytes 1179656 | tf_op jit(solution)/shard_map/gather_keys/ppermute | solution.py:408
  44.3 17.5 %collective-permute-start.9 = (bf16[256,768]{1,0:T(8,128)(2,1)}, bf16[256,768]{1,0:T(8,128)(2,1)S(1)}, u32[]{:S(2)}, u32[]{:S(2)}) collective-permute-start(bf16[256,768]{1,0:T(8,128)(2,1)} %collective-permute-done.6.refs_8_), channel_id=1, source_target_pairs={{0,16},{16,0},{1,17},{17,1},{2,18},{18,2},{3,19},{19,3},{4,20},{20... | collective-permute-start | bytes 1179656 | tf_op jit(solution)/shard_map/gather_keys/ppermute | solution.py:371
  67.2 5.2 %collective-permute-start.12 = (f32[8,1664]{1,0:T(8,128)S(1)}, f32[8,1664]{1,0:T(8,128)S(1)}, u32[]{:S(2)}, u32[]{:S(2)}) collective-permute-start(f32[8,1664]{1,0:T(8,128)S(1)} %get-tuple-element.26.refs_7_), channel_id=1, source_target_pairs={{0,3},{1,2},{2,1},{3,0},{4,7},{5,6},{6,5},{7,4},{8,11},{9,10},{10,... | collective-permute-start | bytes 159752 | tf_op jit(solution)/shard_map/exchange_stats/ppermute | solution.py:375
  67.3 5.7 %collective-permute-start.11 = (f32[8,1664]{1,0:T(8,128)S(1)}, f32[8,1664]{1,0:T(8,128)S(1)}, u32[]{:S(2)}, u32[]{:S(2)}) collective-permute-start(f32[8,1664]{1,0:T(8,128)S(1)} %get-tuple-element.26.refs_7_), channel_id=1, source_target_pairs={{0,2},{1,3},{2,0},{3,1},{4,6},{5,7},{6,4},{7,5},{8,10},{9,11},{10,... | collective-permute-start | bytes 159752 | tf_op jit(solution)/shard_map/exchange_stats/ppermute | solution.py:375
  69.2 3.8 %collective-permute-start.10 = (f32[8,1664]{1,0:T(8,128)S(1)}, f32[8,1664]{1,0:T(8,128)S(1)}, u32[]{:S(2)}, u32[]{:S(2)}) collective-permute-start(f32[8,1664]{1,0:T(8,128)S(1)} %get-tuple-element.26.refs_7_), channel_id=1, source_target_pairs={{0,1},{1,0},{2,3},{3,2},{4,5},{5,4},{6,7},{7,6},{8,9},{9,8},{10,11... | collective-permute-start | bytes 159752 | tf_op jit(solution)/shard_map/exchange_stats/ppermute | solution.py:375
  83.9 5.1 %copy-start.4 = (f32[24,2048]{1,0:T(8,128)}, f32[24,2048]{1,0:T(8,128)S(1)}, u32[]{:S(2)}) copy-start(f32[24,2048]{1,0:T(8,128)S(1)} %get-tuple-element.34.grad_ref) | copy-start | bytes 589828
  83.9 14.9 %all-to-all-start.1 = ((bf16[8,256,128]{2,1,0:T(8,128)(2,1)}), bf16[8,256,128]{2,1,0:T(8,128)(2,1)}, u32[]{:S(2)}, u32[]{:S(2)}) async-start(bf16[8,256,128]{2,1,0:T(8,128)(2,1)} %get-tuple-element.35), calls=%async_computation.1 | async-start | bytes 1048576 | tf_op jit(solution)/shard_map/reduce_keys/all_to_all | solution.py:447
  89.0 0.9 copy-start.5
  94.7 9.3 %collective-permute-start.13 = (bf16[24,2048]{1,0:T(8,128)(2,1)S(1)}, bf16[24,2048]{1,0:T(8,128)(2,1)S(1)}, u32[]{:S(2)}, u32[]{:S(2)}) collective-permute-start(bf16[24,2048]{1,0:T(8,128)(2,1)S(1)} %get-tuple-element.36), channel_id=1, source_target_pairs={{0,1},{1,0},{2,3},{3,2},{4,5},{5,4},{6,7},{7,6},{8,9},{9,8},{10,11... | collective-permute-start | bytes 294920 | tf_op jit(solution)/shard_map/reduce_queries/ppermute | solution.py:375
  94.8 9.2 %collective-permute-start.15 = (bf16[24,2048]{1,0:T(8,128)(2,1)S(1)}, bf16[24,2048]{1,0:T(8,128)(2,1)S(1)}, u32[]{:S(2)}, u32[]{:S(2)}) collective-permute-start(bf16[24,2048]{1,0:T(8,128)(2,1)S(1)} %get-tuple-element.37), channel_id=1, source_target_pairs={{0,3},{1,2},{2,1},{3,0},{4,7},{5,6},{6,5},{7,4},{8,11},{9,10},{10,... | collective-permute-start | bytes 294920 | tf_op jit(solution)/shard_map/reduce_queries/ppermute | solution.py:375
  96.4 7.5 %collective-permute-start.14 = (bf16[24,2048]{1,0:T(8,128)(2,1)S(1)}, bf16[24,2048]{1,0:T(8,128)(2,1)S(1)}, u32[]{:S(2)}, u32[]{:S(2)}) collective-permute-start(bf16[24,2048]{1,0:T(8,128)(2,1)S(1)} %get-tuple-element.38), channel_id=1, source_target_pairs={{0,2},{1,3},{2,0},{3,1},{4,6},{5,7},{6,4},{7,5},{8,10},{9,11},{10,... | collective-permute-start | bytes 294920 | tf_op jit(solution)/shard_map/reduce_queries/ppermute | solution.py:375
  100.5 11.8 %all-to-all-start.2 = ((bf16[8,32,128]{2,1,0:T(8,128)(2,1)}), bf16[8,32,128]{2,1,0:T(8,128)(2,1)S(1)}, u32[]{:S(2)}, u32[]{:S(2)}) async-start(bf16[8,32,128]{2,1,0:T(8,128)(2,1)} %bitcast.18), calls=%async_computation.2 | async-start | bytes 131072 | tf_op jit(solution)/shard_map/reduce_keys/all_to_all | solution.py:449

commit v3 on v2

--- a/solution.py
+++ b/solution.py
@@ -23,8 +23,6 @@
 IQ_AT = LOCAL * DL
 W_AT = IQ_AT + LOCAL * DI
 RAW = W_AT + 128
-FORWARD_SPLIT = True
-BACKWARD_STARTS = (0, 2, 5)
 VMEM_LIMIT = 28 * 1024 * 1024
 
 negative = -1e30
@@ -110,43 +108,30 @@
     return base + (lane // 32) * 1024 + lane % 32
 
 
-class Copies:
-    def __init__(self, sems):
-        self.sems, self.used = sems, 0
-
-    def make(self, source, target):
-        copy = pltpu.make_async_copy(source, target, self.sems.at[self.used])
-        self.used += 1
-        return copy
-
-
 def forward_kernel(count, first, *refs):
     base_ref, pos_ref, prev_ref, q_ref = refs[:4]
     pieces = refs[4 : 4 + count]
-    e_hbm, logit_hbm, stat_ref, keys_hbm = refs[4 + count : 8 + count]
-    expos, logits, stat, sems = refs[8 + count :]
-    copies = Copies(sems)
+    e_ref, logit_ref, keys_ref, stat_ref, stat = refs[4 + count :]
     weight = weight_of(q_ref[:, :KPAD])
-    stores = []
-
-    def store(source, target):
-        copy = copies.make(source, target)
-        copy.start()
-        stores.append(copy)
-
-    done = 0
+
+    def products(j):
+        part = nt(q_ref[:, :KPAD], pieces[j][:, :KPAD])
+        inner = nt(q_ref[:, KPAD:], pieces[j][:, KPAD:])
+        weighted = jnp.maximum(inner, 0.0) * weight
+        return part, coeff * jnp.sum(weighted.reshape(HEADS, ROWS, PIECE), axis=0)
+
+    ready = products(0)
     for j in range(count):
+        part, logit = ready
+        if j + 1 < count:
+            ready = products(j + 1)
         kpos = key_positions(base_ref[first + j])
         bias = jnp.where(kpos <= pos_ref[:, 0:1], 0.0, negative)
-        part = nt(q_ref[:, :KPAD], pieces[j][:, :KPAD])
-        inner = nt(q_ref[:, KPAD:], pieces[j][:, KPAD:])
         part = (part.reshape(HEADS, ROWS, PIECE) + bias[None]).reshape(RH, PIECE)
         best = jnp.max(part, axis=1, keepdims=True)
-        weighted = jnp.maximum(inner, 0.0) * weight
-        logit = coeff * jnp.sum(weighted.reshape(HEADS, ROWS, PIECE), axis=0)
-        logits[j] = logit
+        logit_ref[j] = logit
         expo = jnp.exp2((part - best) * expo_scale)
-        expos[j] = expo.astype(bf16)
+        e_ref[j] = expo.astype(bf16)
         stat[:RH, 2 * j : 2 * j + 1] = best
         stat[:RH, 2 * j + 1 : 2 * j + 2] = jnp.sum(expo, axis=1, keepdims=True)
         masked = logit + bias
@@ -155,45 +140,34 @@
         stat[RH : RH + ROWS, 2 * j + 1 : 2 * j + 2] = jnp.sum(
             jnp.exp2((masked - top) * log2e), axis=1, keepdims=True
         )
-        if j + 1 == count or (count - j - 1) % 2 == 0 and FORWARD_SPLIT:
-            for i in range(done, j + 1):
-                store(expos.at[i], e_hbm.at[i])
-                store(logits.at[i], logit_hbm.at[i])
-                store(pieces[i].at[:, pl.ds(KPAD, DI)], keys_hbm.at[i])
-            done = j + 1
+        keys_ref[j] = pieces[j][:, KPAD:]
+    stat[:RH, 2 * count : 2 * count + 1] = coeff * weight
     stat[RH + ROWS :, :] = jnp.zeros((128 - ROWS, 128), f32)
     turned = jnp.transpose(stat[...])
     pairs = [(turned[2 * j : 2 * j + 1], turned[2 * j + 1 : 2 * j + 2]) for j in range(count)]
     best, total = merge([(prev_ref[0:1, :], prev_ref[1:2, :])] + pairs)
     rows = [best, total] + [p[0] for p in pairs]
-    if len(rows) < 8:
-        rows.append(jnp.zeros((8 - len(rows), STATS), f32))
+    if len(rows) < 7:
+        rows.append(jnp.zeros((7 - len(rows), STATS), f32))
+    rows.append(turned[2 * count : 2 * count + 1])
     stat_ref[...] = jnp.concatenate(rows, axis=0)
-    for copy in stores:
-        copy.wait()
 
 
 def forward(bases, first, positions, prev, q_all, pieces):
     count = len(pieces)
     keys = PIECE * count
-    hbm = pl.BlockSpec(memory_space=pl.ANY)
     vmem = pl.BlockSpec(memory_space=pltpu.VMEM)
     return pl.pallas_call(
         functools.partial(forward_kernel, count, first),
         in_specs=[pl.BlockSpec(memory_space=pltpu.SMEM)] + [vmem] * (3 + count),
-        out_specs=[hbm, hbm, vmem, hbm],
+        out_specs=[vmem] * 4,
         out_shape=[
-            jax.ShapeDtypeStruct((count, RH, PIECE), bf16),
-            jax.ShapeDtypeStruct((count, ROWS, PIECE), f32),
-            jax.ShapeDtypeStruct((8, STATS), f32),
-            jax.ShapeDtypeStruct((count, PIECE, DI), bf16),
-        ],
-        scratch_shapes=[
             pltpu.VMEM((count, RH, PIECE), bf16),
             pltpu.VMEM((count, ROWS, PIECE), f32),
-            pltpu.VMEM((STATS, 128), f32),
-            pltpu.SemaphoreType.DMA((3 * count,)),
+            pltpu.VMEM((count, PIECE, DI), bf16),
+            pltpu.VMEM((8, STATS), f32),
         ],
+        scratch_shapes=[pltpu.VMEM((STATS, 128), f32)],
         compiler_params=pltpu.CompilerParams(vmem_limit_bytes=VMEM_LIMIT),
         cost_estimate=pl.CostEstimate(
             flops=2 * RH * keys * 1536, bytes_accessed=2 * RH * keys, transcendentals=RH * keys
@@ -202,37 +176,19 @@
     )(bases, positions, prev, q_all, *pieces)
 
 
+def in_vmem(arrays):
+    return [pltpu.with_memory_space_constraint(a, pltpu.VMEM) for a in arrays]
+
+
 def backward_keys_kernel(sizes, *refs):
     n = len(sizes)
     place_ref, base_ref, pos_ref = refs[:3]
     stats = refs[3 : 6 + n]
-    e_hbm = refs[6 + n : 6 + 2 * n]
-    logit_hbm = refs[6 + 2 * n : 6 + 3 * n]
-    key_hbm = refs[6 + 3 * n : 6 + 4 * n]
-    q_ref = refs[6 + 4 * n]
-    dk_hbm, grad_hbm, keys_hbm = refs[7 + 4 * n : 10 + 4 * n]
-    rest = refs[10 + 4 * n :]
-    factor, expos, logits, keys_ref, dk_ref, grad_ref, sems = rest
-    count = sum(sizes)
+    e_refs = refs[6 + n : 6 + 2 * n]
+    logit_refs = refs[6 + 2 * n : 6 + 3 * n]
+    key_refs = refs[6 + 3 * n : 6 + 4 * n]
+    q_ref, dk_ref, grad_ref, factor = refs[6 + 4 * n :]
     flat = [(j, i) for j in range(n) for i in range(sizes[j])]
-    copies = Copies(sems)
-    load_e = [copies.make(e_hbm[j].at[i], expos.at[k]) for k, (j, i) in enumerate(flat)]
-    load_logits = [copies.make(logit_hbm[j].at[i], logits.at[k]) for k, (j, i) in enumerate(flat)]
-    load_keys = [copies.make(key_hbm[j].at[i], keys_ref.at[k]) for k, (j, i) in enumerate(flat)]
-
-    def fetch(k):
-        for load in (load_e[k], load_logits[k], load_keys[k]):
-            load.start()
-
-    for k in range(count):
-        fetch(k)
-    stores = []
-
-    def store(source, target):
-        copy = copies.make(source, target)
-        copy.start()
-        stores.append(copy)
-
     other_refs = stats[:3]
     stat_refs = stats[3:]
     pairs = [(stat_refs[n - 1][0:1, :], stat_refs[n - 1][1:2, :])]
@@ -259,40 +215,34 @@
         lax.broadcasted_iota(jnp.int32, (ROWS, BLOCK), 1) % ROWS
         == lax.broadcasted_iota(jnp.int32, (ROWS, BLOCK), 0)
     ).astype(bf16)
-    weight_rows = jnp.transpose(jnp.broadcast_to(coeff * weight_of(q_ref[:, :KPAD]), (RH, 128)))[0:1, :]
-    done = 0
-    for k in range(count):
-        if k in BACKWARD_STARTS:
-            upto = min([i for i in BACKWARD_STARTS if i > k] + [count])
-            for i in range(k, upto):
-                for load in (load_e[i], load_logits[i], load_keys[i]):
-                    load.wait()
-        scaled = expos[k].astype(f32) * factor[:RH, 2 + k : 3 + k]
-        target = jnp.sum(scaled.reshape(HEADS, ROWS, PIECE), axis=0)
-        visible = key_positions(base_ref[k]) <= pos_ref[:, 0:1]
-        masked = jnp.where(visible, logits[k], negative)
-        predicted = jnp.exp2((masked - top) * log2e) * inverse
-        value = jnp.where(visible, loss_scale * (predicted - target), 0.0)
-        rounded = value.astype(bf16)
-        grad_ref[k] = rounded.astype(f32)
-        spread = tn(rounded, repeat)
+    weight_rows = stat_refs[0][7:8, :RH]
+    at = 0
+    for j in range(n):
+        spreads = []
+        for i in range(sizes[j]):
+            k = at + i
+            scaled = e_refs[j][i].astype(f32) * factor[:RH, 2 + k : 3 + k]
+            target = jnp.sum(scaled.reshape(HEADS, ROWS, PIECE), axis=0)
+            visible = key_positions(base_ref[k]) <= pos_ref[:, 0:1]
+            masked = jnp.where(visible, logit_refs[j][i], negative)
+            predicted = jnp.exp2((masked - top) * log2e) * inverse
+            value = jnp.where(visible, loss_scale * (predicted - target), 0.0)
+            rounded = value.astype(bf16)
+            grad_ref[:, k * PIECE : (k + 1) * PIECE] = rounded.astype(f32)
+            spreads.append(tn(rounded, repeat))
+        spread = jnp.concatenate(spreads, axis=0)
+        keys_mat = key_refs[j][...].reshape(sizes[j] * PIECE, DI)
         dk = None
         for r in range(RH // BLOCK):
             iq = q_ref[r * BLOCK : (r + 1) * BLOCK, KPAD:]
-            inner = nt(keys_ref[k], iq)
+            inner = nt(keys_mat, iq)
             weight = weight_rows[:, r * BLOCK : (r + 1) * BLOCK]
             head_grads = jnp.where(inner > 0.0, spread * weight, 0.0).astype(bf16)
             term = nn(head_grads, iq)
             dk = term if dk is None else dk + term
-        dk_ref[k] = dk.astype(bf16)
-        if k + 1 in BACKWARD_STARTS or k + 1 == count:
-            for i in range(done, k + 1):
-                store(dk_ref.at[i], dk_hbm.at[place_ref[i]])
-                store(grad_ref.at[i], grad_hbm.at[:, pl.ds(i * PIECE, PIECE)])
-                store(keys_ref.at[i], keys_hbm.at[pl.ds(i * PIECE, PIECE)])
-            done = k + 1
-    for copy in stores:
-        copy.wait()
+        for i in range(sizes[j]):
+            dk_ref[place_ref[at + i]] = dk[i * PIECE : (i + 1) * PIECE].astype(bf16)
+        at += sizes[j]
 
 
 def tn(left, right):
@@ -312,59 +262,61 @@
     sizes = tuple(e.shape[0] for e in expos)
     count = sum(sizes)
     keys = PIECE * count
-    hbm = pl.BlockSpec(memory_space=pl.ANY)
     vmem = pl.BlockSpec(memory_space=pltpu.VMEM)
     smem = pl.BlockSpec(memory_space=pltpu.SMEM)
+    held = in_vmem([*stats, *expos, *logits, *keys_list])
     return pl.pallas_call(
         functools.partial(backward_keys_kernel, sizes),
-        in_specs=[smem, smem] + [vmem] * (4 + len(sizes)) + [hbm] * (3 * len(sizes)) + [vmem],
-        out_specs=[hbm] * 3,
-        scratch_shapes=[
-            pltpu.VMEM((STATS, 128), f32),
-            pltpu.VMEM((count, RH, PIECE), bf16),
-            pltpu.VMEM((count, ROWS, PIECE), f32),
-            pltpu.VMEM((count, PIECE, DI), bf16),
-            pltpu.VMEM((count, PIECE, DI), bf16),
-            pltpu.VMEM((count, ROWS, PIECE), f32),
-            pltpu.SemaphoreType.DMA((6 * count,)),
-        ],
+        in_specs=[smem, smem] + [vmem] * (5 + 4 * len(sizes)),
+        out_specs=[vmem] * 2,
+        scratch_shapes=[pltpu.VMEM((STATS, 128), f32)],
         out_shape=[
             jax.ShapeDtypeStruct((count, PIECE, DI), bf16),
             jax.ShapeDtypeStruct((ROWS, keys), f32),
-            jax.ShapeDtypeStruct((keys, DI), bf16),
         ],
         compiler_params=pltpu.CompilerParams(vmem_limit_bytes=VMEM_LIMIT),
         cost_estimate=pl.CostEstimate(
             flops=8 * RH * keys * 128, bytes_accessed=2 * RH * keys, transcendentals=0
         ),
         name="backward_keys",
-    )(place, bases, positions, *others, *stats, *expos, *logits, *keys_list, q_all)
-
-
-def backward_queries_kernel(q_ref, keys_ref, grad_ref, dq_ref):
+    )(place, bases, positions, *others, *held, q_all)
+
+
+def backward_queries_kernel(q_ref, grad_ref, *refs):
+    key_refs, dq_ref, keys_ref = refs[:-2], refs[-2], refs[-1]
+
+    @pl.when(pl.program_id(0) == 0)
+    def _():
+        at = 0
+        for ref in key_refs:
+            count = ref.shape[0]
+            keys_ref[at : at + count * PIECE, :] = ref[...].reshape(count * PIECE, DI)
+            at += count * PIECE
+
     dq = nn(head_grads_of(q_ref, keys_ref[...], grad_ref[...]), keys_ref[...])
     for j in range(BLOCK // ROWS):
         dq_ref[0, :, j * DI : (j + 1) * DI] = dq[j * ROWS : (j + 1) * ROWS].astype(bf16)
 
 
-def backward_queries(q_all, iqkeys, grad):
-    keys = iqkeys.shape[0]
+def backward_queries(q_all, keys_list, grad):
+    keys = grad.shape[1]
     return pl.pallas_call(
         backward_queries_kernel,
         grid=(RH // BLOCK,),
         in_specs=[
             pl.BlockSpec((BLOCK, KPAD + DI), lambda i: (i, 0)),
-            pl.BlockSpec((keys, DI), lambda i: (0, 0)),
             pl.BlockSpec((ROWS, keys), lambda i: (0, 0)),
-        ],
+        ]
+        + [pl.BlockSpec(k.shape, lambda i: (0, 0, 0)) for k in keys_list],
         out_specs=pl.BlockSpec((1, ROWS, LOCAL * DI), lambda i: (i, 0, 0)),
         out_shape=jax.ShapeDtypeStruct((4, ROWS, LOCAL * DI), bf16),
+        scratch_shapes=[pltpu.VMEM((keys, DI), bf16)],
         compiler_params=pltpu.CompilerParams(vmem_limit_bytes=VMEM_LIMIT),
         cost_estimate=pl.CostEstimate(
             flops=8 * RH * keys * 128, bytes_accessed=2 * RH * keys, transcendentals=0
         ),
         name="backward_queries",
-    )(q_all, iqkeys, grad)
+    )(q_all, grad, *keys_list)
 
 
 def flip(value, axis):
@@ -416,7 +368,8 @@
         p11, p31 = shift(p01, 1), shift(p01, 3)
         p21 = flip(p20, "yl")
     groups = [
-        [(0, 0, p00), (1, 0, p10), (3, 0, p30), (0, 1, p01), (2, 0, p20)],
+        [(0, 0, p00), (0, 1, p01)],
+        [(1, 0, p10), (3, 0, p30), (2, 0, p20)],
         [(1, 1, p11), (3, 1, p31), (2, 1, p21)],
     ]
     flat = [entry for group in groups for entry in group]
@@ -429,7 +382,7 @@
     expos, logits, stats, keys_list = [], [], [], []
     first = 0
     for group in groups:
-        expo, logit, stat, keys = forward(
+        expo, logit, keys, stat = forward(
             bases, first, pos, stat, q_all, [p for _, _, p in group]
         )
         first += len(group)
@@ -439,14 +392,16 @@
         keys_list.append(keys)
     with jax.named_scope("exchange_stats"):
         others = [head_xor(stat, bits) for bits in (1, 2, 3)]
-    dk, grad, iqkeys = backward_keys(
+    dk, grad = backward_keys(
         place, bases, pos, others, stats, expos, logits, keys_list, q_all
     )
-    dq = backward_queries(q_all, iqkeys, grad)
+    dq = backward_queries(q_all, keys_list, grad)
     with jax.named_scope("reduce_keys"):
         dk_xy = lax.all_to_all(dk, ("yl", "x"), 0, 0, tiled=True)
-        dk_xy = jnp.sum(dk_xy.astype(f32), axis=0).astype(bf16)
-        dk_z = lax.all_to_all(dk_xy.reshape(8, 32, DI), "z", 0, 0, tiled=True)
+        over_xy = dk_xy[0].astype(f32)
+        for j in range(1, 8):
+            over_xy = over_xy + dk_xy[j].astype(f32)
+        dk_z = lax.all_to_all(over_xy.astype(bf16).reshape(8, 32, DI), "z", 0, 0, tiled=True)
         grad_keys = jnp.sum(dk_z.astype(f32), axis=0)
     with jax.named_scope("reduce_queries"):
         grad_queries = dq[0].astype(f32)

time: 114 us -> 107 us (0.939)
  Pallas kernels: 30.3 us -> 24.1 us
  starting transfers between devices: 35.8 us -> 37.2 us
  waiting for transfers between devices: 36.9 us -> 35.5 us
    pallas_call x1, Pallas kernels: 10.9 us -> 7.12 us  [backward_keys(): pl.pallas_call(functools.partial(backward_keys_kernel, sizes), in_specs=[...]
    ppermute x5, waiting for transfers between devices: 10.2 us -> 7.56 us  [shift(): return lax.ppermute(value, 'x', [((i + s) % 4, i) for i in range(4)])]
    pallas_call x2 -> x3, Pallas kernels: 14.3 us -> 11.9 us  [forward(): pl.pallas_call(functools.partial(forward_kernel, count, first), in_specs=...]
    all_to_all x1, starting transfers between devices: 3.38 us -> 5.28 us  [body(): lax.all_to_all(over_xy.astype(bf16).reshape(8, 32, DI), 'z', 0, 0, tiled=...]
    convert_element_type x0 -> x1, other arithmetic: none -> 1.75 us  [body(): over_xy.astype(bf16).reshape(8, 32, DI)]
    reduce_sum x1 -> x0, other arithmetic: 1.75 us -> none  [body(): dk_xy = jnp.sum(dk_xy.astype(f32), axis=0).astype(bf16)]
    ppermute x6, waiting for transfers between devices: 2.38 us -> 3.84 us  [head_xor(): return lax.ppermute(value, HEAD, [(i, i ^ bits) for i in range(4)])]
where the time goes in v3:
time: 107 us
  starting transfers between devices  37.2 us (35%)
  waiting for transfers between devices  35.5 us (33%)
  Pallas kernels  24.1 us (23%)
  local copies, waits for them, and re-layouts  5.15 us (5%)
  other arithmetic  3.86 us (4%)
    pallas_call x3, Pallas kernels, forward(): pl.pallas_call(functools.partial(forward_kernel, count, first), in_specs=...  11.9 us
    ppermute x5, waiting for transfers between devices, flip(): return lax.ppermute(value, axis, [(0, 1), (1, 0)])  9.31 us
    all_to_all x1, starting transfers between devices, body(): lax.all_to_all(own_keys, 'z', 0, 0, tiled=True).reshape(PIECE, KPAD + DI)  8.6 us
    all_to_all x1, waiting for transfers between devices, body(): lax.all_to_all(over_xy.astype(bf16).reshape(8, 32, DI), 'z', 0, 0, tiled=...  7.62 us
    ppermute x5, waiting for transfers between devices, shift(): return lax.ppermute(value, 'x', [((i + s) % 4, i) for i in range(4)])  7.56 us
    ppermute x6, starting transfers between devices, head_xor(): return lax.ppermute(value, HEAD, [(i, i ^ bits) for i in range(4)])  7.2 us
    pallas_call x1, Pallas kernels, backward_keys(): pl.pallas_call(functools.partial(backward_keys_kernel, sizes), in_specs=[...  7.12 us
    all_to_all x1, waiting for transfers between devices, body(): lax.all_to_all(own_keys, 'z', 0, 0, tiled=True).reshape(PIECE, KPAD + DI)  7.09 us
  transfers between devices with their start and end apart: 19, of which 10 were waited for; matrix products, arithmetic and copies ran while one was open for 2% of the time, Pallas kernels for 12%

profile of v3, /device:TPU:2, one launch (start us, length us, event | category | flops | bytes accessed | tf_op | source)
XLA Modules:
  0.0 106.6 jit_solution(12265170658938852622)
XLA Ops:
  0.6 0.0 copy-start
  0.7 0.8 constant_dynamic-slice_fusion
  1.4 0.1 copy-done
  1.5 0.1 constant_dynamic-slice_fusion.1
  1.7 0.1 copy.24
  1.8 0.1 pad.4.clone
  1.9 0.8 broadcast_in_dim.9
  2.7 0.7 fusion.3
  3.5 0.1 stack.50
  3.5 0.1 copy.23
  3.6 0.0 copy-done.6
  3.7 3.3 %collective-permute-start.1 = (bf16[24,11392]{1,0:T(8,128)(2,1)S(1)}, bf16[24,11392]{1,0:T(8,128)(2,1)S(1)}, u32[]{:S(2)}, u32[]{:S(2)}) collective-permute-start(bf16[24,11392]{1,0:T(8,128)(2,1)S(1)} %pad_maximum_fusion.refs_0_), channel_id=1, source_target_pairs={{0,2},{2,0},{1,3},{3,1},{4,6},{6,4},{5,7},{7,5},{8,10},{10,8},{9,1... | collective-permute-start | bytes 1640456 | tf_op jit(solution)/shard_map/gather_queries/ppermute | solution.py:323
  7.0 8.6 %all-to-all-start = ((bf16[8,32,768]{2,1,0:T(8,128)(2,1)}), bf16[8,32,768]{2,1,0:T(8,128)(2,1)S(1)}, u32[]{:S(2)}, u32[]{:S(2)}) async-start(bf16[8,32,768]{2,1,0:T(8,128)(2,1)} %broadcast_in_dim.9), calls=%async_computation | async-start | bytes 786432 | tf_op jit(solution)/shard_map/gather_keys/all_to_all | solution.py:363
  15.6 0.0 collective-permute-start
  15.6 3.8 %collective-permute-done.1.refs_2_ = bf16[24,11392]{1,0:T(8,128)(2,1)S(1)} collective-permute-done((bf16[24,11392]{1,0:T(8,128)(2,1)S(1)}, bf16[24,11392]{1,0:T(8,128)(2,1)S(1)}, u32[]{:S(2)}, u32[]{:S(2)}) %collective-permute-start.1) | collective-permute-done | bytes 546848 | tf_op jit(solution)/shard_map/gather_queries/ppermute | solution.py:323
  19.4 0.0 collective-permute-start.2
  19.4 0.8 copy-done.1
  20.2 0.0 collective-permute-done.refs_1_
  20.2 1.1 %collective-permute-done.2.refs_3_ = bf16[24,11392]{1,0:T(8,128)(2,1)S(1)} collective-permute-done((bf16[24,11392]{1,0:T(8,128)(2,1)S(1)}, bf16[24,11392]{1,0:T(8,128)(2,1)S(1)}, u32[]{:S(2)}, u32[]{:S(2)}) %collective-permute-start.2) | collective-permute-done | bytes 546848 | tf_op jit(solution)/shard_map/gather_queries/ppermute | solution.py:323
  21.4 1.0 copy-done.2
  22.4 0.5 assemble.1.refs_3_.refs_18_.q_ref
  22.9 7.1 %all-to-all-done = bf16[8,32,768]{2,1,0:T(8,128)(2,1)S(1)} async-done(((bf16[8,32,768]{2,1,0:T(8,128)(2,1)}), bf16[8,32,768]{2,1,0:T(8,128)(2,1)S(1)}, u32[]{:S(2)}, u32[]{:S(2)}) %all-to-all-start) | async-done | bytes 393248 | tf_op jit(solution)/shard_map/gather_keys/all_to_all | solution.py:363
  30.0 0.7 collective-permute-start.3
  30.7 2.1 %collective-permute-start.6 = (bf16[256,768]{1,0:T(8,128)(2,1)S(1)}, bf16[256,768]{1,0:T(8,128)(2,1)}, u32[]{:S(2)}, u32[]{:S(2)}) collective-permute-start(bf16[256,768]{1,0:T(8,128)(2,1)S(1)} %bitcast.30), channel_id=1, source_target_pairs={{8,0},{12,4},{0,8},{4,12},{9,1},{13,5},{1,9},{5,13},{10,2},{14,6},... | collective-permute-start | bytes 1179656 | tf_op jit(solution)/shard_map/gather_keys/ppermute | solution.py:360
  32.8 0.1 stack.59.refs_0_
  32.9 0.0 collective-permute-start.5
  32.9 2.0 %collective-permute-start.4 = (bf16[256,768]{1,0:T(8,128)(2,1)S(1)}, bf16[256,768]{1,0:T(8,128)(2,1)S(1)}, u32[]{:S(2)}, u32[]{:S(2)}) collective-permute-start(bf16[256,768]{1,0:T(8,128)(2,1)S(1)} %bitcast.32), channel_id=1, source_target_pairs={{4,0},{8,4},{12,8},{0,12},{5,1},{9,5},{13,9},{1,13},{6,2},{10,6},{... | collective-permute-start | bytes 1179656 | tf_op jit(solution)/shard_map/gather_keys/ppermute | solution.py:360
  34.9 4.3 %collective-permute-done.3.refs_5_ = bf16[256,768]{1,0:T(8,128)(2,1)S(1)} collective-permute-done((bf16[256,768]{1,0:T(8,128)(2,1)S(1)}, bf16[256,768]{1,0:T(8,128)(2,1)S(1)}, u32[]{:S(2)}, u32[]{:S(2)}) %collective-permute-start.3) | collective-permute-done | bytes 393248 | tf_op jit(solution)/shard_map/gather_keys/ppermute | solution.py:323
  39.2 1.5 %collective-permute-start.8 = (bf16[256,768]{1,0:T(8,128)(2,1)S(1)}, bf16[256,768]{1,0:T(8,128)(2,1)S(1)}, u32[]{:S(2)}, u32[]{:S(2)}) collective-permute-start(bf16[256,768]{1,0:T(8,128)(2,1)S(1)} %collective-permute-done.3.refs_5_), channel_id=1, source_target_pairs={{12,0},{0,4},{4,8},{8,12},{13,1},{1,5},{5,9},{9,13},{14,2},{2,6},{... | collective-permute-start | bytes 1179656 | tf_op jit(solution)/shard_map/gather_keys/ppermute | solution.py:360
  40.7 0.5 collective-permute-start.7
  41.3 3.0 %collective-permute-done.6.refs_6_ = bf16[256,768]{1,0:T(8,128)(2,1)} collective-permute-done((bf16[256,768]{1,0:T(8,128)(2,1)S(1)}, bf16[256,768]{1,0:T(8,128)(2,1)}, u32[]{:S(2)}, u32[]{:S(2)}) %collective-permute-start.6) | collective-permute-done | bytes 393248 | tf_op jit(solution)/shard_map/gather_keys/ppermute | solution.py:360
  44.3 1.3 %collective-permute-start.9 = (bf16[256,768]{1,0:T(8,128)(2,1)}, bf16[256,768]{1,0:T(8,128)(2,1)S(1)}, u32[]{:S(2)}, u32[]{:S(2)}) collective-permute-start(bf16[256,768]{1,0:T(8,128)(2,1)} %collective-permute-done.6.refs_6_), channel_id=1, source_target_pairs={{0,16},{16,0},{1,17},{17,1},{2,18},{18,2},{3,19},{19,3},{4,20},{20... | collective-permute-start | bytes 1179656 | tf_op jit(solution)/shard_map/gather_keys/ppermute | solution.py:323
  45.7 0.1 broadcast_in_dim.21.refs_1_.refs_2_
  45.7 3.2 %forward.3 = (bf16[2,1536,256]{2,1,0:T(8,128)(2,1)S(1)}, f32[2,24,256]{2,1,0:T(8,128)S(1)}, bf16[2,256,128]{2,1,0:T(8,128)(2,1)S(1)}, f32[8,1664]{1,0:T(8,128)S(1)}) custom-call(s32[8]{0:T(128)S(1)} %multiply_add_fusion.refs_0_.refs_1_, s32[24,128]{1,0:T(8,128)S(1)} %broadcast_in_dim.21.refs_1_.refs_2_, f32[8,1664]{1,0:T(8,128)S(1)} %copy-done.3, ...), custom_call_target="tpu_custom_call" | custom-call | flops 2415919104 | bytes 1572864 | tf_op jit(solution)/shard_map/forward/pallas_call | solution.py:160
  49.0 0.0 copy-start.4
  49.0 3.7 %collective-permute-done.5.refs_5_ = bf16[256,768]{1,0:T(8,128)(2,1)S(1)} collective-permute-done((bf16[256,768]{1,0:T(8,128)(2,1)S(1)}, bf16[256,768]{1,0:T(8,128)(2,1)S(1)}, u32[]{:S(2)}, u32[]{:S(2)}) %collective-permute-start.5) | collective-permute-done | bytes 393248 | tf_op jit(solution)/shard_map/gather_keys/ppermute | solution.py:360
  52.7 0.0 collective-permute-done.4.refs_4_
  52.7 4.6 %forward.4 = (bf16[3,1536,256]{2,1,0:T(8,128)(2,1)S(1)}, f32[3,24,256]{2,1,0:T(8,128)S(1)}, bf16[3,256,128]{2,1,0:T(8,128)(2,1)S(1)}, f32[8,1664]{1,0:T(8,128)S(1)}) custom-call(s32[8]{0:T(128)S(1)} %multiply_add_fusion.refs_0_.refs_1_, s32[24,128]{1,0:T(8,128)S(1)} %broadcast_in_dim.21.refs_1_.refs_2_, f32[8,1664]{1,0:T(8,128)S(1)} %get-tuple-element.28.refs_2_.refs_6_, ...), custom_call_target="tpu_custom_call" | custom-call | flops 3623878656 | bytes 2359296 | tf_op jit(solution)/shard_map/forward/pallas_call | solution.py:160
  57.2 0.0 collective-permute-done.9.refs_6_
  57.2 0.8 collective-permute-done.8.refs_5_
  58.1 0.0 collective-permute-done.7.refs_4_
  58.1 4.1 %forward.5 = (bf16[3,1536,256]{2,1,0:T(8,128)(2,1)S(1)}, f32[3,24,256]{2,1,0:T(8,128)S(1)}, bf16[3,256,128]{2,1,0:T(8,128)(2,1)S(1)}, f32[8,1664]{1,0:T(8,128)S(1)}) custom-call(s32[8]{0:T(128)S(1)} %multiply_add_fusion.refs_0_.refs_1_, s32[24,128]{1,0:T(8,128)S(1)} %broadcast_in_dim.21.refs_1_.refs_2_, f32[8,1664]{1,0:T(8,128)S(1)} %get-tuple-element.29.refs_2_.refs_7_, ...), custom_call_target="tpu_custom_call" | custom-call | flops 3623878656 | bytes 2359296 | tf_op jit(solution)/shard_map/forward/pallas_call | solution.py:160
  62.2 1.5 %collective-permute-start.12 = (f32[8,1664]{1,0:T(8,128)S(1)}, f32[8,1664]{1,0:T(8,128)S(1)}, u32[]{:S(2)}, u32[]{:S(2)}) collective-permute-start(f32[8,1664]{1,0:T(8,128)S(1)} %get-tuple-element.30.refs_8_), channel_id=1, source_target_pairs={{0,3},{1,2},{2,1},{3,0},{4,7},{5,6},{6,5},{7,4},{8,11},{9,10},{10,... | collective-permute-start | bytes 159752 | tf_op jit(solution)/shard_map/exchange_stats/ppermute | solution.py:327
  63.6 1.7 %collective-permute-start.11 = (f32[8,1664]{1,0:T(8,128)S(1)}, f32[8,1664]{1,0:T(8,128)S(1)}, u32[]{:S(2)}, u32[]{:S(2)}) collective-permute-start(f32[8,1664]{1,0:T(8,128)S(1)} %get-tuple-element.30.refs_8_), channel_id=1, source_target_pairs={{0,2},{1,3},{2,0},{3,1},{4,6},{5,7},{6,4},{7,5},{8,10},{9,11},{10,... | collective-permute-start | bytes 159752 | tf_op jit(solution)/shard_map/exchange_stats/ppermute | solution.py:327
  65.3 0.3 collective-permute-start.10
  65.6 2.1 %collective-permute-done.12.refs_5_ = f32[8,1664]{1,0:T(8,128)S(1)} collective-permute-done((f32[8,1664]{1,0:T(8,128)S(1)}, f32[8,1664]{1,0:T(8,128)S(1)}, u32[]{:S(2)}, u32[]{:S(2)}) %collective-permute-start.12) | collective-permute-done | bytes 53280 | tf_op jit(solution)/shard_map/exchange_stats/ppermute | solution.py:327
  67.8 1.7 %collective-permute-done.11.refs_4_ = f32[8,1664]{1,0:T(8,128)S(1)} collective-permute-done((f32[8,1664]{1,0:T(8,128)S(1)}, f32[8,1664]{1,0:T(8,128)S(1)}, u32[]{:S(2)}, u32[]{:S(2)}) %collective-permute-start.11) | collective-permute-done | bytes 53280 | tf_op jit(solution)/shard_map/exchange_stats/ppermute | solution.py:327
  69.5 0.0 collective-permute-done.10.refs_3_
  69.5 7.1 %backward_keys.1 = (bf16[8,256,128]{2,1,0:T(8,128)(2,1)}, f32[24,2048]{1,0:T(8,128)S(1)}) custom-call(s32[8]{0:T(128)S(1)} %stack.59.refs_0_, s32[8]{0:T(128)S(1)} %multiply_add_fusion.refs_0_.refs_1_, s32[24,128]{1,0:T(8,128)S(1)} %broadcast_in_dim.21.refs_1_.refs_2_, f32[8,1664]{1,0:T(8,128)S(1)} %collective-permute-done.10.refs_3_, ...), custom_call_target="tpu_custom_call" | custom-call | flops 3221225472 | bytes 6291456 | tf_op jit(solution)/shard_map/backward_keys/pallas_call | solution.py:268
  76.6 4.6 %all-to-all-start.1 = ((bf16[8,256,128]{2,1,0:T(8,128)(2,1)}), bf16[8,256,128]{2,1,0:T(8,128)(2,1)}, u32[]{:S(2)}, u32[]{:S(2)}) async-start(bf16[8,256,128]{2,1,0:T(8,128)(2,1)} %get-tuple-element.41), calls=%async_computation.1 | async-start | bytes 1048576 | tf_op jit(solution)/shard_map/reduce_keys/all_to_all | solution.py:400
  81.2 0.9 copy-done.5
  82.1 4.7 %backward_queries.1 = bf16[4,24,2048]{2,1,0:T(8,128)(2,1)S(1)} custom-call(bf16[1536,768]{1,0:T(8,128)(2,1)S(1)} %assemble.1.refs_3_.refs_18_.q_ref, f32[24,2048]{1,0:T(8,128)S(1)} %get-tuple-element.40.grad_ref, bf16[2,256,128]{2,1,0:T(8,128)(2,1)S(1)} %copy-done.5, bf16[3,256,128]{2,1,0:T(8,128)(2,1)S(1)} %get-tuple-element.38.refs_16_.refs_1_, ...), custom_call_target="tpu_custom_call" | custom-call | flops 3221225472 | bytes 6291456 | tf_op jit(solution)/shard_map/backward_queries/pallas_call | solution.py:303
  86.8 0.1 collective-permute-start.13
  86.9 3.1 %collective-permute-start.15 = (bf16[24,2048]{1,0:T(8,128)(2,1)S(1)}, bf16[24,2048]{1,0:T(8,128)(2,1)S(1)}, u32[]{:S(2)}, u32[]{:S(2)}) collective-permute-start(bf16[24,2048]{1,0:T(8,128)(2,1)S(1)} %get-tuple-element.43), channel_id=1, source_target_pairs={{0,3},{1,2},{2,1},{3,0},{4,7},{5,6},{6,5},{7,4},{8,11},{9,10},{10,... | collective-permute-start | bytes 294920 | tf_op jit(solution)/shard_map/reduce_queries/ppermute | solution.py:327
  90.0 0.6 collective-permute-start.14
  90.6 0.0 all-to-all-done.1
  90.6 1.8 %add_convert_fusion = bf16[1,256,128]{2,1,0:T(8,128)(2,1)} fusion(bf16[8,256,128]{2,1,0:T(8,128)(2,1)} %all-to-all-done.1), kind=kLoop, calls=%fused_computation.4 | loop fusion | flops 524288 | bytes 589824 | tf_op jit(solution)/shard_map/reduce_keys/convert_element_type | solution.py:404
  92.4 5.3 %all-to-all-start.2 = ((bf16[8,32,128]{2,1,0:T(8,128)(2,1)}), bf16[8,32,128]{2,1,0:T(8,128)(2,1)S(1)}, u32[]{:S(2)}, u32[]{:S(2)}) async-start(bf16[8,32,128]{2,1,0:T(8,128)(2,1)} %bitcast.18), calls=%async_computation.2 | async-start | bytes 131072 | tf_op jit(solution)/shard_map/reduce_keys/all_to_all | solution.py:404
  97.6 0.0 collective-permute-done.13
  97.7 0.0 collective-permute-done.15
  97.7 0.0 collective-permute-done.14
  97.7 0.7 fusion.1
  98.4 7.6 %all-to-all-done.2 = bf16[8,32,128]{2,1,0:T(8,128)(2,1)S(1)} async-done(((bf16[8,32,128]{2,1,0:T(8,128)(2,1)}), bf16[8,32,128]{2,1,0:T(8,128)(2,1)S(1)}, u32[]{:S(2)}, u32[]{:S(2)}) %all-to-all-start.2) | async-done | bytes 65568 | tf_op jit(solution)/shard_map/reduce_keys/all_to_all | solution.py:404
  106.0 0.6 convert_reduce_fusion
  (21 shorter events, 0.1 us)
Async XLA Ops:
  0.6 0.9 copy-start
  0.6 3.0 %copy-start.7 = (bf16[24,2048]{1,0:T(8,128)(2,1)S(1)}, bf16[24,2048]{1,0:T(8,128)(2,1)}, u32[]{:S(2)}) copy-start(bf16[24,2048]{1,0:T(8,128)(2,1)} %param.8) | copy-start | bytes 294916
  0.7 3.0 %copy-start.6 = (bf16[24,9216]{1,0:T(8,128)(2,1)S(1)}, bf16[24,9216]{1,0:T(8,128)(2,1)}, u32[]{:S(2)}) copy-start(bf16[24,9216]{1,0:T(8,128)(2,1)} %param.6) | copy-start | bytes 1327108
  3.7 15.7 %collective-permute-start.1 = (bf16[24,11392]{1,0:T(8,128)(2,1)S(1)}, bf16[24,11392]{1,0:T(8,128)(2,1)S(1)}, u32[]{:S(2)}, u32[]{:S(2)}) collective-permute-start(bf16[24,11392]{1,0:T(8,128)(2,1)S(1)} %pad_maximum_fusion.refs_0_), channel_id=1, source_target_pairs={{0,2},{2,0},{1,3},{3,1},{4,6},{6,4},{5,7},{7,5},{8,10},{10,8},{9,1... | collective-permute-start | bytes 1640456 | tf_op jit(solution)/shard_map/gather_queries/ppermute | solution.py:323
  7.0 38.7 %copy-start.8 = (s32[24]{0:T(128)S(1)}, s32[24]{0:T(128)}, u32[]{:S(2)}) copy-start(s32[24]{0:T(128)} %param.11) | copy-start | bytes 292
  7.0 38.8 %copy-start.3 = (f32[8,1664]{1,0:T(8,128)S(1)}, f32[8,1664]{1,0:T(8,128)}, u32[]{:S(2)}) copy-start(f32[8,1664]{1,0:T(8,128)} %constant.89.clone.1.refs_2_) | copy-start | bytes 159748
  7.0 23.0 %all-to-all-start = ((bf16[8,32,768]{2,1,0:T(8,128)(2,1)}), bf16[8,32,768]{2,1,0:T(8,128)(2,1)S(1)}, u32[]{:S(2)}, u32[]{:S(2)}) async-start(bf16[8,32,768]{2,1,0:T(8,128)(2,1)} %broadcast_in_dim.9), calls=%async_computation | async-start | bytes 786432 | tf_op jit(solution)/shard_map/gather_keys/all_to_all | solution.py:363
  15.6 4.7 %collective-permute-start = (bf16[24,11392]{1,0:T(8,128)(2,1)S(1)}, bf16[24,11392]{1,0:T(8,128)(2,1)S(1)}, u32[]{:S(2)}, u32[]{:S(2)}) collective-permute-start(bf16[24,11392]{1,0:T(8,128)(2,1)S(1)} %pad_maximum_fusion.refs_0_), channel_id=1, source_target_pairs={{0,1},{1,0},{2,3},{3,2},{4,5},{5,4},{6,7},{7,6},{8,9},{9,8},{10,11... | collective-permute-start | bytes 1640456 | tf_op jit(solution)/shard_map/gather_queries/ppermute | solution.py:323
  19.4 1.9 %collective-permute-start.2 = (bf16[24,11392]{1,0:T(8,128)(2,1)S(1)}, bf16[24,11392]{1,0:T(8,128)(2,1)S(1)}, u32[]{:S(2)}, u32[]{:S(2)}) collective-permute-start(bf16[24,11392]{1,0:T(8,128)(2,1)S(1)} %collective-permute-done.1.refs_2_), channel_id=1, source_target_pairs={{0,1},{1,0},{2,3},{3,2},{4,5},{5,4},{6,7},{7,6},{8,9},{9,8},{10,11... | collective-permute-start | bytes 1640456 | tf_op jit(solution)/shard_map/gather_queries/ppermute | solution.py:323
  19.4 0.8 copy-start.1
  21.4 1.1 copy-start.2
  30.0 9.3 %collective-permute-start.3 = (bf16[256,768]{1,0:T(8,128)(2,1)S(1)}, bf16[256,768]{1,0:T(8,128)(2,1)S(1)}, u32[]{:S(2)}, u32[]{:S(2)}) collective-permute-start(bf16[256,768]{1,0:T(8,128)(2,1)S(1)} %bitcast.29), channel_id=1, source_target_pairs={{0,16},{16,0},{1,17},{17,1},{2,18},{18,2},{3,19},{19,3},{4,20},{20... | collective-permute-start | bytes 1179656 | tf_op jit(solution)/shard_map/gather_keys/ppermute | solution.py:323
  30.7 13.7 %collective-permute-start.6 = (bf16[256,768]{1,0:T(8,128)(2,1)S(1)}, bf16[256,768]{1,0:T(8,128)(2,1)}, u32[]{:S(2)}, u32[]{:S(2)}) collective-permute-start(bf16[256,768]{1,0:T(8,128)(2,1)S(1)} %bitcast.30), channel_id=1, source_target_pairs={{8,0},{12,4},{0,8},{4,12},{9,1},{13,5},{1,9},{5,13},{10,2},{14,6},... | collective-permute-start | bytes 1179656 | tf_op jit(solution)/shard_map/gather_keys/ppermute | solution.py:360
  32.9 19.8 %collective-permute-start.5 = (bf16[256,768]{1,0:T(8,128)(2,1)S(1)}, bf16[256,768]{1,0:T(8,128)(2,1)S(1)}, u32[]{:S(2)}, u32[]{:S(2)}) collective-permute-start(bf16[256,768]{1,0:T(8,128)(2,1)S(1)} %bitcast.31), channel_id=1, source_target_pairs={{12,0},{0,4},{4,8},{8,12},{13,1},{1,5},{5,9},{9,13},{14,2},{2,6},{... | collective-permute-start | bytes 1179656 | tf_op jit(solution)/shard_map/gather_keys/ppermute | solution.py:360
  32.9 19.8 %collective-permute-start.4 = (bf16[256,768]{1,0:T(8,128)(2,1)S(1)}, bf16[256,768]{1,0:T(8,128)(2,1)S(1)}, u32[]{:S(2)}, u32[]{:S(2)}) collective-permute-start(bf16[256,768]{1,0:T(8,128)(2,1)S(1)} %bitcast.32), channel_id=1, source_target_pairs={{4,0},{8,4},{12,8},{0,12},{5,1},{9,5},{13,9},{1,13},{6,2},{10,6},{... | collective-permute-start | bytes 1179656 | tf_op jit(solution)/shard_map/gather_keys/ppermute | solution.py:360
  39.2 18.8 %collective-permute-start.8 = (bf16[256,768]{1,0:T(8,128)(2,1)S(1)}, bf16[256,768]{1,0:T(8,128)(2,1)S(1)}, u32[]{:S(2)}, u32[]{:S(2)}) collective-permute-start(bf16[256,768]{1,0:T(8,128)(2,1)S(1)} %collective-permute-done.3.refs_5_), channel_id=1, source_target_pairs={{12,0},{0,4},{4,8},{8,12},{13,1},{1,5},{5,9},{9,13},{14,2},{2,6},{... | collective-permute-start | bytes 1179656 | tf_op jit(solution)/shard_map/gather_keys/ppermute | solution.py:360
  40.7 17.3 %collective-permute-start.7 = (bf16[256,768]{1,0:T(8,128)(2,1)S(1)}, bf16[256,768]{1,0:T(8,128)(2,1)S(1)}, u32[]{:S(2)}, u32[]{:S(2)}) collective-permute-start(bf16[256,768]{1,0:T(8,128)(2,1)S(1)} %collective-permute-done.3.refs_5_), channel_id=1, source_target_pairs={{4,0},{8,4},{12,8},{0,12},{5,1},{9,5},{13,9},{1,13},{6,2},{10,6},{... | collective-permute-start | bytes 1179656 | tf_op jit(solution)/shard_map/gather_keys/ppermute | solution.py:360
  44.3 12.9 %collective-permute-start.9 = (bf16[256,768]{1,0:T(8,128)(2,1)}, bf16[256,768]{1,0:T(8,128)(2,1)S(1)}, u32[]{:S(2)}, u32[]{:S(2)}) collective-permute-start(bf16[256,768]{1,0:T(8,128)(2,1)} %collective-permute-done.6.refs_6_), channel_id=1, source_target_pairs={{0,16},{16,0},{1,17},{17,1},{2,18},{18,2},{3,19},{19,3},{4,20},{20... | collective-permute-start | bytes 1179656 | tf_op jit(solution)/shard_map/gather_keys/ppermute | solution.py:323
  49.0 20.5 %copy-start.4 = (bf16[2,256,128]{2,1,0:T(8,128)(2,1)}, bf16[2,256,128]{2,1,0:T(8,128)(2,1)S(1)}, u32[]{:S(2)}) copy-start(bf16[2,256,128]{2,1,0:T(8,128)(2,1)S(1)} %get-tuple-element.37.refs_15_.refs_0_) | copy-start | bytes 393220
  62.2 5.6 %collective-permute-start.12 = (f32[8,1664]{1,0:T(8,128)S(1)}, f32[8,1664]{1,0:T(8,128)S(1)}, u32[]{:S(2)}, u32[]{:S(2)}) collective-permute-start(f32[8,1664]{1,0:T(8,128)S(1)} %get-tuple-element.30.refs_8_), channel_id=1, source_target_pairs={{0,3},{1,2},{2,1},{3,0},{4,7},{5,6},{6,5},{7,4},{8,11},{9,10},{10,... | collective-permute-start | bytes 159752 | tf_op jit(solution)/shard_map/exchange_stats/ppermute | solution.py:327
  63.6 5.8 %collective-permute-start.11 = (f32[8,1664]{1,0:T(8,128)S(1)}, f32[8,1664]{1,0:T(8,128)S(1)}, u32[]{:S(2)}, u32[]{:S(2)}) collective-permute-start(f32[8,1664]{1,0:T(8,128)S(1)} %get-tuple-element.30.refs_8_), channel_id=1, source_target_pairs={{0,2},{1,3},{2,0},{3,1},{4,6},{5,7},{6,4},{7,5},{8,10},{9,11},{10,... | collective-permute-start | bytes 159752 | tf_op jit(solution)/shard_map/exchange_stats/ppermute | solution.py:327
  65.3 4.1 %collective-permute-start.10 = (f32[8,1664]{1,0:T(8,128)S(1)}, f32[8,1664]{1,0:T(8,128)S(1)}, u32[]{:S(2)}, u32[]{:S(2)}) collective-permute-start(f32[8,1664]{1,0:T(8,128)S(1)} %get-tuple-element.30.refs_8_), channel_id=1, source_target_pairs={{0,1},{1,0},{2,3},{3,2},{4,5},{5,4},{6,7},{7,6},{8,9},{9,8},{10,11... | collective-permute-start | bytes 159752 | tf_op jit(solution)/shard_map/exchange_stats/ppermute | solution.py:327
  76.6 14.0 %all-to-all-start.1 = ((bf16[8,256,128]{2,1,0:T(8,128)(2,1)}), bf16[8,256,128]{2,1,0:T(8,128)(2,1)}, u32[]{:S(2)}, u32[]{:S(2)}) async-start(bf16[8,256,128]{2,1,0:T(8,128)(2,1)} %get-tuple-element.41), calls=%async_computation.1 | async-start | bytes 1048576 | tf_op jit(solution)/shard_map/reduce_keys/all_to_all | solution.py:400
  81.2 0.9 copy-start.5
  86.8 10.8 %collective-permute-start.13 = (bf16[24,2048]{1,0:T(8,128)(2,1)S(1)}, bf16[24,2048]{1,0:T(8,128)(2,1)S(1)}, u32[]{:S(2)}, u32[]{:S(2)}) collective-permute-start(bf16[24,2048]{1,0:T(8,128)(2,1)S(1)} %get-tuple-element.42), channel_id=1, source_target_pairs={{0,1},{1,0},{2,3},{3,2},{4,5},{5,4},{6,7},{7,6},{8,9},{9,8},{10,11... | collective-permute-start | bytes 294920 | tf_op jit(solution)/shard_map/reduce_queries/ppermute | solution.py:327
  86.9 10.7 %collective-permute-start.15 = (bf16[24,2048]{1,0:T(8,128)(2,1)S(1)}, bf16[24,2048]{1,0:T(8,128)(2,1)S(1)}, u32[]{:S(2)}, u32[]{:S(2)}) collective-permute-start(bf16[24,2048]{1,0:T(8,128)(2,1)S(1)} %get-tuple-element.43), channel_id=1, source_target_pairs={{0,3},{1,2},{2,1},{3,0},{4,7},{5,6},{6,5},{7,4},{8,11},{9,10},{10,... | collective-permute-start | bytes 294920 | tf_op jit(solution)/shard_map/reduce_queries/ppermute | solution.py:327
  90.0 7.7 %collective-permute-start.14 = (bf16[24,2048]{1,0:T(8,128)(2,1)S(1)}, bf16[24,2048]{1,0:T(8,128)(2,1)S(1)}, u32[]{:S(2)}, u32[]{:S(2)}) collective-permute-start(bf16[24,2048]{1,0:T(8,128)(2,1)S(1)} %get-tuple-element.44), channel_id=1, source_target_pairs={{0,2},{1,3},{2,0},{3,1},{4,6},{5,7},{6,4},{7,5},{8,10},{9,11},{10,... | collective-permute-start | bytes 294920 | tf_op jit(solution)/shard_map/reduce_queries/ppermute | solution.py:327
  92.4 13.7 %all-to-all-start.2 = ((bf16[8,32,128]{2,1,0:T(8,128)(2,1)}), bf16[8,32,128]{2,1,0:T(8,128)(2,1)S(1)}, u32[]{:S(2)}, u32[]{:S(2)}) async-start(bf16[8,32,128]{2,1,0:T(8,128)(2,1)} %bitcast.18), calls=%async_computation.2 | async-start | bytes 131072 | tf_op jit(solution)/shard_map/reduce_keys/all_to_all | solution.py:404

commit v4 on v3

--- a/solution.py
+++ b/solution.py
@@ -23,6 +23,8 @@
 IQ_AT = LOCAL * DL
 W_AT = IQ_AT + LOCAL * DI
 RAW = W_AT + 128
+HALF = PIECE // 2
+PACKED = 1408
 VMEM_LIMIT = 28 * 1024 * 1024
 
 negative = -1e30
@@ -105,18 +107,35 @@
 
 def key_positions(base):
     lane = lax.broadcasted_iota(jnp.int32, (1, PIECE), 1)
-    return base + (lane // 32) * 1024 + lane % 32
+    return base + (lane % HALF // 16) * 1024 + lane % 16 + lane // HALF * 16
+
+
+def unpack(piece):
+    tails = piece[:, 1024:1152].astype(f32)
+    keep = lax.broadcasted_iota(jnp.int32, (HALF, 128), 1) < KPAD - DL
+    first = jnp.where(keep, tails, 0.0).astype(bf16)
+    second = jnp.where(keep, pltpu.roll(tails, 64, 1), 0.0).astype(bf16)
+    latents = jnp.concatenate(
+        [
+            jnp.concatenate([piece[:, :512], first], axis=1),
+            jnp.concatenate([piece[:, 512:1024], second], axis=1),
+        ],
+        axis=0,
+    )
+    return latents, jnp.concatenate([piece[:, 1152:1280], piece[:, 1280:]], axis=0)
 
 
 def forward_kernel(count, first, *refs):
     base_ref, pos_ref, prev_ref, q_ref = refs[:4]
     pieces = refs[4 : 4 + count]
-    e_ref, logit_ref, keys_ref, stat_ref, stat = refs[4 + count :]
+    e_ref, logit_ref, keys_ref, own_ref, total_ref, stat = refs[4 + count :]
     weight = weight_of(q_ref[:, :KPAD])
 
     def products(j):
-        part = nt(q_ref[:, :KPAD], pieces[j][:, :KPAD])
-        inner = nt(q_ref[:, KPAD:], pieces[j][:, KPAD:])
+        latents, index_part = unpack(pieces[j][...])
+        keys_ref[j] = index_part
+        part = nt(q_ref[:, :KPAD], latents)
+        inner = nt(q_ref[:, KPAD:], index_part)
         weighted = jnp.maximum(inner, 0.0) * weight
         return part, coeff * jnp.sum(weighted.reshape(HEADS, ROWS, PIECE), axis=0)
 
@@ -140,17 +159,15 @@
         stat[RH : RH + ROWS, 2 * j + 1 : 2 * j + 2] = jnp.sum(
             jnp.exp2((masked - top) * log2e), axis=1, keepdims=True
         )
-        keys_ref[j] = pieces[j][:, KPAD:]
     stat[:RH, 2 * count : 2 * count + 1] = coeff * weight
     stat[RH + ROWS :, :] = jnp.zeros((128 - ROWS, 128), f32)
     turned = jnp.transpose(stat[...])
     pairs = [(turned[2 * j : 2 * j + 1], turned[2 * j + 1 : 2 * j + 2]) for j in range(count)]
     best, total = merge([(prev_ref[0:1, :], prev_ref[1:2, :])] + pairs)
-    rows = [best, total] + [p[0] for p in pairs]
-    if len(rows) < 7:
-        rows.append(jnp.zeros((7 - len(rows), STATS), f32))
-    rows.append(turned[2 * count : 2 * count + 1])
-    stat_ref[...] = jnp.concatenate(rows, axis=0)
+    total_ref[...] = jnp.concatenate([best, total], axis=0)
+    rows = [turned[2 * count : 2 * count + 1]] + [p[0] for p in pairs]
+    rows.append(jnp.zeros((8 - len(rows), STATS), f32))
+    own_ref[...] = jnp.concatenate(rows, axis=0)
 
 
 def forward(bases, first, positions, prev, q_all, pieces):
@@ -160,12 +177,13 @@
     return pl.pallas_call(
         functools.partial(forward_kernel, count, first),
         in_specs=[pl.BlockSpec(memory_space=pltpu.SMEM)] + [vmem] * (3 + count),
-        out_specs=[vmem] * 4,
+        out_specs=[vmem] * 5,
         out_shape=[
             pltpu.VMEM((count, RH, PIECE), bf16),
             pltpu.VMEM((count, ROWS, PIECE), f32),
             pltpu.VMEM((count, PIECE, DI), bf16),
             pltpu.VMEM((8, STATS), f32),
+            pltpu.VMEM((2, STATS), f32),
         ],
         scratch_shapes=[pltpu.VMEM((STATS, 128), f32)],
         compiler_params=pltpu.CompilerParams(vmem_limit_bytes=VMEM_LIMIT),
@@ -183,17 +201,16 @@
 def backward_keys_kernel(sizes, *refs):
     n = len(sizes)
     place_ref, base_ref, pos_ref = refs[:3]
-    stats = refs[3 : 6 + n]
-    e_refs = refs[6 + n : 6 + 2 * n]
-    logit_refs = refs[6 + 2 * n : 6 + 3 * n]
-    key_refs = refs[6 + 3 * n : 6 + 4 * n]
-    q_ref, dk_ref, grad_ref, factor = refs[6 + 4 * n :]
+    total_refs = refs[3:7]
+    stat_refs = refs[7 : 7 + n]
+    e_refs = refs[7 + n : 7 + 2 * n]
+    logit_refs = refs[7 + 2 * n : 7 + 3 * n]
+    key_refs = refs[7 + 3 * n : 7 + 4 * n]
+    q_ref, dk_ref, grad_ref, factor = refs[7 + 4 * n :]
     flat = [(j, i) for j in range(n) for i in range(sizes[j])]
-    other_refs = stats[:3]
-    stat_refs = stats[3:]
-    pairs = [(stat_refs[n - 1][0:1, :], stat_refs[n - 1][1:2, :])]
+    pairs = [(total_refs[0][0:1, :], total_refs[0][1:2, :])]
     for bits in (1, 2, 3):
-        got = other_refs[bits - 1]
+        got = total_refs[bits]
         pair = []
         for r in range(2):
             parts = [got[r : r + 1, (s ^ bits) * 384 : (s ^ bits) * 384 + 384] for s in range(4)]
@@ -204,7 +221,7 @@
     rows = [inverse, gbest]
     for j, i in flat:
         rows.append(
-            jnp.exp2((stat_refs[j][2 + i : 3 + i, :] - gbest) * expo_scale)
+            jnp.exp2((stat_refs[j][1 + i : 2 + i, :] - gbest) * expo_scale)
             * (inverse * (1.0 / HEADS))
         )
     rows.append(jnp.zeros((128 - len(rows), STATS), f32))
@@ -215,7 +232,7 @@
         lax.broadcasted_iota(jnp.int32, (ROWS, BLOCK), 1) % ROWS
         == lax.broadcasted_iota(jnp.int32, (ROWS, BLOCK), 0)
     ).astype(bf16)
-    weight_rows = stat_refs[0][7:8, :RH]
+    weight_rows = stat_refs[0][0:1, :RH]
     at = 0
     for j in range(n):
         spreads = []
@@ -267,7 +284,7 @@
     held = in_vmem([*stats, *expos, *logits, *keys_list])
     return pl.pallas_call(
         functools.partial(backward_keys_kernel, sizes),
-        in_specs=[smem, smem] + [vmem] * (5 + 4 * len(sizes)),
+        in_specs=[smem, smem] + [vmem] * (6 + 4 * len(sizes)),
         out_specs=[vmem] * 2,
         scratch_shapes=[pltpu.VMEM((STATS, 128), f32)],
         out_shape=[
@@ -331,15 +348,12 @@
     z, yl, x = (lax.axis_index(a) for a in CTX)
     head = lax.axis_index(HEAD)
     with jax.named_scope("own_keys"):
+        kv = jnp.transpose(lax.dynamic_slice_in_dim(kv_latent, head * 32, 32, 1))
+        ik = lax.dynamic_slice_in_dim(index_keys, head * 32, 32, 0)
         own_keys = jnp.concatenate(
-            [
-                jnp.transpose(lax.dynamic_slice_in_dim(kv_latent, head * 32, 32, 1)),
-                jnp.zeros((32, KPAD - DL), bf16),
-                lax.dynamic_slice_in_dim(index_keys, head * 32, 32, 0),
-            ],
-            axis=1,
-        )
-        own_keys = jnp.broadcast_to(own_keys[None], (8, 32, KPAD + DI))
+            [kv[:16, :512], kv[16:, :512], kv[:16, 512:], kv[16:, 512:], ik[:16], ik[16:]], axis=1
+        )
+        own_keys = jnp.broadcast_to(own_keys[None], (8, 16, PACKED))
         own_keys, queries, index_queries, head_weights = lax.optimization_barrier(
             (own_keys, queries, index_queries, head_weights)
         )
@@ -360,7 +374,7 @@
         return lax.ppermute(value, "x", [((i + s) % 4, i) for i in range(4)])
 
     with jax.named_scope("gather_keys"):
-        p00 = lax.all_to_all(own_keys, "z", 0, 0, tiled=True).reshape(PIECE, KPAD + DI)
+        p00 = lax.all_to_all(own_keys, "z", 0, 0, tiled=True).reshape(HALF, PACKED)
         p00, q_all = lax.optimization_barrier((p00, q_all))
         p01 = flip(p00, "yl")
         p10, p30 = shift(p00, 1), shift(p00, 3)
@@ -377,23 +391,23 @@
     bases = place * 128 + head * 32
     pos = jnp.broadcast_to(positions[:, None], (ROWS, 128))
     stat = jnp.concatenate(
-        [jnp.full((1, STATS), negative, f32), jnp.zeros((7, STATS), f32)], axis=0
+        [jnp.full((1, STATS), negative, f32), jnp.zeros((1, STATS), f32)], axis=0
     )
     expos, logits, stats, keys_list = [], [], [], []
     first = 0
     for group in groups:
-        expo, logit, keys, stat = forward(
+        expo, logit, keys, own, stat = forward(
             bases, first, pos, stat, q_all, [p for _, _, p in group]
         )
         first += len(group)
         expos.append(expo)
         logits.append(logit)
-        stats.append(stat)
+        stats.append(own)
         keys_list.append(keys)
     with jax.named_scope("exchange_stats"):
         others = [head_xor(stat, bits) for bits in (1, 2, 3)]
     dk, grad = backward_keys(
-        place, bases, pos, others, stats, expos, logits, keys_list, q_all
+        place, bases, pos, [stat] + others, stats, expos, logits, keys_list, q_all
     )
     dq = backward_queries(q_all, keys_list, grad)
     with jax.named_scope("reduce_keys"):
@@ -401,7 +415,10 @@
         over_xy = dk_xy[0].astype(f32)
         for j in range(1, 8):
             over_xy = over_xy + dk_xy[j].astype(f32)
-        dk_z = lax.all_to_all(over_xy.astype(bf16).reshape(8, 32, DI), "z", 0, 0, tiled=True)
+        over_xy = over_xy.astype(bf16).reshape(2, 8, 16, DI)
+        dk_z = lax.all_to_all(
+            jnp.transpose(over_xy, (1, 0, 2, 3)).reshape(8, 32, DI), "z", 0, 0, tiled=True
+        )
         grad_keys = jnp.sum(dk_z.astype(f32), axis=0)
     with jax.named_scope("reduce_queries"):
         grad_queries = dq[0].astype(f32)

time: 107 us -> 104 us (0.972)
  waiting for transfers between devices: 35.5 us -> 32 us
  other arithmetic: 3.86 us -> 2.53 us
  local copies, waits for them, and re-layouts: 5.15 us -> 6.47 us
    all_to_all x2, starting transfers between devices: 13.9 us -> 15.2 us  [the longest x1 8.6 us: body(): p00 = lax.all_to_all(own_keys, 'z', 0, 0, tiled=True).reshape(HALF, PACKED)]
    ppermute x5, waiting for transfers between devices: 9.31 us -> 8.13 us  [flip(): return lax.ppermute(value, axis, [(0, 1), (1, 0)])]
    unnamed x19 -> x21, local copies, waits for them, and re-layouts: 3.04 us -> 3.79 us
  transfers between devices with their start and end apart: 19 -> 19, of which waited for: 10 -> 10; matrix products, arithmetic and copies ran while one was open for 2% -> 3% of each run, Pallas kernels for 12% -> 12%
where the time goes in v4:
time: 104 us
  starting transfers between devices  38 us (37%)
  waiting for transfers between devices  32 us (31%)
  Pallas kernels  24 us (23%)
  local copies, waits for them, and re-layouts  6.47 us (6%)
  other arithmetic  2.53 us (2%)
    pallas_call x3, Pallas kernels, forward(): pl.pallas_call(functools.partial(forward_kernel, count, first), in_specs=...  11.8 us
    all_to_all x1, starting transfers between devices, body(): p00 = lax.all_to_all(own_keys, 'z', 0, 0, tiled=True).reshape(HALF, PACKED)  8.6 us
    ppermute x5, waiting for transfers between devices, flip(): return lax.ppermute(value, axis, [(0, 1), (1, 0)])  8.13 us
    all_to_all x1, waiting for transfers between devices, body(): lax.all_to_all(jnp.transpose(over_xy, (1, 0, 2, 3)).reshape(8, 32, DI), '...  7.62 us
    ppermute x6, starting transfers between devices, head_xor(): return lax.ppermute(value, HEAD, [(i, i ^ bits) for i in range(4)])  7.2 us
    pallas_call x1, Pallas kernels, backward_keys(): pl.pallas_call(functools.partial(backward_keys_kernel, sizes), in_specs=[...  7.03 us
    all_to_all x1, starting transfers between devices, body(): lax.all_to_all(jnp.transpose(over_xy, (1, 0, 2, 3)).reshape(8, 32, DI), '...  6.56 us
    ppermute x5, waiting for transfers between devices, shift(): return lax.ppermute(value, 'x', [((i + s) % 4, i) for i in range(4)])  6.51 us
  transfers between devices with their start and end apart: 19, of which 10 were waited for; matrix products, arithmetic and copies ran while one was open for 3% of the time, Pallas kernels for 12%

profile of v4, /device:TPU:2, one launch (start us, length us, event | category | flops | bytes accessed | tf_op | source)
XLA Modules:
  0.0 103.8 jit_solution(492965308996549743)
XLA Ops:
  0.6 0.0 copy-start
  0.7 0.9 copy-done
  1.5 0.1 constant_dynamic-slice_fusion.2
  1.7 0.1 copy.28
  1.8 0.7 constant_dynamic-slice_fusion.1
  2.5 0.1 concatenate.6
  2.6 0.8 broadcast_in_dim.6
  3.5 0.1 stack.50
  3.6 0.1 copy.26
  3.6 0.0 copy-done.6
  3.7 3.3 %collective-permute-start.1 = (bf16[24,11392]{1,0:T(8,128)(2,1)S(1)}, bf16[24,11392]{1,0:T(8,128)(2,1)S(1)}, u32[]{:S(2)}, u32[]{:S(2)}) collective-permute-start(bf16[24,11392]{1,0:T(8,128)(2,1)S(1)} %pad_maximum_fusion.refs_0_), channel_id=1, source_target_pairs={{0,2},{2,0},{1,3},{3,1},{4,6},{6,4},{5,7},{7,5},{8,10},{10,8},{9,1... | collective-permute-start | bytes 1640456 | tf_op jit(solution)/shard_map/gather_queries/ppermute | solution.py:340
  7.0 8.6 %all-to-all-start = ((bf16[8,16,1408]{2,1,0:T(8,128)(2,1)}), bf16[8,16,1408]{2,1,0:T(8,128)(2,1)S(1)}, u32[]{:S(2)}, u32[]{:S(2)}) async-start(bf16[8,16,1408]{2,1,0:T(8,128)(2,1)} %broadcast_in_dim.6), calls=%async_computation | async-start | bytes 720896 | tf_op jit(solution)/shard_map/gather_keys/all_to_all | solution.py:377
  15.6 0.0 collective-permute-start
  15.6 3.8 %collective-permute-done.1.refs_2_ = bf16[24,11392]{1,0:T(8,128)(2,1)S(1)} collective-permute-done((bf16[24,11392]{1,0:T(8,128)(2,1)S(1)}, bf16[24,11392]{1,0:T(8,128)(2,1)S(1)}, u32[]{:S(2)}, u32[]{:S(2)}) %collective-permute-start.1) | collective-permute-done | bytes 546848 | tf_op jit(solution)/shard_map/gather_queries/ppermute | solution.py:340
  19.4 0.0 collective-permute-start.2
  19.4 0.8 copy-done.1
  20.2 0.0 collective-permute-done.refs_1_
  20.2 1.1 %collective-permute-done.2.refs_3_ = bf16[24,11392]{1,0:T(8,128)(2,1)S(1)} collective-permute-done((bf16[24,11392]{1,0:T(8,128)(2,1)S(1)}, bf16[24,11392]{1,0:T(8,128)(2,1)S(1)}, u32[]{:S(2)}, u32[]{:S(2)}) %collective-permute-start.2) | collective-permute-done | bytes 546848 | tf_op jit(solution)/shard_map/gather_queries/ppermute | solution.py:340
  21.4 1.0 %copy-done.2 = bf16[24,11392]{1,0:T(8,128)(2,1)S(1)} copy-done((bf16[24,11392]{1,0:T(8,128)(2,1)S(1)}, bf16[24,11392]{1,0:T(8,128)(2,1)}, u32[]{:S(2)}) %copy-start.2) | copy-done | bytes 546840
  22.4 0.5 assemble.1.refs_3_.refs_19_.q_ref
  22.9 6.4 %all-to-all-done = bf16[8,16,1408]{2,1,0:T(8,128)(2,1)S(1)} async-done(((bf16[8,16,1408]{2,1,0:T(8,128)(2,1)}), bf16[8,16,1408]{2,1,0:T(8,128)(2,1)S(1)}, u32[]{:S(2)}, u32[]{:S(2)}) %all-to-all-start) | async-done | bytes 360480 | tf_op jit(solution)/shard_map/gather_keys/all_to_all | solution.py:377
  29.3 0.7 collective-permute-start.3
  30.0 2.1 %collective-permute-start.6 = (bf16[128,1408]{1,0:T(8,128)(2,1)S(1)}, bf16[128,1408]{1,0:T(8,128)(2,1)}, u32[]{:S(2)}, u32[]{:S(2)}) collective-permute-start(bf16[128,1408]{1,0:T(8,128)(2,1)S(1)} %bitcast.33), channel_id=1, source_target_pairs={{8,0},{12,4},{0,8},{4,12},{9,1},{13,5},{1,9},{5,13},{10,2},{14,6},... | collective-permute-start | bytes 1081352 | tf_op jit(solution)/shard_map/gather_keys/ppermute | solution.py:374
  32.1 0.1 stack.59.refs_0_
  32.2 0.0 collective-permute-start.5
  32.2 2.0 %collective-permute-start.4 = (bf16[128,1408]{1,0:T(8,128)(2,1)S(1)}, bf16[128,1408]{1,0:T(8,128)(2,1)S(1)}, u32[]{:S(2)}, u32[]{:S(2)}) collective-permute-start(bf16[128,1408]{1,0:T(8,128)(2,1)S(1)} %bitcast.35), channel_id=1, source_target_pairs={{4,0},{8,4},{12,8},{0,12},{5,1},{9,5},{13,9},{1,13},{6,2},{10,6},{... | collective-permute-start | bytes 1081352 | tf_op jit(solution)/shard_map/gather_keys/ppermute | solution.py:374
  34.2 3.2 %collective-permute-done.3.refs_5_ = bf16[128,1408]{1,0:T(8,128)(2,1)S(1)} collective-permute-done((bf16[128,1408]{1,0:T(8,128)(2,1)S(1)}, bf16[128,1408]{1,0:T(8,128)(2,1)S(1)}, u32[]{:S(2)}, u32[]{:S(2)}) %collective-permute-start.3) | collective-permute-done | bytes 360480 | tf_op jit(solution)/shard_map/gather_keys/ppermute | solution.py:340
  37.4 1.5 %collective-permute-start.8 = (bf16[128,1408]{1,0:T(8,128)(2,1)S(1)}, bf16[128,1408]{1,0:T(8,128)(2,1)S(1)}, u32[]{:S(2)}, u32[]{:S(2)}) collective-permute-start(bf16[128,1408]{1,0:T(8,128)(2,1)S(1)} %collective-permute-done.3.refs_5_), channel_id=1, source_target_pairs={{12,0},{0,4},{4,8},{8,12},{13,1},{1,5},{5,9},{9,13},{14,2},{2,6},{... | collective-permute-start | bytes 1081352 | tf_op jit(solution)/shard_map/gather_keys/ppermute | solution.py:374
  38.9 0.5 collective-permute-start.7
  39.4 3.5 %collective-permute-done.6.refs_6_ = bf16[128,1408]{1,0:T(8,128)(2,1)} collective-permute-done((bf16[128,1408]{1,0:T(8,128)(2,1)S(1)}, bf16[128,1408]{1,0:T(8,128)(2,1)}, u32[]{:S(2)}, u32[]{:S(2)}) %collective-permute-start.6) | collective-permute-done | bytes 360480 | tf_op jit(solution)/shard_map/gather_keys/ppermute | solution.py:374
  42.9 1.3 %collective-permute-start.9 = (bf16[128,1408]{1,0:T(8,128)(2,1)}, bf16[128,1408]{1,0:T(8,128)(2,1)S(1)}, u32[]{:S(2)}, u32[]{:S(2)}) collective-permute-start(bf16[128,1408]{1,0:T(8,128)(2,1)} %collective-permute-done.6.refs_6_), channel_id=1, source_target_pairs={{0,16},{16,0},{1,17},{17,1},{2,18},{18,2},{3,19},{19,3},{4,20},{20... | collective-permute-start | bytes 1081352 | tf_op jit(solution)/shard_map/gather_keys/ppermute | solution.py:340
  44.3 0.1 broadcast_in_dim.8.refs_1_.refs_2_
  44.3 3.2 %forward.3 = (bf16[2,1536,256]{2,1,0:T(8,128)(2,1)S(1)}, f32[2,24,256]{2,1,0:T(8,128)S(1)}, bf16[2,256,128]{2,1,0:T(8,128)(2,1)S(1)}, f32[8,1664]{1,0:T(8,128)S(1)}, f32[2,1664]{1,0:T(2,128)S(1)}) custom-call(s32[8]{0:T(128)S(1)} %multiply_add_fusion.refs_0_.refs_1_, s32[24,128]{1,0:T(8,128)S(1)} %broadcast_in_dim.8.refs_1_.refs_2_, ...), custom_call_target="tpu_custom_call" | custom-call | flops 2415919104 | bytes 1572864 | tf_op jit(solution)/shard_map/forward/pallas_call | solution.py:177
  47.6 0.0 copy-start.4
  47.6 3.0 %collective-permute-done.5.refs_5_ = bf16[128,1408]{1,0:T(8,128)(2,1)S(1)} collective-permute-done((bf16[128,1408]{1,0:T(8,128)(2,1)S(1)}, bf16[128,1408]{1,0:T(8,128)(2,1)S(1)}, u32[]{:S(2)}, u32[]{:S(2)}) %collective-permute-start.5) | collective-permute-done | bytes 360480 | tf_op jit(solution)/shard_map/gather_keys/ppermute | solution.py:374
  50.6 0.0 collective-permute-done.4.refs_4_
  50.6 4.5 %forward.4 = (bf16[3,1536,256]{2,1,0:T(8,128)(2,1)S(1)}, f32[3,24,256]{2,1,0:T(8,128)S(1)}, bf16[3,256,128]{2,1,0:T(8,128)(2,1)S(1)}, f32[8,1664]{1,0:T(8,128)S(1)}, f32[2,1664]{1,0:T(2,128)S(1)}) custom-call(s32[8]{0:T(128)S(1)} %multiply_add_fusion.refs_0_.refs_1_, s32[24,128]{1,0:T(8,128)S(1)} %broadcast_in_dim.8.refs_1_.refs_2_, ...), custom_call_target="tpu_custom_call" | custom-call | flops 3623878656 | bytes 2359296 | tf_op jit(solution)/shard_map/forward/pallas_call | solution.py:177
  55.1 0.0 collective-permute-done.9.refs_6_
  55.1 0.0 collective-permute-done.8.refs_5_
  55.1 0.0 collective-permute-done.7.refs_4_
  55.1 4.1 %forward.5 = (bf16[3,1536,256]{2,1,0:T(8,128)(2,1)S(1)}, f32[3,24,256]{2,1,0:T(8,128)S(1)}, bf16[3,256,128]{2,1,0:T(8,128)(2,1)S(1)}, f32[8,1664]{1,0:T(8,128)S(1)}, f32[2,1664]{1,0:T(2,128)S(1)}) custom-call(s32[8]{0:T(128)S(1)} %multiply_add_fusion.refs_0_.refs_1_, s32[24,128]{1,0:T(8,128)S(1)} %broadcast_in_dim.8.refs_1_.refs_2_, ...), custom_call_target="tpu_custom_call" | custom-call | flops 3623878656 | bytes 2359296 | tf_op jit(solution)/shard_map/forward/pallas_call | solution.py:177
  59.2 1.1 %collective-permute-start.12 = (f32[2,1664]{1,0:T(2,128)S(1)}, f32[2,1664]{1,0:T(2,128)S(1)}, u32[]{:S(2)}, u32[]{:S(2)}) collective-permute-start(f32[2,1664]{1,0:T(2,128)S(1)} %get-tuple-element.33.refs_3_), channel_id=1, source_target_pairs={{0,3},{1,2},{2,1},{3,0},{4,7},{5,6},{6,5},{7,4},{8,11},{9,10},{10,... | collective-permute-start | bytes 39944 | tf_op jit(solution)/shard_map/exchange_stats/ppermute | solution.py:344
  60.4 1.7 %collective-permute-start.11 = (f32[2,1664]{1,0:T(2,128)S(1)}, f32[2,1664]{1,0:T(2,128)S(1)}, u32[]{:S(2)}, u32[]{:S(2)}) collective-permute-start(f32[2,1664]{1,0:T(2,128)S(1)} %get-tuple-element.33.refs_3_), channel_id=1, source_target_pairs={{0,2},{1,3},{2,0},{3,1},{4,6},{5,7},{6,4},{7,5},{8,10},{9,11},{10,... | collective-permute-start | bytes 39944 | tf_op jit(solution)/shard_map/exchange_stats/ppermute | solution.py:344
  62.0 0.6 collective-permute-start.10
  62.7 1.3 %collective-permute-done.12.refs_6_ = f32[2,1664]{1,0:T(2,128)S(1)} collective-permute-done((f32[2,1664]{1,0:T(2,128)S(1)}, f32[2,1664]{1,0:T(2,128)S(1)}, u32[]{:S(2)}, u32[]{:S(2)}) %collective-permute-start.12) | collective-permute-done | bytes 13344 | tf_op jit(solution)/shard_map/exchange_stats/ppermute | solution.py:344
  63.9 1.7 %collective-permute-done.11.refs_5_ = f32[2,1664]{1,0:T(2,128)S(1)} collective-permute-done((f32[2,1664]{1,0:T(2,128)S(1)}, f32[2,1664]{1,0:T(2,128)S(1)}, u32[]{:S(2)}, u32[]{:S(2)}) %collective-permute-start.11) | collective-permute-done | bytes 13344 | tf_op jit(solution)/shard_map/exchange_stats/ppermute | solution.py:344
  65.6 0.0 collective-permute-done.10.refs_4_
  65.7 7.0 %backward_keys.1 = (bf16[8,256,128]{2,1,0:T(8,128)(2,1)}, f32[24,2048]{1,0:T(8,128)S(1)}) custom-call(s32[8]{0:T(128)S(1)} %stack.59.refs_0_, s32[8]{0:T(128)S(1)} %multiply_add_fusion.refs_0_.refs_1_, s32[24,128]{1,0:T(8,128)S(1)} %broadcast_in_dim.8.refs_1_.refs_2_, f32[2,1664]{1,0:T(2,128)S(1)} %get-tuple-element.33.refs_3_, ...), custom_call_target="tpu_custom_call" | custom-call | flops 3221225472 | bytes 6291456 | tf_op jit(solution)/shard_map/backward_keys/pallas_call | solution.py:285
  72.7 4.1 %all-to-all-start.1 = ((bf16[8,256,128]{2,1,0:T(8,128)(2,1)}), bf16[8,256,128]{2,1,0:T(8,128)(2,1)}, u32[]{:S(2)}, u32[]{:S(2)}) async-start(bf16[8,256,128]{2,1,0:T(8,128)(2,1)} %get-tuple-element.47), calls=%async_computation.1 | async-start | bytes 1048576 | tf_op jit(solution)/shard_map/reduce_keys/all_to_all | solution.py:414
  76.8 0.0 copy-start.5
  76.8 0.9 copy-done.5
  77.7 4.7 %backward_queries.1 = bf16[4,24,2048]{2,1,0:T(8,128)(2,1)S(1)} custom-call(bf16[1536,768]{1,0:T(8,128)(2,1)S(1)} %assemble.1.refs_3_.refs_19_.q_ref, f32[24,2048]{1,0:T(8,128)S(1)} %get-tuple-element.46.grad_ref, bf16[2,256,128]{2,1,0:T(8,128)(2,1)S(1)} %copy-done.5, bf16[3,256,128]{2,1,0:T(8,128)(2,1)S(1)} %get-tuple-element.44.refs_17_.refs_1_, ...), custom_call_target="tpu_custom_call" | custom-call | flops 3221225472 | bytes 6291456 | tf_op jit(solution)/shard_map/backward_queries/pallas_call | solution.py:320
  82.4 0.1 collective-permute-start.13
  82.6 2.3 %collective-permute-start.15 = (bf16[24,2048]{1,0:T(8,128)(2,1)S(1)}, bf16[24,2048]{1,0:T(8,128)(2,1)S(1)}, u32[]{:S(2)}, u32[]{:S(2)}) collective-permute-start(bf16[24,2048]{1,0:T(8,128)(2,1)S(1)} %get-tuple-element.49), channel_id=1, source_target_pairs={{0,3},{1,2},{2,1},{3,0},{4,7},{5,6},{6,5},{7,4},{8,11},{9,10},{10,... | collective-permute-start | bytes 294920 | tf_op jit(solution)/shard_map/reduce_queries/ppermute | solution.py:344
  84.9 1.3 %collective-permute-start.14 = (bf16[24,2048]{1,0:T(8,128)(2,1)S(1)}, bf16[24,2048]{1,0:T(8,128)(2,1)S(1)}, u32[]{:S(2)}, u32[]{:S(2)}) collective-permute-start(bf16[24,2048]{1,0:T(8,128)(2,1)S(1)} %get-tuple-element.50), channel_id=1, source_target_pairs={{0,2},{1,3},{2,0},{3,1},{4,6},{5,7},{6,4},{7,5},{8,10},{9,11},{10,... | collective-permute-start | bytes 294920 | tf_op jit(solution)/shard_map/reduce_queries/ppermute | solution.py:344
  86.2 0.3 all-to-all-done.1
  86.5 1.1 %add_convert_fusion = bf16[1,256,128]{2,1,0:T(8,128)(2,1)S(1)} fusion(bf16[8,256,128]{2,1,0:T(8,128)(2,1)} %all-to-all-done.1), kind=kLoop, calls=%fused_computation.4 | loop fusion | flops 524288 | bytes 589824 | tf_op jit(solution)/shard_map/reduce_keys/convert_element_type | solution.py:418
  87.6 0.6 copy.27
  88.3 6.6 %all-to-all-start.2 = ((bf16[8,32,128]{2,1,0:T(8,128)(2,1)}), bf16[8,32,128]{2,1,0:T(8,128)(2,1)S(1)}, u32[]{:S(2)}, u32[]{:S(2)}) async-start(bf16[8,32,128]{2,1,0:T(8,128)(2,1)} %bitcast.20), calls=%async_computation.2 | async-start | bytes 131072 | tf_op jit(solution)/shard_map/reduce_keys/all_to_all | solution.py:419
  94.8 0.0 collective-permute-done.13
  94.8 0.0 collective-permute-done.14
  94.8 0.7 fusion.1
  95.6 7.6 %all-to-all-done.2 = bf16[8,32,128]{2,1,0:T(8,128)(2,1)S(1)} async-done(((bf16[8,32,128]{2,1,0:T(8,128)(2,1)}), bf16[8,32,128]{2,1,0:T(8,128)(2,1)S(1)}, u32[]{:S(2)}, u32[]{:S(2)}) %all-to-all-start.2) | async-done | bytes 65568 | tf_op jit(solution)/shard_map/reduce_keys/all_to_all | solution.py:419
  103.2 0.6 convert_reduce_fusion
  (24 shorter events, 0.1 us)
Async XLA Ops:
  0.6 0.9 copy-start
  0.6 2.8 %copy-start.8 = (f32[24,16]{0,1:T(8,128)S(1)}, f32[24,16]{0,1:T(8,128)}, u32[]{:S(2)}) copy-start(f32[24,16]{0,1:T(8,128)} %param.10) | copy-start | bytes 4612
  0.7 3.0 %copy-start.7 = (bf16[24,2048]{1,0:T(8,128)(2,1)S(1)}, bf16[24,2048]{1,0:T(8,128)(2,1)}, u32[]{:S(2)}) copy-start(bf16[24,2048]{1,0:T(8,128)(2,1)} %param.8) | copy-start | bytes 294916
  0.7 3.0 %copy-start.6 = (bf16[24,9216]{1,0:T(8,128)(2,1)S(1)}, bf16[24,9216]{1,0:T(8,128)(2,1)}, u32[]{:S(2)}) copy-start(bf16[24,9216]{1,0:T(8,128)(2,1)} %param.6) | copy-start | bytes 1327108
  3.7 15.7 %collective-permute-start.1 = (bf16[24,11392]{1,0:T(8,128)(2,1)S(1)}, bf16[24,11392]{1,0:T(8,128)(2,1)S(1)}, u32[]{:S(2)}, u32[]{:S(2)}) collective-permute-start(bf16[24,11392]{1,0:T(8,128)(2,1)S(1)} %pad_maximum_fusion.refs_0_), channel_id=1, source_target_pairs={{0,2},{2,0},{1,3},{3,1},{4,6},{6,4},{5,7},{7,5},{8,10},{10,8},{9,1... | collective-permute-start | bytes 1640456 | tf_op jit(solution)/shard_map/gather_queries/ppermute | solution.py:340
  7.0 37.3 %copy-start.9 = (s32[24]{0:T(128)S(1)}, s32[24]{0:T(128)}, u32[]{:S(2)}) copy-start(s32[24]{0:T(128)} %param.11) | copy-start | bytes 292
  7.0 37.4 %copy-start.3 = (f32[2,1664]{1,0:T(2,128)S(1)}, f32[2,1664]{1,0:T(2,128)}, u32[]{:S(2)}) copy-start(f32[2,1664]{1,0:T(2,128)} %constant.88.clone.1.refs_2_) | copy-start | bytes 39940
  7.0 22.3 %all-to-all-start = ((bf16[8,16,1408]{2,1,0:T(8,128)(2,1)}), bf16[8,16,1408]{2,1,0:T(8,128)(2,1)S(1)}, u32[]{:S(2)}, u32[]{:S(2)}) async-start(bf16[8,16,1408]{2,1,0:T(8,128)(2,1)} %broadcast_in_dim.6), calls=%async_computation | async-start | bytes 720896 | tf_op jit(solution)/shard_map/gather_keys/all_to_all | solution.py:377
  15.6 4.7 %collective-permute-start = (bf16[24,11392]{1,0:T(8,128)(2,1)S(1)}, bf16[24,11392]{1,0:T(8,128)(2,1)S(1)}, u32[]{:S(2)}, u32[]{:S(2)}) collective-permute-start(bf16[24,11392]{1,0:T(8,128)(2,1)S(1)} %pad_maximum_fusion.refs_0_), channel_id=1, source_target_pairs={{0,1},{1,0},{2,3},{3,2},{4,5},{5,4},{6,7},{7,6},{8,9},{9,8},{10,11... | collective-permute-start | bytes 1640456 | tf_op jit(solution)/shard_map/gather_queries/ppermute | solution.py:340
  19.4 1.9 %collective-permute-start.2 = (bf16[24,11392]{1,0:T(8,128)(2,1)S(1)}, bf16[24,11392]{1,0:T(8,128)(2,1)S(1)}, u32[]{:S(2)}, u32[]{:S(2)}) collective-permute-start(bf16[24,11392]{1,0:T(8,128)(2,1)S(1)} %collective-permute-done.1.refs_2_), channel_id=1, source_target_pairs={{0,1},{1,0},{2,3},{3,2},{4,5},{5,4},{6,7},{7,6},{8,9},{9,8},{10,11... | collective-permute-start | bytes 1640456 | tf_op jit(solution)/shard_map/gather_queries/ppermute | solution.py:340
  19.4 0.8 copy-start.1
  21.4 1.1 %copy-start.2 = (bf16[24,11392]{1,0:T(8,128)(2,1)S(1)}, bf16[24,11392]{1,0:T(8,128)(2,1)}, u32[]{:S(2)}) copy-start(bf16[24,11392]{1,0:T(8,128)(2,1)} %copy-done.1) | copy-start | bytes 1640452
  29.3 8.1 %collective-permute-start.3 = (bf16[128,1408]{1,0:T(8,128)(2,1)S(1)}, bf16[128,1408]{1,0:T(8,128)(2,1)S(1)}, u32[]{:S(2)}, u32[]{:S(2)}) collective-permute-start(bf16[128,1408]{1,0:T(8,128)(2,1)S(1)} %bitcast.32), channel_id=1, source_target_pairs={{0,16},{16,0},{1,17},{17,1},{2,18},{18,2},{3,19},{19,3},{4,20},{20... | collective-permute-start | bytes 1081352 | tf_op jit(solution)/shard_map/gather_keys/ppermute | solution.py:340
  30.0 13.0 %collective-permute-start.6 = (bf16[128,1408]{1,0:T(8,128)(2,1)S(1)}, bf16[128,1408]{1,0:T(8,128)(2,1)}, u32[]{:S(2)}, u32[]{:S(2)}) collective-permute-start(bf16[128,1408]{1,0:T(8,128)(2,1)S(1)} %bitcast.33), channel_id=1, source_target_pairs={{8,0},{12,4},{0,8},{4,12},{9,1},{13,5},{1,9},{5,13},{10,2},{14,6},... | collective-permute-start | bytes 1081352 | tf_op jit(solution)/shard_map/gather_keys/ppermute | solution.py:374
  32.2 18.4 %collective-permute-start.5 = (bf16[128,1408]{1,0:T(8,128)(2,1)S(1)}, bf16[128,1408]{1,0:T(8,128)(2,1)S(1)}, u32[]{:S(2)}, u32[]{:S(2)}) collective-permute-start(bf16[128,1408]{1,0:T(8,128)(2,1)S(1)} %bitcast.34), channel_id=1, source_target_pairs={{12,0},{0,4},{4,8},{8,12},{13,1},{1,5},{5,9},{9,13},{14,2},{2,6},{... | collective-permute-start | bytes 1081352 | tf_op jit(solution)/shard_map/gather_keys/ppermute | solution.py:374
  32.2 18.4 %collective-permute-start.4 = (bf16[128,1408]{1,0:T(8,128)(2,1)S(1)}, bf16[128,1408]{1,0:T(8,128)(2,1)S(1)}, u32[]{:S(2)}, u32[]{:S(2)}) collective-permute-start(bf16[128,1408]{1,0:T(8,128)(2,1)S(1)} %bitcast.35), channel_id=1, source_target_pairs={{4,0},{8,4},{12,8},{0,12},{5,1},{9,5},{13,9},{1,13},{6,2},{10,6},{... | collective-permute-start | bytes 1081352 | tf_op jit(solution)/shard_map/gather_keys/ppermute | solution.py:374
  37.4 17.8 %collective-permute-start.8 = (bf16[128,1408]{1,0:T(8,128)(2,1)S(1)}, bf16[128,1408]{1,0:T(8,128)(2,1)S(1)}, u32[]{:S(2)}, u32[]{:S(2)}) collective-permute-start(bf16[128,1408]{1,0:T(8,128)(2,1)S(1)} %collective-permute-done.3.refs_5_), channel_id=1, source_target_pairs={{12,0},{0,4},{4,8},{8,12},{13,1},{1,5},{5,9},{9,13},{14,2},{2,6},{... | collective-permute-start | bytes 1081352 | tf_op jit(solution)/shard_map/gather_keys/ppermute | solution.py:374
  38.9 16.3 %collective-permute-start.7 = (bf16[128,1408]{1,0:T(8,128)(2,1)S(1)}, bf16[128,1408]{1,0:T(8,128)(2,1)S(1)}, u32[]{:S(2)}, u32[]{:S(2)}) collective-permute-start(bf16[128,1408]{1,0:T(8,128)(2,1)S(1)} %collective-permute-done.3.refs_5_), channel_id=1, source_target_pairs={{4,0},{8,4},{12,8},{0,12},{5,1},{9,5},{13,9},{1,13},{6,2},{10,6},{... | collective-permute-start | bytes 1081352 | tf_op jit(solution)/shard_map/gather_keys/ppermute | solution.py:374
  42.9 12.2 %collective-permute-start.9 = (bf16[128,1408]{1,0:T(8,128)(2,1)}, bf16[128,1408]{1,0:T(8,128)(2,1)S(1)}, u32[]{:S(2)}, u32[]{:S(2)}) collective-permute-start(bf16[128,1408]{1,0:T(8,128)(2,1)} %collective-permute-done.6.refs_6_), channel_id=1, source_target_pairs={{0,16},{16,0},{1,17},{17,1},{2,18},{18,2},{3,19},{19,3},{4,20},{20... | collective-permute-start | bytes 1081352 | tf_op jit(solution)/shard_map/gather_keys/ppermute | solution.py:340
  47.6 18.1 %copy-start.4 = (bf16[2,256,128]{2,1,0:T(8,128)(2,1)}, bf16[2,256,128]{2,1,0:T(8,128)(2,1)S(1)}, u32[]{:S(2)}) copy-start(bf16[2,256,128]{2,1,0:T(8,128)(2,1)S(1)} %get-tuple-element.43.refs_16_.refs_0_) | copy-start | bytes 393220
  59.2 4.7 %collective-permute-start.12 = (f32[2,1664]{1,0:T(2,128)S(1)}, f32[2,1664]{1,0:T(2,128)S(1)}, u32[]{:S(2)}, u32[]{:S(2)}) collective-permute-start(f32[2,1664]{1,0:T(2,128)S(1)} %get-tuple-element.33.refs_3_), channel_id=1, source_target_pairs={{0,3},{1,2},{2,1},{3,0},{4,7},{5,6},{6,5},{7,4},{8,11},{9,10},{10,... | collective-permute-start | bytes 39944 | tf_op jit(solution)/shard_map/exchange_stats/ppermute | solution.py:344
  60.4 5.3 %collective-permute-start.11 = (f32[2,1664]{1,0:T(2,128)S(1)}, f32[2,1664]{1,0:T(2,128)S(1)}, u32[]{:S(2)}, u32[]{:S(2)}) collective-permute-start(f32[2,1664]{1,0:T(2,128)S(1)} %get-tuple-element.33.refs_3_), channel_id=1, source_target_pairs={{0,2},{1,3},{2,0},{3,1},{4,6},{5,7},{6,4},{7,5},{8,10},{9,11},{10,... | collective-permute-start | bytes 39944 | tf_op jit(solution)/shard_map/exchange_stats/ppermute | solution.py:344
  62.0 3.6 %collective-permute-start.10 = (f32[2,1664]{1,0:T(2,128)S(1)}, f32[2,1664]{1,0:T(2,128)S(1)}, u32[]{:S(2)}, u32[]{:S(2)}) collective-permute-start(f32[2,1664]{1,0:T(2,128)S(1)} %get-tuple-element.33.refs_3_), channel_id=1, source_target_pairs={{0,1},{1,0},{2,3},{3,2},{4,5},{5,4},{6,7},{7,6},{8,9},{9,8},{10,11... | collective-permute-start | bytes 39944 | tf_op jit(solution)/shard_map/exchange_stats/ppermute | solution.py:344
  72.7 13.8 %all-to-all-start.1 = ((bf16[8,256,128]{2,1,0:T(8,128)(2,1)}), bf16[8,256,128]{2,1,0:T(8,128)(2,1)}, u32[]{:S(2)}, u32[]{:S(2)}) async-start(bf16[8,256,128]{2,1,0:T(8,128)(2,1)} %get-tuple-element.47), calls=%async_computation.1 | async-start | bytes 1048576 | tf_op jit(solution)/shard_map/reduce_keys/all_to_all | solution.py:414
  76.8 0.9 copy-start.5
  82.4 12.4 %collective-permute-start.13 = (bf16[24,2048]{1,0:T(8,128)(2,1)S(1)}, bf16[24,2048]{1,0:T(8,128)(2,1)S(1)}, u32[]{:S(2)}, u32[]{:S(2)}) collective-permute-start(bf16[24,2048]{1,0:T(8,128)(2,1)S(1)} %get-tuple-element.48), channel_id=1, source_target_pairs={{0,1},{1,0},{2,3},{3,2},{4,5},{5,4},{6,7},{7,6},{8,9},{9,8},{10,11... | collective-permute-start | bytes 294920 | tf_op jit(solution)/shard_map/reduce_queries/ppermute | solution.py:344
  82.6 12.3 %collective-permute-start.15 = (bf16[24,2048]{1,0:T(8,128)(2,1)S(1)}, bf16[24,2048]{1,0:T(8,128)(2,1)S(1)}, u32[]{:S(2)}, u32[]{:S(2)}) collective-permute-start(bf16[24,2048]{1,0:T(8,128)(2,1)S(1)} %get-tuple-element.49), channel_id=1, source_target_pairs={{0,3},{1,2},{2,1},{3,0},{4,7},{5,6},{6,5},{7,4},{8,11},{9,10},{10,... | collective-permute-start | bytes 294920 | tf_op jit(solution)/shard_map/reduce_queries/ppermute | solution.py:344
  84.9 9.9 %collective-permute-start.14 = (bf16[24,2048]{1,0:T(8,128)(2,1)S(1)}, bf16[24,2048]{1,0:T(8,128)(2,1)S(1)}, u32[]{:S(2)}, u32[]{:S(2)}) collective-permute-start(bf16[24,2048]{1,0:T(8,128)(2,1)S(1)} %get-tuple-element.50), channel_id=1, source_target_pairs={{0,2},{1,3},{2,0},{3,1},{4,6},{5,7},{6,4},{7,5},{8,10},{9,11},{10,... | collective-permute-start | bytes 294920 | tf_op jit(solution)/shard_map/reduce_queries/ppermute | solution.py:344
  88.3 14.9 %all-to-all-start.2 = ((bf16[8,32,128]{2,1,0:T(8,128)(2,1)}), bf16[8,32,128]{2,1,0:T(8,128)(2,1)S(1)}, u32[]{:S(2)}, u32[]{:S(2)}) async-start(bf16[8,32,128]{2,1,0:T(8,128)(2,1)} %bitcast.20), calls=%async_computation.2 | async-start | bytes 131072 | tf_op jit(solution)/shard_map/reduce_keys/all_to_all | solution.py:419

commit v5 on v4

--- a/solution.py
+++ b/solution.py
@@ -100,7 +100,7 @@
         out_specs=pl.BlockSpec((RH, KPAD + DI), lambda i: (0, 0)),
         out_shape=jax.ShapeDtypeStruct((RH, KPAD + DI), bf16),
         compiler_params=pltpu.CompilerParams(vmem_limit_bytes=VMEM_LIMIT),
-        cost_estimate=pl.CostEstimate(flops=0, bytes_accessed=5000000, transcendentals=0),
+        cost_estimate=pl.CostEstimate(flops=0, bytes_accessed=50000000, transcendentals=0),
         name="assemble",
     )(*raws)
 
@@ -289,7 +289,7 @@
         scratch_shapes=[pltpu.VMEM((STATS, 128), f32)],
         out_shape=[
             jax.ShapeDtypeStruct((count, PIECE, DI), bf16),
-            jax.ShapeDtypeStruct((ROWS, keys), f32),
+            pltpu.VMEM((ROWS, keys), f32),
         ],
         compiler_params=pltpu.CompilerParams(vmem_limit_bytes=VMEM_LIMIT),
         cost_estimate=pl.CostEstimate(
@@ -300,40 +300,28 @@
 
 
 def backward_queries_kernel(q_ref, grad_ref, *refs):
-    key_refs, dq_ref, keys_ref = refs[:-2], refs[-2], refs[-1]
-
-    @pl.when(pl.program_id(0) == 0)
-    def _():
-        at = 0
-        for ref in key_refs:
-            count = ref.shape[0]
-            keys_ref[at : at + count * PIECE, :] = ref[...].reshape(count * PIECE, DI)
-            at += count * PIECE
-
-    dq = nn(head_grads_of(q_ref, keys_ref[...], grad_ref[...]), keys_ref[...])
-    for j in range(BLOCK // ROWS):
-        dq_ref[0, :, j * DI : (j + 1) * DI] = dq[j * ROWS : (j + 1) * ROWS].astype(bf16)
+    key_refs, dq_ref = refs[:-1], refs[-1]
+    keys_mat = jnp.concatenate([r[...].reshape(r.shape[0] * PIECE, DI) for r in key_refs], axis=0)
+    for r in range(RH // BLOCK):
+        q_block = q_ref.at[r * BLOCK : (r + 1) * BLOCK]
+        dq = nn(head_grads_of(q_block, keys_mat, grad_ref[...]), keys_mat)
+        for j in range(BLOCK // ROWS):
+            dq_ref[r, :, j * DI : (j + 1) * DI] = dq[j * ROWS : (j + 1) * ROWS].astype(bf16)
 
 
 def backward_queries(q_all, keys_list, grad):
-    keys = grad.shape[1]
+    vmem = pl.BlockSpec(memory_space=pltpu.VMEM)
     return pl.pallas_call(
         backward_queries_kernel,
-        grid=(RH // BLOCK,),
-        in_specs=[
-            pl.BlockSpec((BLOCK, KPAD + DI), lambda i: (i, 0)),
-            pl.BlockSpec((ROWS, keys), lambda i: (0, 0)),
-        ]
-        + [pl.BlockSpec(k.shape, lambda i: (0, 0, 0)) for k in keys_list],
-        out_specs=pl.BlockSpec((1, ROWS, LOCAL * DI), lambda i: (i, 0, 0)),
+        in_specs=[vmem] * (2 + len(keys_list)),
+        out_specs=vmem,
         out_shape=jax.ShapeDtypeStruct((4, ROWS, LOCAL * DI), bf16),
-        scratch_shapes=[pltpu.VMEM((keys, DI), bf16)],
         compiler_params=pltpu.CompilerParams(vmem_limit_bytes=VMEM_LIMIT),
         cost_estimate=pl.CostEstimate(
-            flops=8 * RH * keys * 128, bytes_accessed=2 * RH * keys, transcendentals=0
+            flops=32 * RH * KEYS * 128, bytes_accessed=2 * RH * KEYS, transcendentals=0
         ),
         name="backward_queries",
-    )(q_all, grad, *keys_list)
+    )(q_all, *in_vmem([grad, *keys_list]))
 
 
 def flip(value, axis):
@@ -375,10 +363,10 @@
 
     with jax.named_scope("gather_keys"):
         p00 = lax.all_to_all(own_keys, "z", 0, 0, tiled=True).reshape(HALF, PACKED)
-        p00, q_all = lax.optimization_barrier((p00, q_all))
         p01 = flip(p00, "yl")
-        p10, p30 = shift(p00, 1), shift(p00, 3)
         p20 = shift(p00, 2)
+        later, q_all = lax.optimization_barrier((p00, q_all))
+        p10, p30 = shift(later, 1), shift(later, 3)
         p11, p31 = shift(p01, 1), shift(p01, 3)
         p21 = flip(p20, "yl")
     groups = [

time: 104 us -> 103 us (level)
  waiting for transfers between devices: 32 us -> 26.1 us
  local copies, waits for them, and re-layouts: 6.47 us -> 10.9 us
    unnamed x21 -> x29, local copies, waits for them, and re-layouts: 3.79 us -> 8.2 us
    ppermute x5, waiting for transfers between devices: 8.13 us -> 3.99 us  [flip(): return lax.ppermute(value, axis, [(0, 1), (1, 0)])]
    ppermute x5, waiting for transfers between devices: 6.51 us -> 2.85 us  [shift(): return lax.ppermute(value, 'x', [((i + s) % 4, i) for i in range(4)])]
    all_to_all x1, starting transfers between devices: 6.56 us -> 3.71 us  [body(): lax.all_to_all(jnp.transpose(over_xy, (1, 0, 2, 3)).reshape(8, 32, DI), '...]
    all_to_all x1, waiting for transfers between devices: 6.39 us -> 8.89 us  [body(): p00 = lax.all_to_all(own_keys, 'z', 0, 0, tiled=True).reshape(HALF, PACKED)]
    all_to_all x1, starting transfers between devices: 4.1 us -> 6.58 us  [body(): dk_xy = lax.all_to_all(dk, ('yl', 'x'), 0, 0, tiled=True)]
    pallas_call x1, Pallas kernels: 4.69 us -> 3.61 us  [backward_queries(): pl.pallas_call(backward_queries_kernel, in_specs=[vmem] * (2 + len(keys_l...]
  transfers between devices with their start and end apart: 19 -> 19, of which waited for: 10 -> 9; matrix products, arithmetic and copies ran while one was open for 3% -> 3% of each run, Pallas kernels for 12% -> 12%
where the time goes in v5:
time: 103 us; the launch traced here: 102 us
  starting transfers between devices  38.2 us (37%)
  waiting for transfers between devices  26.1 us (25%)
  Pallas kernels  23.4 us (23%)
  local copies, waits for them, and re-layouts  10.9 us (11%)
  other arithmetic  2.53 us (2%)
    pallas_call x3, Pallas kernels, forward(): pl.pallas_call(functools.partial(forward_kernel, count, first), in_specs=...  12.3 us
    all_to_all x1, waiting for transfers between devices, body(): p00 = lax.all_to_all(own_keys, 'z', 0, 0, tiled=True).reshape(HALF, PACKED)  8.89 us
    all_to_all x1, starting transfers between devices, body(): p00 = lax.all_to_all(own_keys, 'z', 0, 0, tiled=True).reshape(HALF, PACKED)  8.47 us
    unnamed x29, local copies, waits for them, and re-layouts  8.2 us
    all_to_all x1, waiting for transfers between devices, body(): lax.all_to_all(jnp.transpose(over_xy, (1, 0, 2, 3)).reshape(8, 32, DI), '...  7.5 us
    ppermute x6, starting transfers between devices, head_xor(): return lax.ppermute(value, HEAD, [(i, i ^ bits) for i in range(4)])  7.19 us
    pallas_call x1, Pallas kernels, backward_keys(): pl.pallas_call(functools.partial(backward_keys_kernel, sizes), in_specs=[...  7.08 us
    ppermute x5, starting transfers between devices, shift(): return lax.ppermute(value, 'x', [((i + s) % 4, i) for i in range(4)])  6.95 us
  transfers between devices with their start and end apart: 19, of which 9 were waited for; matrix products, arithmetic and copies ran while one was open for 3% of the time, Pallas kernels for 12%

profile of v5, /device:TPU:2, one launch (start us, length us, event | category | flops | bytes accessed | tf_op | source)
XLA Modules:
  0.0 102.0 jit_solution(8574898146842344499)
XLA Ops:
  0.6 0.0 copy-start
  0.7 0.9 copy-done
  1.5 0.1 constant_dynamic-slice_fusion.2
  1.7 0.1 copy.28
  1.8 0.7 constant_dynamic-slice_fusion.1
  2.5 0.1 concatenate.6
  2.6 0.8 broadcast_in_dim.6
  3.5 0.1 stack.50
  3.5 0.1 copy.26
  3.6 0.0 copy-done.10
  3.7 3.3 %collective-permute-start.1 = (bf16[24,11392]{1,0:T(8,128)(2,1)S(1)}, bf16[24,11392]{1,0:T(8,128)(2,1)S(1)}, u32[]{:S(2)}, u32[]{:S(2)}) collective-permute-start(bf16[24,11392]{1,0:T(8,128)(2,1)S(1)} %pad_maximum_fusion.refs_0_), channel_id=1, source_target_pairs={{0,2},{2,0},{1,3},{3,1},{4,6},{6,4},{5,7},{7,5},{8,10},{10,8},{9,1... | collective-permute-start | bytes 1640456 | tf_op jit(solution)/shard_map/gather_queries/ppermute | solution.py:328
  7.0 8.5 %all-to-all-start = ((bf16[8,16,1408]{2,1,0:T(8,128)(2,1)}), bf16[8,16,1408]{2,1,0:T(8,128)(2,1)S(1)}, u32[]{:S(2)}, u32[]{:S(2)}) async-start(bf16[8,16,1408]{2,1,0:T(8,128)(2,1)} %broadcast_in_dim.6), calls=%async_computation | async-start | bytes 720896 | tf_op jit(solution)/shard_map/gather_keys/all_to_all | solution.py:365
  15.4 0.0 collective-permute-start
  15.4 4.0 %collective-permute-done.1.refs_2_ = bf16[24,11392]{1,0:T(8,128)(2,1)S(1)} collective-permute-done((bf16[24,11392]{1,0:T(8,128)(2,1)S(1)}, bf16[24,11392]{1,0:T(8,128)(2,1)S(1)}, u32[]{:S(2)}, u32[]{:S(2)}) %collective-permute-start.1) | collective-permute-done | bytes 546848 | tf_op jit(solution)/shard_map/gather_queries/ppermute | solution.py:328
  19.4 0.0 collective-permute-start.2
  19.4 0.8 copy-done.1
  20.2 8.9 %all-to-all-done = bf16[8,16,1408]{2,1,0:T(8,128)(2,1)S(1)} async-done(((bf16[8,16,1408]{2,1,0:T(8,128)(2,1)}), bf16[8,16,1408]{2,1,0:T(8,128)(2,1)S(1)}, u32[]{:S(2)}, u32[]{:S(2)}) %all-to-all-start) | async-done | bytes 360480 | tf_op jit(solution)/shard_map/gather_keys/all_to_all | solution.py:365
  29.1 0.7 collective-permute-start.3
  29.8 2.1 %collective-permute-start.6 = (bf16[128,1408]{1,0:T(8,128)(2,1)S(1)}, bf16[128,1408]{1,0:T(8,128)(2,1)}, u32[]{:S(2)}, u32[]{:S(2)}) collective-permute-start(bf16[128,1408]{1,0:T(8,128)(2,1)S(1)} %bitcast.33), channel_id=1, source_target_pairs={{8,0},{12,4},{0,8},{4,12},{9,1},{13,5},{1,9},{5,13},{10,2},{14,6},... | collective-permute-start | bytes 1081352 | tf_op jit(solution)/shard_map/gather_keys/ppermute | solution.py:362
  31.9 0.1 stack.59.refs_0_
  32.0 0.0 collective-permute-done.refs_1_
  32.0 0.8 copy-done.3
  32.8 0.8 copy-done.5
  33.7 1.0 %copy-done.2 = bf16[24,11392]{1,0:T(8,128)(2,1)S(1)} copy-done((bf16[24,11392]{1,0:T(8,128)(2,1)S(1)}, bf16[24,11392]{1,0:T(8,128)(2,1)}, u32[]{:S(2)}) %copy-start.2) | copy-done | bytes 546840
  34.7 1.0 %copy-done.4 = bf16[24,11392]{1,0:T(8,128)(2,1)S(1)} copy-done((bf16[24,11392]{1,0:T(8,128)(2,1)S(1)}, bf16[24,11392]{1,0:T(8,128)(2,1)}, u32[]{:S(2)}) %copy-start.4) | copy-done | bytes 546840
  35.8 1.0 %copy-done.6 = bf16[24,11392]{1,0:T(8,128)(2,1)S(1)} copy-done((bf16[24,11392]{1,0:T(8,128)(2,1)S(1)}, bf16[24,11392]{1,0:T(8,128)(2,1)}, u32[]{:S(2)}) %copy-start.6) | copy-done | bytes 546840
  36.8 0.5 assemble.1.refs_3_.refs_19_.q_ref
  37.3 0.1 collective-permute-start.5
  37.4 2.0 %collective-permute-start.4 = (bf16[128,1408]{1,0:T(8,128)(2,1)S(1)}, bf16[128,1408]{1,0:T(8,128)(2,1)S(1)}, u32[]{:S(2)}, u32[]{:S(2)}) collective-permute-start(bf16[128,1408]{1,0:T(8,128)(2,1)S(1)} %bitcast.35), channel_id=1, source_target_pairs={{4,0},{8,4},{12,8},{0,12},{5,1},{9,5},{13,9},{1,13},{6,2},{10,6},{... | collective-permute-start | bytes 1081352 | tf_op jit(solution)/shard_map/gather_keys/ppermute | solution.py:362
  39.4 0.0 collective-permute-done.3.refs_5_
  39.4 0.1 collective-permute-start.8
  39.5 2.6 %collective-permute-start.7 = (bf16[128,1408]{1,0:T(8,128)(2,1)}, bf16[128,1408]{1,0:T(8,128)(2,1)S(1)}, u32[]{:S(2)}, u32[]{:S(2)}) collective-permute-start(bf16[128,1408]{1,0:T(8,128)(2,1)} %collective-permute-done.3.refs_5_), channel_id=1, source_target_pairs={{4,0},{8,4},{12,8},{0,12},{5,1},{9,5},{13,9},{1,13},{6,2},{10,6},{... | collective-permute-start | bytes 1081352 | tf_op jit(solution)/shard_map/gather_keys/ppermute | solution.py:362
  42.1 1.3 %collective-permute-start.9 = (bf16[128,1408]{1,0:T(8,128)(2,1)}, bf16[128,1408]{1,0:T(8,128)(2,1)S(1)}, u32[]{:S(2)}, u32[]{:S(2)}) collective-permute-start(bf16[128,1408]{1,0:T(8,128)(2,1)} %collective-permute-done.6.refs_6_), channel_id=1, source_target_pairs={{0,16},{16,0},{1,17},{17,1},{2,18},{18,2},{3,19},{19,3},{4,20},{20... | collective-permute-start | bytes 1081352 | tf_op jit(solution)/shard_map/gather_keys/ppermute | solution.py:328
  43.5 0.1 broadcast_in_dim.8.refs_1_.refs_2_
  43.5 3.7 %forward.3 = (bf16[2,1536,256]{2,1,0:T(8,128)(2,1)S(1)}, f32[2,24,256]{2,1,0:T(8,128)S(1)}, bf16[2,256,128]{2,1,0:T(8,128)(2,1)S(1)}, f32[8,1664]{1,0:T(8,128)S(1)}, f32[2,1664]{1,0:T(2,128)S(1)}) custom-call(s32[8]{0:T(128)S(1)} %multiply_add_fusion.refs_0_.refs_1_, s32[24,128]{1,0:T(8,128)S(1)} %broadcast_in_dim.8.refs_1_.refs_2_, ...), custom_call_target="tpu_custom_call" | custom-call | flops 2415919104 | bytes 1572864 | tf_op jit(solution)/shard_map/forward/pallas_call | solution.py:177
  47.2 1.6 %collective-permute-done.5.refs_5_ = bf16[128,1408]{1,0:T(8,128)(2,1)S(1)} collective-permute-done((bf16[128,1408]{1,0:T(8,128)(2,1)S(1)}, bf16[128,1408]{1,0:T(8,128)(2,1)S(1)}, u32[]{:S(2)}, u32[]{:S(2)}) %collective-permute-start.5) | collective-permute-done | bytes 360480 | tf_op jit(solution)/shard_map/gather_keys/ppermute | solution.py:362
  48.8 0.0 collective-permute-done.4.refs_4_
  48.8 4.5 %forward.4 = (bf16[3,1536,256]{2,1,0:T(8,128)(2,1)S(1)}, f32[3,24,256]{2,1,0:T(8,128)S(1)}, bf16[3,256,128]{2,1,0:T(8,128)(2,1)S(1)}, f32[8,1664]{1,0:T(8,128)S(1)}, f32[2,1664]{1,0:T(2,128)S(1)}) custom-call(s32[8]{0:T(128)S(1)} %multiply_add_fusion.refs_0_.refs_1_, s32[24,128]{1,0:T(8,128)S(1)} %broadcast_in_dim.8.refs_1_.refs_2_, ...), custom_call_target="tpu_custom_call" | custom-call | flops 3623878656 | bytes 2359296 | tf_op jit(solution)/shard_map/forward/pallas_call | solution.py:177
  53.4 0.0 collective-permute-done.9.refs_6_
  53.4 1.2 %collective-permute-done.8.refs_5_ = bf16[128,1408]{1,0:T(8,128)(2,1)S(1)} collective-permute-done((bf16[128,1408]{1,0:T(8,128)(2,1)}, bf16[128,1408]{1,0:T(8,128)(2,1)S(1)}, u32[]{:S(2)}, u32[]{:S(2)}) %collective-permute-start.8) | collective-permute-done | bytes 360480 | tf_op jit(solution)/shard_map/gather_keys/ppermute | solution.py:362
  54.6 0.0 collective-permute-done.7.refs_4_
  54.6 4.1 %forward.5 = (bf16[3,1536,256]{2,1,0:T(8,128)(2,1)S(1)}, f32[3,24,256]{2,1,0:T(8,128)S(1)}, bf16[3,256,128]{2,1,0:T(8,128)(2,1)S(1)}, f32[8,1664]{1,0:T(8,128)S(1)}, f32[2,1664]{1,0:T(2,128)S(1)}) custom-call(s32[8]{0:T(128)S(1)} %multiply_add_fusion.refs_0_.refs_1_, s32[24,128]{1,0:T(8,128)S(1)} %broadcast_in_dim.8.refs_1_.refs_2_, ...), custom_call_target="tpu_custom_call" | custom-call | flops 3623878656 | bytes 2359296 | tf_op jit(solution)/shard_map/forward/pallas_call | solution.py:177
  58.7 0.1 collective-permute-start.12
  58.8 1.9 %collective-permute-start.11 = (f32[2,1664]{1,0:T(2,128)S(1)}, f32[2,1664]{1,0:T(2,128)S(1)}, u32[]{:S(2)}, u32[]{:S(2)}) collective-permute-start(f32[2,1664]{1,0:T(2,128)S(1)} %get-tuple-element.33.refs_3_), channel_id=1, source_target_pairs={{0,2},{1,3},{2,0},{3,1},{4,6},{5,7},{6,4},{7,5},{8,10},{9,11},{10,... | collective-permute-start | bytes 39944 | tf_op jit(solution)/shard_map/exchange_stats/ppermute | solution.py:332
  60.7 1.4 %collective-permute-start.10 = (f32[2,1664]{1,0:T(2,128)S(1)}, f32[2,1664]{1,0:T(2,128)S(1)}, u32[]{:S(2)}, u32[]{:S(2)}) collective-permute-start(f32[2,1664]{1,0:T(2,128)S(1)} %get-tuple-element.33.refs_3_), channel_id=1, source_target_pairs={{0,1},{1,0},{2,3},{3,2},{4,5},{5,4},{6,7},{7,6},{8,9},{9,8},{10,11... | collective-permute-start | bytes 39944 | tf_op jit(solution)/shard_map/exchange_stats/ppermute | solution.py:332
  62.1 1.3 %collective-permute-done.12.refs_6_ = f32[2,1664]{1,0:T(2,128)S(1)} collective-permute-done((f32[2,1664]{1,0:T(2,128)S(1)}, f32[2,1664]{1,0:T(2,128)S(1)}, u32[]{:S(2)}, u32[]{:S(2)}) %collective-permute-start.12) | collective-permute-done | bytes 13344 | tf_op jit(solution)/shard_map/exchange_stats/ppermute | solution.py:332
  63.4 0.7 collective-permute-done.11.refs_5_
  64.1 7.1 %backward_keys.1 = (bf16[8,256,128]{2,1,0:T(8,128)(2,1)}, f32[24,2048]{1,0:T(8,128)S(1)}) custom-call(s32[8]{0:T(128)S(1)} %stack.59.refs_0_, s32[8]{0:T(128)S(1)} %multiply_add_fusion.refs_0_.refs_1_, s32[24,128]{1,0:T(8,128)S(1)} %broadcast_in_dim.8.refs_1_.refs_2_, f32[2,1664]{1,0:T(2,128)S(1)} %get-tuple-element.33.refs_3_, ...), custom_call_target="tpu_custom_call" | custom-call | flops 3221225472 | bytes 6291456 | tf_op jit(solution)/shard_map/backward_keys/pallas_call | solution.py:285
  71.2 0.7 copy-done.8
  71.9 6.6 %all-to-all-start.1 = ((bf16[8,256,128]{2,1,0:T(8,128)(2,1)}), bf16[8,256,128]{2,1,0:T(8,128)(2,1)}, u32[]{:S(2)}, u32[]{:S(2)}) async-start(bf16[8,256,128]{2,1,0:T(8,128)(2,1)} %get-tuple-element.47), calls=%async_computation.1 | async-start | bytes 1048576 | tf_op jit(solution)/shard_map/reduce_keys/all_to_all | solution.py:402
  78.4 0.9 copy-done.9
  79.4 3.6 %backward_queries.1 = bf16[4,24,2048]{2,1,0:T(8,128)(2,1)S(1)} custom-call(bf16[1536,768]{1,0:T(8,128)(2,1)S(1)} %assemble.1.refs_3_.refs_19_.q_ref, f32[24,2048]{1,0:T(8,128)S(1)} %copy-done.9, bf16[2,256,128]{2,1,0:T(8,128)(2,1)S(1)} %get-tuple-element.43.refs_16_.refs_0_, bf16[3,256,128]{2,1,0:T(8,128)(2,1)S(1)} %get-tuple-element.44.refs_17_.refs_1_, ...), custom_call_target="tpu_custom_call" | custom-call | flops 12884901888 | bytes 6291456 | tf_op jit(solution)/shard_map/backward_queries/pallas_call | solution.py:314
  83.0 0.1 collective-permute-start.13
  83.1 2.1 %collective-permute-start.15 = (bf16[24,2048]{1,0:T(8,128)(2,1)S(1)}, bf16[24,2048]{1,0:T(8,128)(2,1)S(1)}, u32[]{:S(2)}, u32[]{:S(2)}) collective-permute-start(bf16[24,2048]{1,0:T(8,128)(2,1)S(1)} %get-tuple-element.49), channel_id=1, source_target_pairs={{0,3},{1,2},{2,1},{3,0},{4,7},{5,6},{6,5},{7,4},{8,11},{9,10},{10,... | collective-permute-start | bytes 294920 | tf_op jit(solution)/shard_map/reduce_queries/ppermute | solution.py:332
  85.2 1.5 %collective-permute-start.14 = (bf16[24,2048]{1,0:T(8,128)(2,1)S(1)}, bf16[24,2048]{1,0:T(8,128)(2,1)S(1)}, u32[]{:S(2)}, u32[]{:S(2)}) collective-permute-start(bf16[24,2048]{1,0:T(8,128)(2,1)S(1)} %get-tuple-element.50), channel_id=1, source_target_pairs={{0,2},{1,3},{2,0},{3,1},{4,6},{5,7},{6,4},{7,5},{8,10},{9,11},{10,... | collective-permute-start | bytes 294920 | tf_op jit(solution)/shard_map/reduce_queries/ppermute | solution.py:332
  86.8 0.8 all-to-all-done.1
  87.5 1.1 %add_convert_fusion = bf16[1,256,128]{2,1,0:T(8,128)(2,1)S(1)} fusion(bf16[8,256,128]{2,1,0:T(8,128)(2,1)} %all-to-all-done.1), kind=kLoop, calls=%fused_computation.4 | loop fusion | flops 524288 | bytes 589824 | tf_op jit(solution)/shard_map/reduce_keys/convert_element_type | solution.py:406
  88.7 0.6 copy.27
  89.3 3.7 %all-to-all-start.2 = ((bf16[8,32,128]{2,1,0:T(8,128)(2,1)}), bf16[8,32,128]{2,1,0:T(8,128)(2,1)S(1)}, u32[]{:S(2)}, u32[]{:S(2)}) async-start(bf16[8,32,128]{2,1,0:T(8,128)(2,1)} %bitcast.20), calls=%async_computation.2 | async-start | bytes 131072 | tf_op jit(solution)/shard_map/reduce_keys/all_to_all | solution.py:407
  93.0 0.0 collective-permute-done.13
  93.0 0.1 collective-permute-done.14
  93.2 0.7 fusion.1
  93.9 7.5 %all-to-all-done.2 = bf16[8,32,128]{2,1,0:T(8,128)(2,1)S(1)} async-done(((bf16[8,32,128]{2,1,0:T(8,128)(2,1)}), bf16[8,32,128]{2,1,0:T(8,128)(2,1)S(1)}, u32[]{:S(2)}, u32[]{:S(2)}) %all-to-all-start.2) | async-done | bytes 65568 | tf_op jit(solution)/shard_map/reduce_keys/all_to_all | solution.py:407
  101.4 0.6 convert_reduce_fusion
  (32 shorter events, 0.2 us)
Async XLA Ops:
  0.6 0.9 copy-start
  0.6 2.7 %copy-start.12 = (f32[24,16]{0,1:T(8,128)S(1)}, f32[24,16]{0,1:T(8,128)}, u32[]{:S(2)}) copy-start(f32[24,16]{0,1:T(8,128)} %param.10) | copy-start | bytes 4612
  0.7 3.0 %copy-start.11 = (bf16[24,2048]{1,0:T(8,128)(2,1)S(1)}, bf16[24,2048]{1,0:T(8,128)(2,1)}, u32[]{:S(2)}) copy-start(bf16[24,2048]{1,0:T(8,128)(2,1)} %param.8) | copy-start | bytes 294916
  0.7 3.0 %copy-start.10 = (bf16[24,9216]{1,0:T(8,128)(2,1)S(1)}, bf16[24,9216]{1,0:T(8,128)(2,1)}, u32[]{:S(2)}) copy-start(bf16[24,9216]{1,0:T(8,128)(2,1)} %param.6) | copy-start | bytes 1327108
  3.7 15.7 %collective-permute-start.1 = (bf16[24,11392]{1,0:T(8,128)(2,1)S(1)}, bf16[24,11392]{1,0:T(8,128)(2,1)S(1)}, u32[]{:S(2)}, u32[]{:S(2)}) collective-permute-start(bf16[24,11392]{1,0:T(8,128)(2,1)S(1)} %pad_maximum_fusion.refs_0_), channel_id=1, source_target_pairs={{0,2},{2,0},{1,3},{3,1},{4,6},{6,4},{5,7},{7,5},{8,10},{10,8},{9,1... | collective-permute-start | bytes 1640456 | tf_op jit(solution)/shard_map/gather_queries/ppermute | solution.py:328
  7.0 22.2 %all-to-all-start = ((bf16[8,16,1408]{2,1,0:T(8,128)(2,1)}), bf16[8,16,1408]{2,1,0:T(8,128)(2,1)S(1)}, u32[]{:S(2)}, u32[]{:S(2)}) async-start(bf16[8,16,1408]{2,1,0:T(8,128)(2,1)} %broadcast_in_dim.6), calls=%async_computation | async-start | bytes 720896 | tf_op jit(solution)/shard_map/gather_keys/all_to_all | solution.py:365
  15.4 16.6 %collective-permute-start = (bf16[24,11392]{1,0:T(8,128)(2,1)S(1)}, bf16[24,11392]{1,0:T(8,128)(2,1)S(1)}, u32[]{:S(2)}, u32[]{:S(2)}) collective-permute-start(bf16[24,11392]{1,0:T(8,128)(2,1)S(1)} %pad_maximum_fusion.refs_0_), channel_id=1, source_target_pairs={{0,1},{1,0},{2,3},{3,2},{4,5},{5,4},{6,7},{7,6},{8,9},{9,8},{10,11... | collective-permute-start | bytes 1640456 | tf_op jit(solution)/shard_map/gather_queries/ppermute | solution.py:328
  19.4 13.4 %collective-permute-start.2 = (bf16[24,11392]{1,0:T(8,128)(2,1)S(1)}, bf16[24,11392]{1,0:T(8,128)(2,1)S(1)}, u32[]{:S(2)}, u32[]{:S(2)}) collective-permute-start(bf16[24,11392]{1,0:T(8,128)(2,1)S(1)} %collective-permute-done.1.refs_2_), channel_id=1, source_target_pairs={{0,1},{1,0},{2,3},{3,2},{4,5},{5,4},{6,7},{7,6},{8,9},{9,8},{10,11... | collective-permute-start | bytes 1640456 | tf_op jit(solution)/shard_map/gather_queries/ppermute | solution.py:328
  19.4 0.8 copy-start.1
  29.1 10.2 %collective-permute-start.3 = (bf16[128,1408]{1,0:T(8,128)(2,1)S(1)}, bf16[128,1408]{1,0:T(8,128)(2,1)}, u32[]{:S(2)}, u32[]{:S(2)}) collective-permute-start(bf16[128,1408]{1,0:T(8,128)(2,1)S(1)} %bitcast.32), channel_id=1, source_target_pairs={{0,16},{16,0},{1,17},{17,1},{2,18},{18,2},{3,19},{19,3},{4,20},{20... | collective-permute-start | bytes 1081352 | tf_op jit(solution)/shard_map/gather_keys/ppermute | solution.py:328
  29.8 12.3 %collective-permute-start.6 = (bf16[128,1408]{1,0:T(8,128)(2,1)S(1)}, bf16[128,1408]{1,0:T(8,128)(2,1)}, u32[]{:S(2)}, u32[]{:S(2)}) collective-permute-start(bf16[128,1408]{1,0:T(8,128)(2,1)S(1)} %bitcast.33), channel_id=1, source_target_pairs={{8,0},{12,4},{0,8},{4,12},{9,1},{13,5},{1,9},{5,13},{10,2},{14,6},... | collective-permute-start | bytes 1081352 | tf_op jit(solution)/shard_map/gather_keys/ppermute | solution.py:362
  31.9 11.5 %copy-start.13 = (s32[24]{0:T(128)S(1)}, s32[24]{0:T(128)}, u32[]{:S(2)}) copy-start(s32[24]{0:T(128)} %param.11) | copy-start | bytes 292
  32.0 0.8 copy-start.3
  32.8 0.8 copy-start.5
  33.7 1.0 %copy-start.2 = (bf16[24,11392]{1,0:T(8,128)(2,1)S(1)}, bf16[24,11392]{1,0:T(8,128)(2,1)}, u32[]{:S(2)}) copy-start(bf16[24,11392]{1,0:T(8,128)(2,1)} %copy-done.1) | copy-start | bytes 1640452
  34.7 1.0 %copy-start.4 = (bf16[24,11392]{1,0:T(8,128)(2,1)S(1)}, bf16[24,11392]{1,0:T(8,128)(2,1)}, u32[]{:S(2)}) copy-start(bf16[24,11392]{1,0:T(8,128)(2,1)} %copy-done.3) | copy-start | bytes 1640452
  35.8 1.0 %copy-start.6 = (bf16[24,11392]{1,0:T(8,128)(2,1)S(1)}, bf16[24,11392]{1,0:T(8,128)(2,1)}, u32[]{:S(2)}) copy-start(bf16[24,11392]{1,0:T(8,128)(2,1)} %copy-done.5) | copy-start | bytes 1640452
  36.8 6.7 %copy-start.7 = (f32[2,1664]{1,0:T(2,128)S(1)}, f32[2,1664]{1,0:T(2,128)}, u32[]{:S(2)}) copy-start(f32[2,1664]{1,0:T(2,128)} %constant.88.clone.1.refs_2_) | copy-start | bytes 39940
  37.3 11.5 %collective-permute-start.5 = (bf16[128,1408]{1,0:T(8,128)(2,1)S(1)}, bf16[128,1408]{1,0:T(8,128)(2,1)S(1)}, u32[]{:S(2)}, u32[]{:S(2)}) collective-permute-start(bf16[128,1408]{1,0:T(8,128)(2,1)S(1)} %bitcast.34), channel_id=1, source_target_pairs={{12,0},{0,4},{4,8},{8,12},{13,1},{1,5},{5,9},{9,13},{14,2},{2,6},{... | collective-permute-start | bytes 1081352 | tf_op jit(solution)/shard_map/gather_keys/ppermute | solution.py:362
  37.4 11.5 %collective-permute-start.4 = (bf16[128,1408]{1,0:T(8,128)(2,1)S(1)}, bf16[128,1408]{1,0:T(8,128)(2,1)S(1)}, u32[]{:S(2)}, u32[]{:S(2)}) collective-permute-start(bf16[128,1408]{1,0:T(8,128)(2,1)S(1)} %bitcast.35), channel_id=1, source_target_pairs={{4,0},{8,4},{12,8},{0,12},{5,1},{9,5},{13,9},{1,13},{6,2},{10,6},{... | collective-permute-start | bytes 1081352 | tf_op jit(solution)/shard_map/gather_keys/ppermute | solution.py:362
  39.4 15.2 %collective-permute-start.8 = (bf16[128,1408]{1,0:T(8,128)(2,1)}, bf16[128,1408]{1,0:T(8,128)(2,1)S(1)}, u32[]{:S(2)}, u32[]{:S(2)}) collective-permute-start(bf16[128,1408]{1,0:T(8,128)(2,1)} %collective-permute-done.3.refs_5_), channel_id=1, source_target_pairs={{12,0},{0,4},{4,8},{8,12},{13,1},{1,5},{5,9},{9,13},{14,2},{2,6},{... | collective-permute-start | bytes 1081352 | tf_op jit(solution)/shard_map/gather_keys/ppermute | solution.py:362
  39.5 15.1 %collective-permute-start.7 = (bf16[128,1408]{1,0:T(8,128)(2,1)}, bf16[128,1408]{1,0:T(8,128)(2,1)S(1)}, u32[]{:S(2)}, u32[]{:S(2)}) collective-permute-start(bf16[128,1408]{1,0:T(8,128)(2,1)} %collective-permute-done.3.refs_5_), channel_id=1, source_target_pairs={{4,0},{8,4},{12,8},{0,12},{5,1},{9,5},{13,9},{1,13},{6,2},{10,6},{... | collective-permute-start | bytes 1081352 | tf_op jit(solution)/shard_map/gather_keys/ppermute | solution.py:362
  42.1 11.2 %collective-permute-start.9 = (bf16[128,1408]{1,0:T(8,128)(2,1)}, bf16[128,1408]{1,0:T(8,128)(2,1)S(1)}, u32[]{:S(2)}, u32[]{:S(2)}) collective-permute-start(bf16[128,1408]{1,0:T(8,128)(2,1)} %collective-permute-done.6.refs_6_), channel_id=1, source_target_pairs={{0,16},{16,0},{1,17},{17,1},{2,18},{18,2},{3,19},{19,3},{4,20},{20... | collective-permute-start | bytes 1081352 | tf_op jit(solution)/shard_map/gather_keys/ppermute | solution.py:328
  58.7 4.7 %collective-permute-start.12 = (f32[2,1664]{1,0:T(2,128)S(1)}, f32[2,1664]{1,0:T(2,128)S(1)}, u32[]{:S(2)}, u32[]{:S(2)}) collective-permute-start(f32[2,1664]{1,0:T(2,128)S(1)} %get-tuple-element.33.refs_3_), channel_id=1, source_target_pairs={{0,3},{1,2},{2,1},{3,0},{4,7},{5,6},{6,5},{7,4},{8,11},{9,10},{10,... | collective-permute-start | bytes 39944 | tf_op jit(solution)/shard_map/exchange_stats/ppermute | solution.py:332
  58.8 5.3 %collective-permute-start.11 = (f32[2,1664]{1,0:T(2,128)S(1)}, f32[2,1664]{1,0:T(2,128)S(1)}, u32[]{:S(2)}, u32[]{:S(2)}) collective-permute-start(f32[2,1664]{1,0:T(2,128)S(1)} %get-tuple-element.33.refs_3_), channel_id=1, source_target_pairs={{0,2},{1,3},{2,0},{3,1},{4,6},{5,7},{6,4},{7,5},{8,10},{9,11},{10,... | collective-permute-start | bytes 39944 | tf_op jit(solution)/shard_map/exchange_stats/ppermute | solution.py:332
  60.7 3.4 %collective-permute-start.10 = (f32[2,1664]{1,0:T(2,128)S(1)}, f32[2,1664]{1,0:T(2,128)S(1)}, u32[]{:S(2)}, u32[]{:S(2)}) collective-permute-start(f32[2,1664]{1,0:T(2,128)S(1)} %get-tuple-element.33.refs_3_), channel_id=1, source_target_pairs={{0,1},{1,0},{2,3},{3,2},{4,5},{5,4},{6,7},{7,6},{8,9},{9,8},{10,11... | collective-permute-start | bytes 39944 | tf_op jit(solution)/shard_map/exchange_stats/ppermute | solution.py:332
  71.2 0.7 copy-start.8
  71.9 15.7 %all-to-all-start.1 = ((bf16[8,256,128]{2,1,0:T(8,128)(2,1)}), bf16[8,256,128]{2,1,0:T(8,128)(2,1)}, u32[]{:S(2)}, u32[]{:S(2)}) async-start(bf16[8,256,128]{2,1,0:T(8,128)(2,1)} %get-tuple-element.47), calls=%async_computation.1 | async-start | bytes 1048576 | tf_op jit(solution)/shard_map/reduce_keys/all_to_all | solution.py:402
  78.4 0.9 copy-start.9
  83.0 10.0 %collective-permute-start.13 = (bf16[24,2048]{1,0:T(8,128)(2,1)S(1)}, bf16[24,2048]{1,0:T(8,128)(2,1)S(1)}, u32[]{:S(2)}, u32[]{:S(2)}) collective-permute-start(bf16[24,2048]{1,0:T(8,128)(2,1)S(1)} %get-tuple-element.48), channel_id=1, source_target_pairs={{0,1},{1,0},{2,3},{3,2},{4,5},{5,4},{6,7},{7,6},{8,9},{9,8},{10,11... | collective-permute-start | bytes 294920 | tf_op jit(solution)/shard_map/reduce_queries/ppermute | solution.py:332
  83.1 9.9 %collective-permute-start.15 = (bf16[24,2048]{1,0:T(8,128)(2,1)S(1)}, bf16[24,2048]{1,0:T(8,128)(2,1)S(1)}, u32[]{:S(2)}, u32[]{:S(2)}) collective-permute-start(bf16[24,2048]{1,0:T(8,128)(2,1)S(1)} %get-tuple-element.49), channel_id=1, source_target_pairs={{0,3},{1,2},{2,1},{3,0},{4,7},{5,6},{6,5},{7,4},{8,11},{9,10},{10,... | collective-permute-start | bytes 294920 | tf_op jit(solution)/shard_map/reduce_queries/ppermute | solution.py:332
  85.2 7.9 %collective-permute-start.14 = (bf16[24,2048]{1,0:T(8,128)(2,1)S(1)}, bf16[24,2048]{1,0:T(8,128)(2,1)S(1)}, u32[]{:S(2)}, u32[]{:S(2)}) collective-permute-start(bf16[24,2048]{1,0:T(8,128)(2,1)S(1)} %get-tuple-element.50), channel_id=1, source_target_pairs={{0,2},{1,3},{2,0},{3,1},{4,6},{5,7},{6,4},{7,5},{8,10},{9,11},{10,... | collective-permute-start | bytes 294920 | tf_op jit(solution)/shard_map/reduce_queries/ppermute | solution.py:332
  89.3 12.1 %all-to-all-start.2 = ((bf16[8,32,128]{2,1,0:T(8,128)(2,1)}), bf16[8,32,128]{2,1,0:T(8,128)(2,1)S(1)}, u32[]{:S(2)}, u32[]{:S(2)}) async-start(bf16[8,32,128]{2,1,0:T(8,128)(2,1)} %bitcast.20), calls=%async_computation.2 | async-start | bytes 131072 | tf_op jit(solution)/shard_map/reduce_keys/all_to_all | solution.py:407

commit v6 on v5

--- a/solution.py
+++ b/solution.py
@@ -370,8 +370,8 @@
         p11, p31 = shift(p01, 1), shift(p01, 3)
         p21 = flip(p20, "yl")
     groups = [
-        [(0, 0, p00), (0, 1, p01)],
-        [(1, 0, p10), (3, 0, p30), (2, 0, p20)],
+        [(0, 0, p00), (0, 1, p01), (2, 0, p20)],
+        [(1, 0, p10), (3, 0, p30)],
         [(1, 1, p11), (3, 1, p31), (2, 1, p21)],
     ]
     flat = [entry for group in groups for entry in group]

time: 103 us -> 102 us (level)
  transfers between devices with their start and end apart: 19 -> 19, of which waited for: 9 -> 8; matrix products, arithmetic and copies ran while one was open for 3% -> 3% of each run, Pallas kernels for 12% -> 12%
where the time goes in v6:
time: 102 us
  starting transfers between devices  38.2 us (37%)
  waiting for transfers between devices  26.4 us (26%)
  Pallas kernels  23.4 us (23%)
  local copies, waits for them, and re-layouts  10.2 us (10%)
  other arithmetic  2.53 us (2%)
    pallas_call x3, Pallas kernels, forward(): pl.pallas_call(functools.partial(forward_kernel, count, first), in_specs=...  12 us
    all_to_all x1, waiting for transfers between devices, body(): p00 = lax.all_to_all(own_keys, 'z', 0, 0, tiled=True).reshape(HALF, PACKED)  8.89 us
    all_to_all x1, starting transfers between devices, body(): p00 = lax.all_to_all(own_keys, 'z', 0, 0, tiled=True).reshape(HALF, PACKED)  8.47 us
    all_to_all x1, waiting for transfers between devices, body(): lax.all_to_all(jnp.transpose(over_xy, (1, 0, 2, 3)).reshape(8, 32, DI), '...  7.62 us
    unnamed x29, local copies, waits for them, and re-layouts  7.53 us
    pallas_call x1, Pallas kernels, backward_keys(): pl.pallas_call(functools.partial(backward_keys_kernel, sizes), in_specs=[...  7.36 us
    ppermute x6, starting transfers between devices, head_xor(): return lax.ppermute(value, HEAD, [(i, i ^ bits) for i in range(4)])  7.19 us
    ppermute x5, starting transfers between devices, shift(): return lax.ppermute(value, 'x', [((i + s) % 4, i) for i in range(4)])  6.95 us
  transfers between devices with their start and end apart: 19, of which 8 were waited for; matrix products, arithmetic and copies ran while one was open for 3% of the time, Pallas kernels for 12%

profile of v6, /device:TPU:2, one launch (start us, length us, event | category | flops | bytes accessed | tf_op | source)
XLA Modules:
  0.0 101.6 jit_solution(10337832373240463956)
XLA Ops:
  0.6 0.0 copy-start
  0.7 0.9 copy-done
  1.5 0.1 constant_dynamic-slice_fusion.2
  1.7 0.1 copy.28
  1.8 0.7 constant_dynamic-slice_fusion.1
  2.5 0.1 concatenate.6
  2.6 0.8 broadcast_in_dim.6
  3.5 0.1 stack.50
  3.5 0.1 copy.26
  3.6 0.0 copy-done.10
  3.7 3.3 %collective-permute-start.1 = (bf16[24,11392]{1,0:T(8,128)(2,1)S(1)}, bf16[24,11392]{1,0:T(8,128)(2,1)S(1)}, u32[]{:S(2)}, u32[]{:S(2)}) collective-permute-start(bf16[24,11392]{1,0:T(8,128)(2,1)S(1)} %pad_maximum_fusion.refs_0_), channel_id=1, source_target_pairs={{0,2},{2,0},{1,3},{3,1},{4,6},{6,4},{5,7},{7,5},{8,10},{10,8},{9,1... | collective-permute-start | bytes 1640456 | tf_op jit(solution)/shard_map/gather_queries/ppermute | solution.py:328
  7.0 8.5 %all-to-all-start = ((bf16[8,16,1408]{2,1,0:T(8,128)(2,1)}), bf16[8,16,1408]{2,1,0:T(8,128)(2,1)S(1)}, u32[]{:S(2)}, u32[]{:S(2)}) async-start(bf16[8,16,1408]{2,1,0:T(8,128)(2,1)} %broadcast_in_dim.6), calls=%async_computation | async-start | bytes 720896 | tf_op jit(solution)/shard_map/gather_keys/all_to_all | solution.py:365
  15.4 0.0 collective-permute-start
  15.4 4.0 %collective-permute-done.1.refs_2_ = bf16[24,11392]{1,0:T(8,128)(2,1)S(1)} collective-permute-done((bf16[24,11392]{1,0:T(8,128)(2,1)S(1)}, bf16[24,11392]{1,0:T(8,128)(2,1)S(1)}, u32[]{:S(2)}, u32[]{:S(2)}) %collective-permute-start.1) | collective-permute-done | bytes 546848 | tf_op jit(solution)/shard_map/gather_queries/ppermute | solution.py:328
  19.4 0.0 collective-permute-start.2
  19.4 0.8 copy-done.1
  20.2 8.9 %all-to-all-done = bf16[8,16,1408]{2,1,0:T(8,128)(2,1)S(1)} async-done(((bf16[8,16,1408]{2,1,0:T(8,128)(2,1)}), bf16[8,16,1408]{2,1,0:T(8,128)(2,1)S(1)}, u32[]{:S(2)}, u32[]{:S(2)}) %all-to-all-start) | async-done | bytes 360480 | tf_op jit(solution)/shard_map/gather_keys/all_to_all | solution.py:365
  29.1 0.7 collective-permute-start.3
  29.8 2.1 %collective-permute-start.4 = (bf16[128,1408]{1,0:T(8,128)(2,1)S(1)}, bf16[128,1408]{1,0:T(8,128)(2,1)}, u32[]{:S(2)}, u32[]{:S(2)}) collective-permute-start(bf16[128,1408]{1,0:T(8,128)(2,1)S(1)} %bitcast.33), channel_id=1, source_target_pairs={{8,0},{12,4},{0,8},{4,12},{9,1},{13,5},{1,9},{5,13},{10,2},{14,6},... | collective-permute-start | bytes 1081352 | tf_op jit(solution)/shard_map/gather_keys/ppermute | solution.py:362
  31.9 0.1 stack.59.refs_0_
  32.0 0.0 collective-permute-done.refs_1_
  32.0 0.8 copy-done.3
  32.8 0.0 collective-permute-done.2.refs_3_
  32.8 0.8 copy-done.5
  33.7 1.0 %copy-done.2 = bf16[24,11392]{1,0:T(8,128)(2,1)S(1)} copy-done((bf16[24,11392]{1,0:T(8,128)(2,1)S(1)}, bf16[24,11392]{1,0:T(8,128)(2,1)}, u32[]{:S(2)}) %copy-start.2) | copy-done | bytes 546840
  34.7 1.0 %copy-done.4 = bf16[24,11392]{1,0:T(8,128)(2,1)S(1)} copy-done((bf16[24,11392]{1,0:T(8,128)(2,1)S(1)}, bf16[24,11392]{1,0:T(8,128)(2,1)}, u32[]{:S(2)}) %copy-start.4) | copy-done | bytes 546840
  35.8 1.0 %copy-done.6 = bf16[24,11392]{1,0:T(8,128)(2,1)S(1)} copy-done((bf16[24,11392]{1,0:T(8,128)(2,1)S(1)}, bf16[24,11392]{1,0:T(8,128)(2,1)}, u32[]{:S(2)}) %copy-start.6) | copy-done | bytes 546840
  36.8 0.5 assemble.1.refs_3_.refs_19_.q_ref
  37.3 0.1 collective-permute-start.6
  37.4 2.0 %collective-permute-start.5 = (bf16[128,1408]{1,0:T(8,128)(2,1)S(1)}, bf16[128,1408]{1,0:T(8,128)(2,1)S(1)}, u32[]{:S(2)}, u32[]{:S(2)}) collective-permute-start(bf16[128,1408]{1,0:T(8,128)(2,1)S(1)} %bitcast.35), channel_id=1, source_target_pairs={{4,0},{8,4},{12,8},{0,12},{5,1},{9,5},{13,9},{1,13},{6,2},{10,6},{... | collective-permute-start | bytes 1081352 | tf_op jit(solution)/shard_map/gather_keys/ppermute | solution.py:362
  39.4 0.1 collective-permute-start.8
  39.5 2.6 %collective-permute-start.7 = (bf16[128,1408]{1,0:T(8,128)(2,1)}, bf16[128,1408]{1,0:T(8,128)(2,1)S(1)}, u32[]{:S(2)}, u32[]{:S(2)}) collective-permute-start(bf16[128,1408]{1,0:T(8,128)(2,1)} %collective-permute-done.3.refs_5_), channel_id=1, source_target_pairs={{4,0},{8,4},{12,8},{0,12},{5,1},{9,5},{13,9},{1,13},{6,2},{10,6},{... | collective-permute-start | bytes 1081352 | tf_op jit(solution)/shard_map/gather_keys/ppermute | solution.py:362
  42.1 0.0 collective-permute-done.4.refs_6_
  42.1 1.3 %collective-permute-start.9 = (bf16[128,1408]{1,0:T(8,128)(2,1)}, bf16[128,1408]{1,0:T(8,128)(2,1)S(1)}, u32[]{:S(2)}, u32[]{:S(2)}) collective-permute-start(bf16[128,1408]{1,0:T(8,128)(2,1)} %collective-permute-done.4.refs_6_), channel_id=1, source_target_pairs={{0,16},{16,0},{1,17},{17,1},{2,18},{18,2},{3,19},{19,3},{4,20},{20... | collective-permute-start | bytes 1081352 | tf_op jit(solution)/shard_map/gather_keys/ppermute | solution.py:328
  43.5 0.1 broadcast_in_dim.8.refs_1_.refs_2_
  43.5 4.7 %forward.3 = (bf16[3,1536,256]{2,1,0:T(8,128)(2,1)S(1)}, f32[3,24,256]{2,1,0:T(8,128)S(1)}, bf16[3,256,128]{2,1,0:T(8,128)(2,1)S(1)}, f32[8,1664]{1,0:T(8,128)S(1)}, f32[2,1664]{1,0:T(2,128)S(1)}) custom-call(s32[8]{0:T(128)S(1)} %multiply_add_fusion.refs_0_.refs_1_, s32[24,128]{1,0:T(8,128)S(1)} %broadcast_in_dim.8.refs_1_.refs_2_, ...), custom_call_target="tpu_custom_call" | custom-call | flops 3623878656 | bytes 2359296 | tf_op jit(solution)/shard_map/forward/pallas_call | solution.py:177
  48.2 0.0 copy-start.8
  48.2 0.6 collective-permute-done.6.refs_5_
  48.8 0.0 collective-permute-done.5.refs_4_
  48.8 3.2 %forward.4 = (bf16[2,1536,256]{2,1,0:T(8,128)(2,1)S(1)}, f32[2,24,256]{2,1,0:T(8,128)S(1)}, bf16[2,256,128]{2,1,0:T(8,128)(2,1)S(1)}, f32[8,1664]{1,0:T(8,128)S(1)}, f32[2,1664]{1,0:T(2,128)S(1)}) custom-call(s32[8]{0:T(128)S(1)} %multiply_add_fusion.refs_0_.refs_1_, s32[24,128]{1,0:T(8,128)S(1)} %broadcast_in_dim.8.refs_1_.refs_2_, ...), custom_call_target="tpu_custom_call" | custom-call | flops 2415919104 | bytes 1572864 | tf_op jit(solution)/shard_map/forward/pallas_call | solution.py:177
  52.1 2.5 %collective-permute-done.8.refs_5_ = bf16[128,1408]{1,0:T(8,128)(2,1)S(1)} collective-permute-done((bf16[128,1408]{1,0:T(8,128)(2,1)}, bf16[128,1408]{1,0:T(8,128)(2,1)S(1)}, u32[]{:S(2)}, u32[]{:S(2)}) %collective-permute-start.8) | collective-permute-done | bytes 360480 | tf_op jit(solution)/shard_map/gather_keys/ppermute | solution.py:362
  54.6 0.0 collective-permute-done.7.refs_4_
  54.6 4.1 %forward.5 = (bf16[3,1536,256]{2,1,0:T(8,128)(2,1)S(1)}, f32[3,24,256]{2,1,0:T(8,128)S(1)}, bf16[3,256,128]{2,1,0:T(8,128)(2,1)S(1)}, f32[8,1664]{1,0:T(8,128)S(1)}, f32[2,1664]{1,0:T(2,128)S(1)}) custom-call(s32[8]{0:T(128)S(1)} %multiply_add_fusion.refs_0_.refs_1_, s32[24,128]{1,0:T(8,128)S(1)} %broadcast_in_dim.8.refs_1_.refs_2_, ...), custom_call_target="tpu_custom_call" | custom-call | flops 3623878656 | bytes 2359296 | tf_op jit(solution)/shard_map/forward/pallas_call | solution.py:177
  58.7 0.1 collective-permute-start.12
  58.8 1.9 %collective-permute-start.11 = (f32[2,1664]{1,0:T(2,128)S(1)}, f32[2,1664]{1,0:T(2,128)S(1)}, u32[]{:S(2)}, u32[]{:S(2)}) collective-permute-start(f32[2,1664]{1,0:T(2,128)S(1)} %get-tuple-element.33.refs_3_), channel_id=1, source_target_pairs={{0,2},{1,3},{2,0},{3,1},{4,6},{5,7},{6,4},{7,5},{8,10},{9,11},{10,... | collective-permute-start | bytes 39944 | tf_op jit(solution)/shard_map/exchange_stats/ppermute | solution.py:332
  60.7 1.4 %collective-permute-start.10 = (f32[2,1664]{1,0:T(2,128)S(1)}, f32[2,1664]{1,0:T(2,128)S(1)}, u32[]{:S(2)}, u32[]{:S(2)}) collective-permute-start(f32[2,1664]{1,0:T(2,128)S(1)} %get-tuple-element.33.refs_3_), channel_id=1, source_target_pairs={{0,1},{1,0},{2,3},{3,2},{4,5},{5,4},{6,7},{7,6},{8,9},{9,8},{10,11... | collective-permute-start | bytes 39944 | tf_op jit(solution)/shard_map/exchange_stats/ppermute | solution.py:332
  62.1 1.3 %collective-permute-done.12.refs_6_ = f32[2,1664]{1,0:T(2,128)S(1)} collective-permute-done((f32[2,1664]{1,0:T(2,128)S(1)}, f32[2,1664]{1,0:T(2,128)S(1)}, u32[]{:S(2)}, u32[]{:S(2)}) %collective-permute-start.12) | collective-permute-done | bytes 13344 | tf_op jit(solution)/shard_map/exchange_stats/ppermute | solution.py:332
  63.4 0.7 collective-permute-done.11.refs_5_
  64.1 7.4 %backward_keys.1 = (bf16[8,256,128]{2,1,0:T(8,128)(2,1)}, f32[24,2048]{1,0:T(8,128)S(1)}) custom-call(s32[8]{0:T(128)S(1)} %stack.59.refs_0_, s32[8]{0:T(128)S(1)} %multiply_add_fusion.refs_0_.refs_1_, s32[24,128]{1,0:T(8,128)S(1)} %broadcast_in_dim.8.refs_1_.refs_2_, f32[2,1664]{1,0:T(2,128)S(1)} %get-tuple-element.33.refs_3_, ...), custom_call_target="tpu_custom_call" | custom-call | flops 3221225472 | bytes 6291456 | tf_op jit(solution)/shard_map/backward_keys/pallas_call | solution.py:285
  71.5 5.9 %all-to-all-start.1 = ((bf16[8,256,128]{2,1,0:T(8,128)(2,1)}), bf16[8,256,128]{2,1,0:T(8,128)(2,1)}, u32[]{:S(2)}, u32[]{:S(2)}) async-start(bf16[8,256,128]{2,1,0:T(8,128)(2,1)} %get-tuple-element.47), calls=%async_computation.1 | async-start | bytes 1048576 | tf_op jit(solution)/shard_map/reduce_keys/all_to_all | solution.py:402
  77.3 0.9 copy-done.9
  78.3 3.6 %backward_queries.1 = bf16[4,24,2048]{2,1,0:T(8,128)(2,1)S(1)} custom-call(bf16[1536,768]{1,0:T(8,128)(2,1)S(1)} %assemble.1.refs_3_.refs_19_.q_ref, f32[24,2048]{1,0:T(8,128)S(1)} %get-tuple-element.46.grad_ref, bf16[3,256,128]{2,1,0:T(8,128)(2,1)S(1)} %copy-done.9, bf16[2,256,128]{2,1,0:T(8,128)(2,1)S(1)} %get-tuple-element.44.refs_17_.refs_1_, ...), custom_call_target="tpu_custom_call" | custom-call | flops 12884901888 | bytes 6291456 | tf_op jit(solution)/shard_map/backward_queries/pallas_call | solution.py:314
  81.9 0.1 collective-permute-start.13
  82.0 2.4 %collective-permute-start.15 = (bf16[24,2048]{1,0:T(8,128)(2,1)S(1)}, bf16[24,2048]{1,0:T(8,128)(2,1)S(1)}, u32[]{:S(2)}, u32[]{:S(2)}) collective-permute-start(bf16[24,2048]{1,0:T(8,128)(2,1)S(1)} %get-tuple-element.49), channel_id=1, source_target_pairs={{0,3},{1,2},{2,1},{3,0},{4,7},{5,6},{6,5},{7,4},{8,11},{9,10},{10,... | collective-permute-start | bytes 294920 | tf_op jit(solution)/shard_map/reduce_queries/ppermute | solution.py:332
  84.4 1.3 %collective-permute-start.14 = (bf16[24,2048]{1,0:T(8,128)(2,1)S(1)}, bf16[24,2048]{1,0:T(8,128)(2,1)S(1)}, u32[]{:S(2)}, u32[]{:S(2)}) collective-permute-start(bf16[24,2048]{1,0:T(8,128)(2,1)S(1)} %get-tuple-element.50), channel_id=1, source_target_pairs={{0,2},{1,3},{2,0},{3,1},{4,6},{5,7},{6,4},{7,5},{8,10},{9,11},{10,... | collective-permute-start | bytes 294920 | tf_op jit(solution)/shard_map/reduce_queries/ppermute | solution.py:332
  85.7 0.8 all-to-all-done.1
  86.5 1.1 %add_convert_fusion = bf16[1,256,128]{2,1,0:T(8,128)(2,1)S(1)} fusion(bf16[8,256,128]{2,1,0:T(8,128)(2,1)} %all-to-all-done.1), kind=kLoop, calls=%fused_computation.4 | loop fusion | flops 524288 | bytes 589824 | tf_op jit(solution)/shard_map/reduce_keys/convert_element_type | solution.py:406
  87.6 0.6 copy.27
  88.3 4.4 %all-to-all-start.2 = ((bf16[8,32,128]{2,1,0:T(8,128)(2,1)}), bf16[8,32,128]{2,1,0:T(8,128)(2,1)S(1)}, u32[]{:S(2)}, u32[]{:S(2)}) async-start(bf16[8,32,128]{2,1,0:T(8,128)(2,1)} %bitcast.20), calls=%async_computation.2 | async-start | bytes 131072 | tf_op jit(solution)/shard_map/reduce_keys/all_to_all | solution.py:407
  92.6 0.0 collective-permute-done.15
  92.6 0.0 collective-permute-done.14
  92.7 0.7 fusion.1
  93.4 7.6 %all-to-all-done.2 = bf16[8,32,128]{2,1,0:T(8,128)(2,1)S(1)} async-done(((bf16[8,32,128]{2,1,0:T(8,128)(2,1)}), bf16[8,32,128]{2,1,0:T(8,128)(2,1)S(1)}, u32[]{:S(2)}, u32[]{:S(2)}) %all-to-all-start.2) | async-done | bytes 65568 | tf_op jit(solution)/shard_map/reduce_keys/all_to_all | solution.py:407
  101.0 0.6 convert_reduce_fusion
  (32 shorter events, 0.2 us)
Async XLA Ops:
  0.6 0.9 copy-start
  0.6 2.7 %copy-start.12 = (f32[24,16]{0,1:T(8,128)S(1)}, f32[24,16]{0,1:T(8,128)}, u32[]{:S(2)}) copy-start(f32[24,16]{0,1:T(8,128)} %param.10) | copy-start | bytes 4612
  0.7 3.0 %copy-start.11 = (bf16[24,2048]{1,0:T(8,128)(2,1)S(1)}, bf16[24,2048]{1,0:T(8,128)(2,1)}, u32[]{:S(2)}) copy-start(bf16[24,2048]{1,0:T(8,128)(2,1)} %param.8) | copy-start | bytes 294916
  0.7 3.0 %copy-start.10 = (bf16[24,9216]{1,0:T(8,128)(2,1)S(1)}, bf16[24,9216]{1,0:T(8,128)(2,1)}, u32[]{:S(2)}) copy-start(bf16[24,9216]{1,0:T(8,128)(2,1)} %param.6) | copy-start | bytes 1327108
  3.7 15.7 %collective-permute-start.1 = (bf16[24,11392]{1,0:T(8,128)(2,1)S(1)}, bf16[24,11392]{1,0:T(8,128)(2,1)S(1)}, u32[]{:S(2)}, u32[]{:S(2)}) collective-permute-start(bf16[24,11392]{1,0:T(8,128)(2,1)S(1)} %pad_maximum_fusion.refs_0_), channel_id=1, source_target_pairs={{0,2},{2,0},{1,3},{3,1},{4,6},{6,4},{5,7},{7,5},{8,10},{10,8},{9,1... | collective-permute-start | bytes 1640456 | tf_op jit(solution)/shard_map/gather_queries/ppermute | solution.py:328
  7.0 22.2 %all-to-all-start = ((bf16[8,16,1408]{2,1,0:T(8,128)(2,1)}), bf16[8,16,1408]{2,1,0:T(8,128)(2,1)S(1)}, u32[]{:S(2)}, u32[]{:S(2)}) async-start(bf16[8,16,1408]{2,1,0:T(8,128)(2,1)} %broadcast_in_dim.6), calls=%async_computation | async-start | bytes 720896 | tf_op jit(solution)/shard_map/gather_keys/all_to_all | solution.py:365
  15.4 16.6 %collective-permute-start = (bf16[24,11392]{1,0:T(8,128)(2,1)S(1)}, bf16[24,11392]{1,0:T(8,128)(2,1)S(1)}, u32[]{:S(2)}, u32[]{:S(2)}) collective-permute-start(bf16[24,11392]{1,0:T(8,128)(2,1)S(1)} %pad_maximum_fusion.refs_0_), channel_id=1, source_target_pairs={{0,1},{1,0},{2,3},{3,2},{4,5},{5,4},{6,7},{7,6},{8,9},{9,8},{10,11... | collective-permute-start | bytes 1640456 | tf_op jit(solution)/shard_map/gather_queries/ppermute | solution.py:328
  19.4 13.4 %collective-permute-start.2 = (bf16[24,11392]{1,0:T(8,128)(2,1)S(1)}, bf16[24,11392]{1,0:T(8,128)(2,1)S(1)}, u32[]{:S(2)}, u32[]{:S(2)}) collective-permute-start(bf16[24,11392]{1,0:T(8,128)(2,1)S(1)} %collective-permute-done.1.refs_2_), channel_id=1, source_target_pairs={{0,1},{1,0},{2,3},{3,2},{4,5},{5,4},{6,7},{7,6},{8,9},{9,8},{10,11... | collective-permute-start | bytes 1640456 | tf_op jit(solution)/shard_map/gather_queries/ppermute | solution.py:328
  19.4 0.8 copy-start.1
  29.1 10.2 %collective-permute-start.3 = (bf16[128,1408]{1,0:T(8,128)(2,1)S(1)}, bf16[128,1408]{1,0:T(8,128)(2,1)}, u32[]{:S(2)}, u32[]{:S(2)}) collective-permute-start(bf16[128,1408]{1,0:T(8,128)(2,1)S(1)} %bitcast.32), channel_id=1, source_target_pairs={{0,16},{16,0},{1,17},{17,1},{2,18},{18,2},{3,19},{19,3},{4,20},{20... | collective-permute-start | bytes 1081352 | tf_op jit(solution)/shard_map/gather_keys/ppermute | solution.py:328
  29.8 12.3 %collective-permute-start.4 = (bf16[128,1408]{1,0:T(8,128)(2,1)S(1)}, bf16[128,1408]{1,0:T(8,128)(2,1)}, u32[]{:S(2)}, u32[]{:S(2)}) collective-permute-start(bf16[128,1408]{1,0:T(8,128)(2,1)S(1)} %bitcast.33), channel_id=1, source_target_pairs={{8,0},{12,4},{0,8},{4,12},{9,1},{13,5},{1,9},{5,13},{10,2},{14,6},... | collective-permute-start | bytes 1081352 | tf_op jit(solution)/shard_map/gather_keys/ppermute | solution.py:362
  31.9 11.5 %copy-start.13 = (s32[24]{0:T(128)S(1)}, s32[24]{0:T(128)}, u32[]{:S(2)}) copy-start(s32[24]{0:T(128)} %param.11) | copy-start | bytes 292
  32.0 0.8 copy-start.3
  32.8 0.8 copy-start.5
  33.7 1.0 %copy-start.2 = (bf16[24,11392]{1,0:T(8,128)(2,1)S(1)}, bf16[24,11392]{1,0:T(8,128)(2,1)}, u32[]{:S(2)}) copy-start(bf16[24,11392]{1,0:T(8,128)(2,1)} %copy-done.1) | copy-start | bytes 1640452
  34.7 1.0 %copy-start.4 = (bf16[24,11392]{1,0:T(8,128)(2,1)S(1)}, bf16[24,11392]{1,0:T(8,128)(2,1)}, u32[]{:S(2)}) copy-start(bf16[24,11392]{1,0:T(8,128)(2,1)} %copy-done.3) | copy-start | bytes 1640452
  35.8 1.0 %copy-start.6 = (bf16[24,11392]{1,0:T(8,128)(2,1)S(1)}, bf16[24,11392]{1,0:T(8,128)(2,1)}, u32[]{:S(2)}) copy-start(bf16[24,11392]{1,0:T(8,128)(2,1)} %copy-done.5) | copy-start | bytes 1640452
  36.8 6.7 %copy-start.7 = (f32[2,1664]{1,0:T(2,128)S(1)}, f32[2,1664]{1,0:T(2,128)}, u32[]{:S(2)}) copy-start(f32[2,1664]{1,0:T(2,128)} %constant.88.clone.1.refs_2_) | copy-start | bytes 39940
  37.3 11.5 %collective-permute-start.6 = (bf16[128,1408]{1,0:T(8,128)(2,1)S(1)}, bf16[128,1408]{1,0:T(8,128)(2,1)S(1)}, u32[]{:S(2)}, u32[]{:S(2)}) collective-permute-start(bf16[128,1408]{1,0:T(8,128)(2,1)S(1)} %bitcast.34), channel_id=1, source_target_pairs={{12,0},{0,4},{4,8},{8,12},{13,1},{1,5},{5,9},{9,13},{14,2},{2,6},{... | collective-permute-start | bytes 1081352 | tf_op jit(solution)/shard_map/gather_keys/ppermute | solution.py:362
  37.4 11.5 %collective-permute-start.5 = (bf16[128,1408]{1,0:T(8,128)(2,1)S(1)}, bf16[128,1408]{1,0:T(8,128)(2,1)S(1)}, u32[]{:S(2)}, u32[]{:S(2)}) collective-permute-start(bf16[128,1408]{1,0:T(8,128)(2,1)S(1)} %bitcast.35), channel_id=1, source_target_pairs={{4,0},{8,4},{12,8},{0,12},{5,1},{9,5},{13,9},{1,13},{6,2},{10,6},{... | collective-permute-start | bytes 1081352 | tf_op jit(solution)/shard_map/gather_keys/ppermute | solution.py:362
  39.4 15.2 %collective-permute-start.8 = (bf16[128,1408]{1,0:T(8,128)(2,1)}, bf16[128,1408]{1,0:T(8,128)(2,1)S(1)}, u32[]{:S(2)}, u32[]{:S(2)}) collective-permute-start(bf16[128,1408]{1,0:T(8,128)(2,1)} %collective-permute-done.3.refs_5_), channel_id=1, source_target_pairs={{12,0},{0,4},{4,8},{8,12},{13,1},{1,5},{5,9},{9,13},{14,2},{2,6},{... | collective-permute-start | bytes 1081352 | tf_op jit(solution)/shard_map/gather_keys/ppermute | solution.py:362
  39.5 15.1 %collective-permute-start.7 = (bf16[128,1408]{1,0:T(8,128)(2,1)}, bf16[128,1408]{1,0:T(8,128)(2,1)S(1)}, u32[]{:S(2)}, u32[]{:S(2)}) collective-permute-start(bf16[128,1408]{1,0:T(8,128)(2,1)} %collective-permute-done.3.refs_5_), channel_id=1, source_target_pairs={{4,0},{8,4},{12,8},{0,12},{5,1},{9,5},{13,9},{1,13},{6,2},{10,6},{... | collective-permute-start | bytes 1081352 | tf_op jit(solution)/shard_map/gather_keys/ppermute | solution.py:362
  42.1 9.9 %collective-permute-start.9 = (bf16[128,1408]{1,0:T(8,128)(2,1)}, bf16[128,1408]{1,0:T(8,128)(2,1)S(1)}, u32[]{:S(2)}, u32[]{:S(2)}) collective-permute-start(bf16[128,1408]{1,0:T(8,128)(2,1)} %collective-permute-done.4.refs_6_), channel_id=1, source_target_pairs={{0,16},{16,0},{1,17},{17,1},{2,18},{18,2},{3,19},{19,3},{4,20},{20... | collective-permute-start | bytes 1081352 | tf_op jit(solution)/shard_map/gather_keys/ppermute | solution.py:328
  48.2 15.9 %copy-start.8 = (bf16[3,256,128]{2,1,0:T(8,128)(2,1)}, bf16[3,256,128]{2,1,0:T(8,128)(2,1)S(1)}, u32[]{:S(2)}) copy-start(bf16[3,256,128]{2,1,0:T(8,128)(2,1)S(1)} %get-tuple-element.43.refs_16_.refs_0_) | copy-start | bytes 589828
  58.7 4.7 %collective-permute-start.12 = (f32[2,1664]{1,0:T(2,128)S(1)}, f32[2,1664]{1,0:T(2,128)S(1)}, u32[]{:S(2)}, u32[]{:S(2)}) collective-permute-start(f32[2,1664]{1,0:T(2,128)S(1)} %get-tuple-element.33.refs_3_), channel_id=1, source_target_pairs={{0,3},{1,2},{2,1},{3,0},{4,7},{5,6},{6,5},{7,4},{8,11},{9,10},{10,... | collective-permute-start | bytes 39944 | tf_op jit(solution)/shard_map/exchange_stats/ppermute | solution.py:332
  58.8 5.3 %collective-permute-start.11 = (f32[2,1664]{1,0:T(2,128)S(1)}, f32[2,1664]{1,0:T(2,128)S(1)}, u32[]{:S(2)}, u32[]{:S(2)}) collective-permute-start(f32[2,1664]{1,0:T(2,128)S(1)} %get-tuple-element.33.refs_3_), channel_id=1, source_target_pairs={{0,2},{1,3},{2,0},{3,1},{4,6},{5,7},{6,4},{7,5},{8,10},{9,11},{10,... | collective-permute-start | bytes 39944 | tf_op jit(solution)/shard_map/exchange_stats/ppermute | solution.py:332
  60.7 3.4 %collective-permute-start.10 = (f32[2,1664]{1,0:T(2,128)S(1)}, f32[2,1664]{1,0:T(2,128)S(1)}, u32[]{:S(2)}, u32[]{:S(2)}) collective-permute-start(f32[2,1664]{1,0:T(2,128)S(1)} %get-tuple-element.33.refs_3_), channel_id=1, source_target_pairs={{0,1},{1,0},{2,3},{3,2},{4,5},{5,4},{6,7},{7,6},{8,9},{9,8},{10,11... | collective-permute-start | bytes 39944 | tf_op jit(solution)/shard_map/exchange_stats/ppermute | solution.py:332
  71.5 15.0 %all-to-all-start.1 = ((bf16[8,256,128]{2,1,0:T(8,128)(2,1)}), bf16[8,256,128]{2,1,0:T(8,128)(2,1)}, u32[]{:S(2)}, u32[]{:S(2)}) async-start(bf16[8,256,128]{2,1,0:T(8,128)(2,1)} %get-tuple-element.47), calls=%async_computation.1 | async-start | bytes 1048576 | tf_op jit(solution)/shard_map/reduce_keys/all_to_all | solution.py:402
  77.3 0.9 copy-start.9
  81.9 10.7 %collective-permute-start.13 = (bf16[24,2048]{1,0:T(8,128)(2,1)S(1)}, bf16[24,2048]{1,0:T(8,128)(2,1)S(1)}, u32[]{:S(2)}, u32[]{:S(2)}) collective-permute-start(bf16[24,2048]{1,0:T(8,128)(2,1)S(1)} %get-tuple-element.48), channel_id=1, source_target_pairs={{0,1},{1,0},{2,3},{3,2},{4,5},{5,4},{6,7},{7,6},{8,9},{9,8},{10,11... | collective-permute-start | bytes 294920 | tf_op jit(solution)/shard_map/reduce_queries/ppermute | solution.py:332
  82.0 10.6 %collective-permute-start.15 = (bf16[24,2048]{1,0:T(8,128)(2,1)S(1)}, bf16[24,2048]{1,0:T(8,128)(2,1)S(1)}, u32[]{:S(2)}, u32[]{:S(2)}) collective-permute-start(bf16[24,2048]{1,0:T(8,128)(2,1)S(1)} %get-tuple-element.49), channel_id=1, source_target_pairs={{0,3},{1,2},{2,1},{3,0},{4,7},{5,6},{6,5},{7,4},{8,11},{9,10},{10,... | collective-permute-start | bytes 294920 | tf_op jit(solution)/shard_map/reduce_queries/ppermute | solution.py:332
  84.4 8.2 %collective-permute-start.14 = (bf16[24,2048]{1,0:T(8,128)(2,1)S(1)}, bf16[24,2048]{1,0:T(8,128)(2,1)S(1)}, u32[]{:S(2)}, u32[]{:S(2)}) collective-permute-start(bf16[24,2048]{1,0:T(8,128)(2,1)S(1)} %get-tuple-element.50), channel_id=1, source_target_pairs={{0,2},{1,3},{2,0},{3,1},{4,6},{5,7},{6,4},{7,5},{8,10},{9,11},{10,... | collective-permute-start | bytes 294920 | tf_op jit(solution)/shard_map/reduce_queries/ppermute | solution.py:332
  88.3 12.7 %all-to-all-start.2 = ((bf16[8,32,128]{2,1,0:T(8,128)(2,1)}), bf16[8,32,128]{2,1,0:T(8,128)(2,1)S(1)}, u32[]{:S(2)}, u32[]{:S(2)}) async-start(bf16[8,32,128]{2,1,0:T(8,128)(2,1)} %bitcast.20), calls=%async_computation.2 | async-start | bytes 131072 | tf_op jit(solution)/shard_map/reduce_keys/all_to_all | solution.py:407
